TPU v7x, 32 devices: a whole 2x2x4 slice. The times are simulated.
32 devices in a mesh: hist: 8 (over z, x), row: 4 (over y, core).
Axes of the slice: x: 2, y: 2, z: 4, core: 2. Of those that a mesh axis runs over, the one named last changes fastest.
Arguments:
- row_less: float32 [2, 96, 1024], P(None, 'hist'), may hold values from -40 to 40
- row_great: float32 [2, 96, 1024], P(None, 'hist'), may hold values from -5 to 5
- coupling: float32 [32, 32], replicated, may hold values from -1 to 1
- damping: float32 [96, 32], P('hist'), may hold values from 0.2 to 1, as said below
- phases: float32 [96, 32], P('hist'), may hold values from -3.140625 to 3.140625
- lesser_hist: bfloat16 [2, 96, 96, 1024], P(None, 'row', 'hist'), may hold values from -5 to 5
- advanced_hist: bfloat16 [2, 96, 96, 1024], P(None, 'row', 'hist'), may hold values from -5 to 5
- retarded_hist: bfloat16 [2, 96, 96, 1024], P(None, 'row', 'hist'), may hold values from -5 to 5
Outputs:
- stepped_row: float32 [2, 96, 1024], P(None, 'hist')
- column_term: float32 [2, 96, 1024], P(None, 'row')
Inputs may be any that keep to these rules, and one draw needn't show every extreme that they name: `damping`: one-step magnitudes.
All inputs are finite; a program needn't handle non-finite values.
Results may differ from a plain program's by a relative error of at most 0.0029.
Values may be sent and summed in bfloat16 or wider, within the bound.
No kernel may reach another device: no remote copies, remote signals or barrier semaphores. Data moves between devices by JAX's collectives and lax.ppermute only.
A program may use at most 128 MiB of HBM per device.

v0:
```python
import jax
import jax.numpy as jnp
from jax import lax
from jax.sharding import PartitionSpec as P


def carried_in(x, axis, combine, identity):
    size, mine = (lax.axis_size(axis), lax.axis_index(axis))
    everything = jax.tree.map(lambda part: lax.all_gather(part, axis), x)
    start = jax.tree.map(
        lambda part, zero: jnp.broadcast_to(jnp.asarray(zero, part.dtype), part.shape), x, identity
    )

    def hop(k, before):
        at = size - 1 - k
        reached = at > mine
        new = combine(before, jax.tree.map(lambda part: part[at], everything))
        return jax.tree.map(lambda a, b: jnp.where(reached, a, b), new, before)

    return lax.fori_loop(0, size, hop, start)


def self_energy(row_less, row_great, coupling):
    steps_here = row_less.shape[1]
    bands = coupling.shape[0]
    less_real = row_less[0].reshape(steps_here, bands, bands)
    less_imag = row_less[1].reshape(steps_here, bands, bands)
    great_real = row_great[0].reshape(steps_here, bands, bands)
    great_imag = row_great[1].reshape(steps_here, bands, bands)
    polar_real = -(less_real * great_real + less_imag * great_imag)
    polar_imag = -(less_imag * great_real - less_real * great_imag)
    highest = lax.Precision.HIGHEST

    def sandwich(polar):
        partial_value = jnp.einsum("ik,skl->sil", coupling, polar, precision=highest)
        return jnp.einsum("sil,jl->sij", partial_value, coupling, precision=highest)

    screen_real = sandwich(polar_real)
    screen_imag = sandwich(polar_imag)
    sigma_less = jnp.stack(
        [
            less_real * screen_real - less_imag * screen_imag,
            less_real * screen_imag + less_imag * screen_real,
        ]
    )
    sigma_great = jnp.stack(
        [
            great_real * screen_real + great_imag * screen_imag,
            great_imag * screen_real - great_real * screen_imag,
        ]
    )
    return ((sigma_great - sigma_less).astype(jnp.bfloat16), sigma_less.astype(jnp.bfloat16))


def contract_row(sigma, hist):
    return jnp.einsum("sik,stkj->tij", sigma, hist, preferred_element_type=jnp.float32)


def contract_column(hist, sigma):
    return jnp.einsum("tsik,sjk->tij", hist, sigma, preferred_element_type=jnp.float32)


def add_pair(earlier, latter):
    return (earlier[0] + latter[0], earlier[1] + latter[1])


def shards(
    row_less, row_great, coupling, damping, phases, lesser_hist, advanced_hist, retarded_hist
):
    bands = coupling.shape[0]
    steps_here = row_less.shape[1]
    rows_here = lesser_hist.shape[1]
    hist_count = lax.axis_size("hist")
    all_steps = steps_here * hist_count
    weight = float(all_steps * bands) ** (-0.5)
    hist_place = lax.axis_index("hist")
    row_place = lax.axis_index("row")
    sigma_ret, sigma_less = self_energy(row_less, row_great, coupling)
    retarded = retarded_hist.reshape(2, rows_here, steps_here, bands, bands)
    later_steps = row_place * rows_here + jnp.arange(rows_here, dtype=jnp.int32)
    earlier_steps = hist_place * steps_here + jnp.arange(steps_here, dtype=jnp.int32)
    causal_column = earlier_steps[None, :] <= later_steps[:, None]
    retarded = jnp.where(
        causal_column[None, :, :, None, None], retarded, jnp.zeros((), jnp.bfloat16)
    )
    column_real = -(
        contract_column(retarded[0], sigma_less[0]) + contract_column(retarded[1], sigma_less[1])
    )
    column_imag = -(
        contract_column(retarded[1], sigma_less[0]) - contract_column(retarded[0], sigma_less[1])
    )
    column_part = weight * jnp.stack([column_real, column_imag]).reshape(
        2, rows_here, bands * bands
    )
    stacked = jnp.stack([sigma_ret, sigma_less]).reshape(2, 2, steps_here, bands * bands)
    whole_row = lax.all_gather(stacked, "hist", axis=2, tiled=True)
    nearby = lax.dynamic_slice_in_dim(whole_row, row_place * rows_here, rows_here, 2)
    nearby = nearby.reshape(2, 2, rows_here, bands, bands)
    near_ret = nearby[0]
    near_less = nearby[1]
    lesser = lesser_hist.reshape(2, rows_here, steps_here, bands, bands)
    summed_steps = row_place * rows_here + jnp.arange(rows_here, dtype=jnp.int32)
    target_steps = hist_place * steps_here + jnp.arange(steps_here, dtype=jnp.int32)
    causal_row = summed_steps[:, None] <= target_steps[None, :]
    advanced = jnp.where(
        causal_row[None, :, :, None, None],
        advanced_hist.reshape(2, rows_here, steps_here, bands, bands),
        jnp.zeros((), jnp.bfloat16),
    )
    real_part = (
        contract_row(near_ret[0], lesser[0])
        - contract_row(near_ret[1], lesser[1])
        + contract_row(near_less[0], advanced[0])
        - contract_row(near_less[1], advanced[1])
    )
    imag_part = (
        contract_row(near_ret[0], lesser[1])
        + contract_row(near_ret[1], lesser[0])
        + contract_row(near_less[0], advanced[1])
        + contract_row(near_less[1], advanced[0])
    )
    partial_row = weight * jnp.stack([real_part, imag_part]).reshape(2, steps_here, bands * bands)
    log_rate = jnp.log(damping)
    inner_log = jnp.cumsum(log_rate[::-1], axis=0)[::-1]
    inner_phase = jnp.cumsum(phases[::-1], axis=0)[::-1]
    zero_row = jnp.zeros((bands,), jnp.float32)
    above_log, above_phase = carried_in(
        (inner_log[0], inner_phase[0]), "hist", add_pair, (zero_row, zero_row)
    )
    summed_log = inner_log + above_log[None, :]
    summed_phase = inner_phase + above_phase[None, :]
    magnitude = jnp.exp(summed_log)
    factor_real = jnp.repeat(magnitude * jnp.cos(summed_phase), bands, axis=1)
    factor_imag = jnp.repeat(-magnitude * jnp.sin(summed_phase), bands, axis=1)
    collision = lax.psum(partial_row, "row")
    sum_real = row_less[0] + collision[0]
    sum_imag = row_less[1] + collision[1]
    stepped_real = factor_real * sum_real - factor_imag * sum_imag
    stepped_imag = factor_real * sum_imag + factor_imag * sum_real
    local_squares = jnp.sum(stepped_real * stepped_real) + jnp.sum(stepped_imag * stepped_imag)
    squares = lax.psum(local_squares, "hist")
    column_term = lax.psum(column_part, "hist")
    norm_scale = jnp.sqrt(squares / (2 * all_steps * bands * bands) + 1e-06)
    stepped_row = jnp.stack([stepped_real, stepped_imag]) / norm_scale
    return (stepped_row, column_term)


def solution(mesh):
    return jax.shard_map(
        shards,
        mesh=mesh,
        in_specs=(
            P(None, "hist", None),
            P(None, "hist", None),
            P(),
            P("hist", None),
            P("hist", None),
            P(None, "row", "hist", None),
            P(None, "row", "hist", None),
            P(None, "row", "hist", None),
        ),
        out_specs=(P(None, "hist", None), P(None, "row", None)),
        check_vma=False,
    )
```

profile of v0, /device:TPU:0, one launch (start us, length us, event | category | flops | bytes accessed | tf_op | source)
XLA Modules:
  0.0 218.7 jit_solution(3770860185508676707)
XLA Ops:
  7.2 1.1 fusion.52
  9.2 1.2 slice_reduce_fusion.1
  13.2 4.8 %reshape.251 = bf16[2,24,12,32,32]{4,3,1,2,0:T(8,128)(2,1)} reshape(bf16[2,24,12,1024]{3,1,2,0:T(8,128)(2,1)S(1)} %copy-done.6) | data formatting | bytes 2359296 | tf_op jit(solution)/shard_map/reshape | solution.py:107
  18.1 6.7 %copy.58 = bf16[2,24,12,32,32]{3,4,1,2,0:T(8,128)(2,1)} copy(bf16[2,24,12,32,32]{4,3,1,2,0:T(8,128)(2,1)} %reshape.251) | data formatting | bytes 2359296 | tf_op jit(solution)/shard_map/reshape | solution.py:107
  24.8 4.7 %reshape.253 = bf16[2,24,12,32,32]{4,3,1,2,0:T(8,128)(2,1)} reshape(bf16[2,24,12,1024]{3,1,2,0:T(8,128)(2,1)S(1)} %copy-done.7) | data formatting | bytes 2359296 | tf_op jit(solution)/shard_map/reshape | solution.py:79
  29.5 6.7 %copy.63 = bf16[2,24,12,32,32]{3,4,1,2,0:T(8,128)(2,1)} copy(bf16[2,24,12,32,32]{4,3,1,2,0:T(8,128)(2,1)} %reshape.253) | data formatting | bytes 2359296 | tf_op jit(solution)/shard_map/reshape | solution.py:79
  37.4 34.0 %all_gather.11 = bf16[2,2,96,1024]{3,1,0,2:T(2,128)(2,1)S(1)} all-gather(bf16[2,2,12,1024]{3,1,0,2:T(2,128)(2,1)S(1)} %copy.57), channel_id=1, replica_groups=mesh['hist'=8,'row'=4] {'hist'}, dimensions={2}, use_global_device_ids=true | all-gather | bytes 884736 | tf_op jit(solution)/shard_map/all_gather | solution.py:96
  71.5 1.7 dynamic-slice_reduce_fusion
  75.0 1.8 squeeze.77
  77.9 2.8 %squeeze.75 = bf16[24,12,32,32]{3,2,0,1:T(8,128)(2,1)} reshape(bf16[1,24,12,1024]{3,1,2,0:T(8,128)(2,1)S(1)} %get-tuple-element.211) | data formatting | bytes 1179648 | tf_op jit(solution)/shard_map/squeeze | solution.py:111
  84.1 7.0 %broadcast_select_fusion.4 = (bf16[2,24,12,32,32]{3,4,1,2,0:T(8,128)(2,1)}, bf16[2,24,12,32,32]{3,4,1,2,0:T(8,128)(2,1)S(1)}) fusion(bf16[2,24,12,32,32]{3,4,1,2,0:T(8,128)(2,1)} %copy.63, pred[24,12]{0,1:T(8,128)(4,1)S(1)} %get-tuple-element.226, bf16[2,24,12,32,32]{3,4,1,2,0:T(8,128)(2,1)} %copy.58, pred[24,12]{0,1:T(8,128)(4,1)S(1)} %get-tuple-element.227), kind=kLoop, calls=%fused_computation.4 | loop fusion | flops 1179648 | bytes 4719168 | tf_op jit(solution)/shard_map/jit(_where)/select_n | solution.py:83
  91.1 1.8 fusion.16
  93.9 1.8 fusion.22
  96.6 3.9 %fusion.23 = f32[12,32,32]{2,1,0:T(8,128)S(1)} fusion(f32[12,32,32]{2,1,0:T(8,128)S(1)} %fusion.27, bf16[24,32,32,1]{2,1,0,3:T(8,128)(2,1)} %reshape.263, bf16[2,24,12,32,32]{3,4,1,2,0:T(8,128)(2,1)} %copy-done.2), kind=kOutput, calls=%fused_computation.39 | convolution fusion | flops 18886656 | bytes 2654208 | tf_op jit(solution)/shard_map/sik,stkj->tij/dot_general | solution.py:56
  100.6 1.9 fusion.20
  103.3 2.6 %fusion.8 = f32[24,32,32]{2,1,0:T(8,128)S(1)} fusion(bf16[2,24,12,32,32]{3,4,1,2,0:T(8,128)(2,1)} %get-tuple-element.228, f32[12,32,32]{2,1,0:T(8,128)S(1)} %copy-done.9), kind=kOutput, calls=%fused_computation.18 | convolution fusion | flops 18886656 | bytes 2506752 | tf_op jit(solution)/shard_map/tsik,sjk->tij/dot_general | solution.py:60
  106.0 2.5 %fusion.9 = f32[24,32,32]{2,1,0:T(8,128)S(1)} fusion(bf16[2,24,12,32,32]{3,4,1,2,0:T(8,128)(2,1)} %get-tuple-element.228, f32[12,32,32]{2,1,0:T(8,128)S(1)} %copy-done.11), kind=kOutput, calls=%fused_computation.19 | convolution fusion | flops 18886656 | bytes 2506752 | tf_op jit(solution)/shard_map/tsik,sjk->tij/dot_general | solution.py:60
  109.5 2.5 %fusion.13 = f32[24,32,32]{2,1,0:T(8,128)S(1)} fusion(f32[24,32,32]{2,1,0:T(8,128)S(1)} %fusion.9, bf16[2,24,12,32,32]{3,4,1,2,0:T(8,128)(2,1)} %get-tuple-element.228, f32[12,32,32]{2,1,0:T(8,128)S(1)} %copy-done.9), kind=kOutput, calls=%fused_computation.23 | convolution fusion | flops 18935808 | bytes 2605056 | tf_op jit(solution)/shard_map/tsik,sjk->tij/dot_general | solution.py:60
  113.1 20.4 %all-gather = f32[8,1,32]{2,1,0:T(1,128)S(1)} all-gather(f32[1,1,32]{2,1,0:T(1,128)S(1)} %slice_bitcast_fusion.45), channel_id=1, replica_groups=mesh['hist'=8,'row'=4] {'hist'}, dimensions={0}, use_global_device_ids=true | all-gather | bytes 1152 | tf_op jit(solution)/shard_map/all_gather | solution.py:9
  133.5 16.2 %all-gather.1 = f32[8,1,32]{2,1,0:T(1,128)S(1)} all-gather(f32[1,1,32]{2,1,0:T(1,128)S(1)} %slice_bitcast_fusion.44), channel_id=1, replica_groups=mesh['hist'=8,'row'=4] {'hist'}, dimensions={0}, use_global_device_ids=true | all-gather | bytes 1152 | tf_op jit(solution)/shard_map/all_gather | solution.py:9
  150.6 1.6 multiply_reduce_fusion.1
  153.5 19.6 %psum.22 = f32[]{:T(128)} all-reduce(f32[]{:T(128)S(6)} %add.177), channel_id=1, replica_groups=mesh['hist'=8,'row'=4] {'hist'}, use_global_device_ids=true, to_apply=%region_7.8 | all-reduce | flops 1 | bytes 8 | tf_op jit(solution)/shard_map/psum | solution.py:141
  174.6 35.6 %all-reduce.5.cloned.1.call-done = f32[2,24,1024]{2,1,0:T(8,128)} async-done(((f32[2,24,1024]{2,1,0:T(8,128)}), f32[2,24,1024]{2,1,0:T(8,128)}) %all-reduce.5.cloned.1.call-update) | async-done | bytes 196624 | tf_op jit(solution)/shard_map/psum | solution.py:142
  210.2 1.6 copy.113
  (121 shorter events, 17.6 us)
Async XLA Ops:
  7.2 3.5 %copy-start = (f32[32,32]{1,0:T(8,128)S(1)}, f32[32,32]{1,0:T(8,128)}, u32[]{:S(2)}) copy-start(f32[32,32]{1,0:T(8,128)} %param.12) | copy-start | bytes 12292
  7.2 6.0 %copy-start.6 = (bf16[2,24,12,1024]{3,1,2,0:T(8,128)(2,1)S(1)}, bf16[2,24,12,1024]{3,1,2,0:T(8,128)(2,1)}, u32[]{:S(2)}) copy-start(bf16[2,24,12,1024]{3,1,2,0:T(8,128)(2,1)} %param.16) | copy-start | bytes 3538948
  7.2 143.4 %all-reduce.3.cloned.1.call-start = ((), (), s32[]{:S(2)}) async-start(), calls=%async_computation | async-start | bytes 262144 | tf_op jit(solution)/shard_map/psum | solution.py:135
  18.1 6.7 %copy-start.7 = (bf16[2,24,12,1024]{3,1,2,0:T(8,128)(2,1)S(1)}, bf16[2,24,12,1024]{3,1,2,0:T(8,128)(2,1)}, u32[]{:S(2)}) copy-start(bf16[2,24,12,1024]{3,1,2,0:T(8,128)(2,1)} %param.17) | copy-start | bytes 3538948
  36.7 37.3 %copy-start.10 = (f32[12,32,32]{2,1,0:T(8,128)}, f32[12,32,32]{2,1,0:T(8,128)S(1)}, u32[]{:S(2)}) copy-start(f32[12,32,32]{2,1,0:T(8,128)S(1)} %get-tuple-element.216) | copy-start | bytes 147460
  36.7 38.3 %copy-start.8 = (f32[12,32,32]{2,1,0:T(8,128)}, f32[12,32,32]{2,1,0:T(8,128)S(1)}, u32[]{:S(2)}) copy-start(f32[12,32,32]{2,1,0:T(8,128)S(1)} %get-tuple-element.217) | copy-start | bytes 147460
  36.7 38.1 %copy-start.5 = (bf16[2,24,12,1024]{3,1,2,0:T(8,128)(2,1)S(1)}, bf16[2,24,12,1024]{3,1,2,0:T(8,128)(2,1)}, u32[]{:S(2)}) copy-start(bf16[2,24,12,1024]{3,1,2,0:T(8,128)(2,1)} %param.15) | copy-start | bytes 3538948
  76.8 3.9 %copy-start.18 = (bf16[24,1024]{1,0:T(8,128)(2,1)S(1)}, bf16[24,1024]{1,0:T(8,128)(2,1)}, u32[]{:S(2)}) copy-start(bf16[24,1024]{1,0:T(8,128)(2,1)} %get-tuple-element.187) | copy-start | bytes 147460
  76.8 4.8 %copy-start.4 = (bf16[24,32,32,1]{2,1,0,3:T(8,128)(2,1)S(1)}, bf16[24,32,32,1]{2,1,0,3:T(8,128)(2,1)}, u32[]{:S(2)}) copy-start(bf16[24,32,32,1]{2,1,0,3:T(8,128)(2,1)} %reshape.261) | copy-start | bytes 147460
  81.6 1.7 copy-start.1
  81.6 2.4 %copy-start.21 = (s32[24]{0:T(128)S(1)}, s32[24]{0:T(128)}, u32[]{:S(2)}) copy-start(s32[24]{0:T(128)} %iota_add_fusion.1) | copy-start | bytes 292
  81.6 2.4 %copy-start.22 = (s32[12]{0:T(128)S(1)}, s32[12]{0:T(128)}, u32[]{:S(2)}) copy-start(s32[12]{0:T(128)} %iota_add_fusion) | copy-start | bytes 148
  84.1 7.0 %copy-start.16 = (bf16[24,32,32,1]{2,1,0,3:T(8,128)(2,1)S(1)}, bf16[24,32,32,1]{2,1,0,3:T(8,128)(2,1)}, u32[]{:S(2)}) copy-start(bf16[24,32,32,1]{2,1,0,3:T(8,128)(2,1)} %reshape.265) | copy-start | bytes 147460
  91.0 2.6 %copy-start.2 = (bf16[2,24,12,32,32]{3,4,1,2,0:T(8,128)(2,1)}, bf16[2,24,12,32,32]{3,4,1,2,0:T(8,128)(2,1)S(1)}, u32[]{:S(2)}) copy-start(bf16[2,24,12,32,32]{3,4,1,2,0:T(8,128)(2,1)S(1)} %get-tuple-element.229) | copy-start | bytes 3538948
  95.9 4.7 %copy-start.3 = (bf16[2,24,12,32,32]{3,4,1,2,0:T(8,128)(2,1)S(1)}, bf16[2,24,12,32,32]{3,4,1,2,0:T(8,128)(2,1)}, u32[]{:S(2)}) copy-start(bf16[2,24,12,32,32]{3,4,1,2,0:T(8,128)(2,1)} %copy-done.2) | copy-start | bytes 3538948
  100.6 2.8 %copy-start.9 = (f32[12,32,32]{2,1,0:T(8,128)S(1)}, f32[12,32,32]{2,1,0:T(8,128)}, u32[]{:S(2)}) copy-start(f32[12,32,32]{2,1,0:T(8,128)} %copy-done.8) | copy-start | bytes 147460
  100.6 7.9 %slice-start = ((s8[4718592]{0:T(1024)(128)(4,1)}), s8[524288]{0:T(1024)(128)(4,1)S(1)}, s32[]{:S(2)}) async-start(s8[4718592]{0:T(1024)(128)(4,1)} %bitcast.183), calls=%async_computation.2 | async-start | bytes 1048576
  102.4 3.5 %copy-start.11 = (f32[12,32,32]{2,1,0:T(8,128)S(1)}, f32[12,32,32]{2,1,0:T(8,128)}, u32[]{:S(2)}) copy-start(f32[12,32,32]{2,1,0:T(8,128)} %copy-done.10) | copy-start | bytes 147460
  103.3 106.9 %all-reduce.5.cloned.1.call-start = ((), (), s32[]{:S(2)}) async-start(), calls=%async_computation.1 | async-start | bytes 393216 | tf_op jit(solution)/shard_map/psum | solution.py:142
  103.3 5.1 %slice-start.1 = ((s8[4718592]{0:T(1024)(128)(4,1)}), s8[4194304]{0:T(1024)(128)(4,1)S(1)}, s32[]{:S(2)}) async-start(s8[4718592]{0:T(1024)(128)(4,1)} %bitcast.183), calls=%async_computation.3 | async-start | bytes 8388608
  109.5 3.5 %copy-start.19 = (f32[12,32]{1,0:T(8,128)S(1)}, f32[12,32]{1,0:T(8,128)}, u32[]{:S(2)}) copy-start(f32[12,32]{1,0:T(8,128)} %param.13) | copy-start | bytes 4612
  109.5 3.6 %copy-start.20 = (f32[12,32]{1,0:T(8,128)S(1)}, f32[12,32]{1,0:T(8,128)}, u32[]{:S(2)}) copy-start(f32[12,32]{1,0:T(8,128)} %param.14) | copy-start | bytes 4612
  109.5 41.1 %copy-start.13 = (f32[1,12,1024]{2,0,1:T(1,128)S(1)}, f32[1,12,1024]{2,0,1:T(1,128)}, u32[]{:S(2)}) copy-start(f32[1,12,1024]{2,0,1:T(1,128)} %copy-done.12) | copy-start | bytes 147460
  109.5 41.1 %copy-start.15 = (f32[1,12,1024]{2,0,1:T(1,128)S(1)}, f32[1,12,1024]{2,0,1:T(1,128)}, u32[]{:S(2)}) copy-start(f32[1,12,1024]{2,0,1:T(1,128)} %copy-done.14) | copy-start | bytes 147460
  (3 other events, 2.3 us)
Sparse Core Ops, SparseCore 0:
  103.4 32.3 all-reduce.2
  140.0 70.1 all-reduce.4
where the time goes:
time: 219 us
  blocking collectives  90.2 us (41%)
  local copies, waits for them, and re-layouts  41.8 us (19%)
  waiting for transfers between devices  35.6 us (16%)
  matrix products  22.8 us (10%)
  between operations  16.6 us (8%)
  other arithmetic  11.3 us (5%)
    all_gather x2, blocking collectives, carried_in(): everything = jax.tree.map(lambda part: lax.all_gather(part, axis), x)  36.5 us
    psum x1, waiting for transfers between devices, shards(): column_term = lax.psum(column_part, 'hist')  35.6 us
    all_gather x1, blocking collectives, shards(): whole_row = lax.all_gather(stacked, 'hist', axis=2, tiled=True)  34 us
    psum x1, blocking collectives, shards(): squares = lax.psum(local_squares, 'hist')  19.6 us
    dot_general x8, matrix products, contract_row(): jnp.einsum('sik,stkj->tij', sigma, hist, preferred_element_type=jnp.float32)  12.5 us
    reshape x2, local copies, waits for them, and re-layouts, shards(): advanced_hist.reshape(2, rows_here, steps_here, bands, bands)  11.6 us
    reshape x2, local copies, waits for them, and re-layouts, shards(): retarded = retarded_hist.reshape(2, rows_here, steps_here, bands, bands)  11.4 us
    dot_general x4, matrix products, contract_column(): jnp.einsum('tsik,sjk->tij', hist, sigma, preferred_element_type=jnp.float32)  8.42 us
  transfers between devices with their start and end apart: 2, of which 1 were waited for; matrix products, arithmetic and copies ran while one was open for 6% of the time, Pallas kernels for 0%

commit v1 on v0

v1 whole, which is shorter than its diff:
```python
import functools

import jax
import jax.numpy as jnp
from jax import lax
from jax.experimental import pallas as pl
from jax.experimental.pallas import tpu as pltpu
from jax.sharding import PartitionSpec as P

F32, BF16 = (jnp.float32, jnp.bfloat16)
HIGHEST = lax.Precision.HIGHEST
EXTRA = 16
VMEM_LIMIT = 48 * 1024 * 1024


def swap_places(x, turn):
    hist_count, row_count = (lax.axis_size("hist"), lax.axis_size("row"))
    ratio = hist_count // row_count
    cores = 2 if row_count % 2 == 0 else 1
    span = row_count // cores
    pairs = []
    for slow in range(row_count):
        for fast in range(ratio):
            for row in range(row_count):
                source = (slow * ratio + fast) * row_count + row
                goal = row % cores * span + (row // cores + 1 + turn) % span
                target = (goal * ratio + (fast + turn) % ratio) * row_count + slow
                pairs.append((source, target))
    return lax.ppermute(x, ("hist", "row"), pairs)


def crossed(x, axis, bit):
    size = lax.axis_size(axis)
    return lax.ppermute(x, axis, [(k, k ^ bit) for k in range(size)])


def lane_block(shape, width):
    return lax.broadcasted_iota(jnp.int32, shape, len(shape) - 1) // width


def swap_blocks(parts):
    width = parts[0].shape[1] // 4
    block = lane_block(parts[0].shape, width)
    parts = list(parts)
    for bit in (2, 1):
        new = list(parts)
        for a in range(4):
            if a & bit == 0:
                low, high = (parts[a], parts[a | bit])
                shift = bit * width
                keep = block & bit == 0
                new[a] = jnp.where(keep, low, pltpu.roll(high, shift, 1))
                new[a | bit] = jnp.where(keep, pltpu.roll(low, 4 * width - shift, 1), high)
        parts = new
    return parts


def energy_kernel(bands, steps, order_ref, less_ref, great_ref, coupling_ref, damping_ref, phases_ref, send_ref, packed_ref, work):
    groups = bands // 4
    chunks = steps // 4
    for which, ref in enumerate((less_ref, great_ref)):
        for part in range(2):
            for chunk in range(chunks):
                blocks = [
                    ref[pl.ds((chunk * 4 + k) * groups * 2 + part, groups, stride=2), :]
                    for k in range(4)
                ]
                for k, block in enumerate(swap_blocks(blocks)):
                    work[which, part, pl.ds(chunk * bands + k, groups, stride=4), :] = block
    less_real, less_imag = (work[0, 0], work[0, 1])
    great_real, great_imag = (work[1, 0], work[1, 1])
    polar = jnp.concatenate(
        [
            -(less_real * great_real + less_imag * great_imag),
            -(less_imag * great_real - less_real * great_imag),
        ],
        axis=0,
    )
    coupling = coupling_ref[...]
    wide = jnp.concatenate([coupling] * 4, axis=1)
    tall = jnp.concatenate([wide] * 4, axis=0)
    at_row = lax.broadcasted_iota(jnp.int32, tall.shape, 0) // bands
    blocked = jnp.where(at_row == lane_block(tall.shape, bands), tall, 0.0)
    half = lax.dot_general(
        polar, blocked, (((1,), (1,)), ((), ())), precision=HIGHEST, preferred_element_type=F32
    )
    rows = chunks * bands
    both = jnp.concatenate([half[:rows], half[rows:]], axis=1)
    screens = []
    for chunk in range(chunks):
        screens.append(
            jnp.dot(
                coupling,
                both[chunk * bands : (chunk + 1) * bands],
                precision=HIGHEST,
                preferred_element_type=F32,
            )
        )
    screen = jnp.concatenate(screens, axis=0)
    lanes = 4 * bands
    screen_real, screen_imag = (screen[:, :lanes], screen[:, lanes:])
    sigma_real = less_real * screen_real - less_imag * screen_imag
    sigma_imag = less_real * screen_imag + less_imag * screen_real
    wide_real = great_real * screen_real + great_imag * screen_imag
    wide_imag = great_imag * screen_real - great_real * screen_imag
    outs = (wide_real - sigma_real, wide_imag - sigma_imag, sigma_real, sigma_imag)
    for chunk in range(chunks):
        at = slice(chunk * bands, (chunk + 1) * bands)
        to = slice(chunk * lanes, (chunk + 1) * lanes)
        for k, out in enumerate(outs):
            first = (chunk * 4 + k) * bands
            send_ref[first : first + bands, :] = out[at].astype(BF16)
        packed_ref[:bands, to] = less_real[at]
        packed_ref[bands:, to] = less_imag[at]
    log_total = jnp.sum(jnp.log(damping_ref[...]), axis=0, keepdims=True)
    phase_total = jnp.sum(phases_ref[...], axis=0, keepdims=True)
    last = steps * bands
    send_ref[last:, :] = jnp.zeros((EXTRA, lanes), BF16)
    send_ref[last:, :bands] = pieces_of((log_total, phase_total)).astype(BF16)


def order_kernel(bands, steps, ratio, order_ref):
    groups = bands // 4
    padded = order_ref.shape[1] // bands
    taken = steps * bands
    source = lax.broadcasted_iota(jnp.int32, (taken, 1), 0)
    band = source % bands
    target = (band % 4) * (groups * padded) + (band // 4) * padded + source // bands
    column = lax.broadcasted_iota(jnp.int32, (taken, order_ref.shape[1]), 1)
    for turn in range(ratio):
        fast = (lax.axis_index("hist") + ratio - turn) % ratio
        hit = column == target + fast * steps
        order_ref[turn * taken : (turn + 1) * taken, :] = jnp.where(hit, 1.0, 0.0).astype(BF16)


def column_kernel(bands, steps, rows, weight, retarded_ref, send_ref, keep_ref, give_ref):
    lanes = 4 * bands
    groups = bands // 4
    hist_start, row_start = (lax.axis_index("hist") * steps, lax.axis_index("row") * rows)
    block = lane_block((bands, lanes), bands)
    later = row_start + lax.broadcasted_iota(jnp.int32, (rows, groups * lanes), 0)
    total = None
    for chunk in range(steps // 4):
        turned = []
        for part in range(2):
            first = (chunk * 4 + 2 + part) * bands
            own = send_ref[first : first + bands, :].astype(F32)
            turned.append([own] + [pltpu.roll(own, d * bands, 1) for d in range(1, 4)])
        for k in range(4):
            step = chunk * 4 + k
            real, imag = [
                jnp.concatenate(
                    [jnp.where(block == b, turned[part][(b - k) % 4], 0.0) for b in range(4)],
                    axis=0,
                )
                for part in range(2)
            ]
            weights = jnp.concatenate(
                [
                    jnp.concatenate([real, imag], axis=1),
                    jnp.concatenate([-imag, real], axis=1),
                ],
                axis=0,
            ).astype(BF16)
            causal = hist_start + step <= later
            halves = []
            for part in range(2):
                whole = jnp.where(causal, retarded_ref[part, step].astype(F32), 0.0)
                halves.append(
                    jnp.concatenate(
                        [whole[:, g * lanes : (g + 1) * lanes] for g in range(groups)], axis=0
                    ).astype(BF16)
                )
            term = lax.dot_general(
                jnp.concatenate(halves, axis=1),
                weights,
                (((1,), (1,)), ((), ())),
                preferred_element_type=F32,
            )
            total = term if total is None else total + term
    low = lax.axis_index("hist") % 2 == 0
    for g in range(groups // 2):
        for part in range(2):
            halves = [
                -weight * total[k * rows : (k + 1) * rows, part * lanes : (part + 1) * lanes]
                for k in (g, g + groups // 2)
            ]
            to = slice((2 * g + part) * rows, (2 * g + part + 1) * rows)
            keep_ref[to, :] = jnp.where(low, halves[0], halves[1])
            give_ref[to, :] = jnp.where(low, halves[1], halves[0])


def add_kernel(own_ref, other_ref, out_ref):
    total = own_ref[...].astype(F32) + other_ref[...].astype(F32)
    out_ref[...] = total.astype(out_ref.dtype)


def final_kernel(count, stepped_ref, own_ref, other_ref, sum_ref, more_ref, row_ref, column_ref):
    squares = (own_ref[...] + other_ref[...])[0:1]
    row_ref[...] = stepped_ref[...] / jnp.sqrt(squares / count + 1e-06)
    low = lax.axis_index("hist") % 2 == 0
    half, back = (sum_ref[...], more_ref[...])
    column = jnp.concatenate([jnp.where(low, half, back), jnp.where(low, back, half)], axis=0)
    rows, lanes = (column_ref.shape[1], column.shape[1])
    for part in range(2):
        for g in range(column_ref.shape[2] // lanes):
            at = (2 * g + part) * rows
            column_ref[part, :, g * lanes : (g + 1) * lanes] = column[at : at + rows]


def row_kernel(bands, steps, rows, weight, ratio, order_ref, lesser_ref, advanced_ref, *refs):
    arrived_refs, out_ref = (refs[:ratio], refs[ratio])
    lanes = 4 * bands
    groups = bands // 4
    padded = order_ref.shape[1] // bands
    depth = groups * padded
    taken = steps * bands
    ordered = None
    for turn, ref in enumerate(arrived_refs):
        sigma = jnp.concatenate([ref[c * lanes : (c + 1) * lanes, :] for c in range(steps // 4)], axis=1)
        term = jnp.dot(
            sigma,
            order_ref[turn * taken : (turn + 1) * taken, :],
            preferred_element_type=F32,
        )
        ordered = term if ordered is None else ordered + term
    lefts = []
    for which in range(2):
        real = ordered[2 * which * bands : (2 * which + 1) * bands]
        imag = ordered[(2 * which + 1) * bands : (2 * which + 2) * bands]
        for pair in ((real, imag), (-imag, real)):
            lefts.append(
                jnp.concatenate(
                    [part[:, k * depth : (k + 1) * depth] for k in range(4) for part in pair],
                    axis=0,
                ).astype(BF16)
            )
    hist_start, row_start = (lax.axis_index("hist") * steps, lax.axis_index("row") * rows)
    earlier = row_start + lax.broadcasted_iota(jnp.int32, (rows, groups * lanes), 0)
    filler = jnp.zeros((padded - rows, lanes), F32)

    def right(which, part, step):
        ref = (lesser_ref, advanced_ref)[which]
        whole = ref[part, step].astype(F32)
        if which == 1:
            whole = jnp.where(earlier <= hist_start + step, whole, 0.0)
        pieces = []
        for g in range(groups):
            pieces.append(whole[:, g * lanes : (g + 1) * lanes])
            if padded > rows:
                pieces.append(filler)
        return jnp.concatenate(pieces, axis=0).astype(BF16)

    block = lane_block((2 * bands, lanes), bands)
    for chunk in range(steps // 4):
        gathered = None
        for pair in range(2):
            first = chunk * 4 + pair * 2
            total = None
            for which in range(2):
                for part in range(2):
                    rights = jnp.concatenate(
                        [right(which, part, first), right(which, part, first + 1)], axis=1
                    )
                    term = jnp.dot(
                        lefts[2 * which + part], rights, preferred_element_type=F32
                    )
                    total = term if total is None else total + term
            for k in range(2):
                own = total[:, k * lanes : (k + 1) * lanes]
                picked = own[: 2 * bands]
                for b in range(1, 4):
                    picked = jnp.where(block == b, own[2 * bands * b : 2 * bands * (b + 1)], picked)
                picked = picked + pltpu.roll(picked, 2 * bands, 1)
                picked = picked + pltpu.roll(picked, bands, 1)
                gathered = (
                    picked if gathered is None else jnp.where(block == 2 * pair + k, picked, gathered)
                )
        out_ref[: 2 * bands, chunk * lanes : (chunk + 1) * lanes] = weight * gathered
    above_log = jnp.zeros((1, bands), F32)
    above_phase = jnp.zeros((1, bands), F32)
    for turn, ref in enumerate(arrived_refs):
        fast = (lax.axis_index("hist") + ratio - turn) % ratio
        later = jnp.where(lax.axis_index("row") * ratio + fast > lax.axis_index("hist"), 1.0, 0.0)
        extra = ref[taken:, :bands].astype(F32)
        above_log = above_log + later * (extra[0:1] + extra[1:2] + extra[2:3])
        above_phase = above_phase + later * (extra[3:4] + extra[4:5] + extra[5:6])
    at = lax.broadcasted_iota(jnp.int32, (8, bands), 0)
    out_ref[2 * bands :, :] = jnp.zeros((8, steps * bands), F32)
    out_ref[2 * bands :, :bands] = jnp.where(at == 0, above_log, jnp.where(at == 1, above_phase, 0.0))


def pieces_of(totals):
    shape = (EXTRA, totals[0].shape[1])
    row = lax.broadcasted_iota(jnp.int32, shape, 0)
    extra = jnp.zeros(shape, F32)
    at = 0
    for total in totals:
        for _ in range(3):
            piece = total.astype(BF16).astype(F32)
            extra = jnp.where(row == at, piece, extra)
            total = total - piece
            at += 1
    return extra


def narrow_kernel(bands, own_ref, other_ref, out_ref):
    total = own_ref[...] + other_ref[...]
    lanes = 4 * bands
    last = total.shape[1] // lanes * 2 * bands
    for k in range(total.shape[1] // lanes):
        part = total[: 2 * bands, k * lanes : (k + 1) * lanes]
        out_ref[2 * bands * k : 2 * bands * (k + 1), :] = part.astype(BF16)
    out_ref[last:, :] = jnp.zeros((EXTRA, lanes), BF16)
    above = total[2 * bands :, :bands]
    out_ref[last:, :bands] = pieces_of((above[0:1], above[1:2])).astype(BF16)


def step_kernel(
    bands, steps, damping_ref, phases_ref, packed_ref, own_ref, other_ref,
    out_ref, square_ref, work
):
    lanes = 4 * bands
    groups = bands // 4
    last = steps // 4 * 2 * bands
    extra = own_ref[last:, :bands].astype(F32) + other_ref[last:, :bands].astype(F32)
    above_log = extra[0:1] + extra[1:2] + extra[2:3]
    above_phase = extra[3:4] + extra[4:5] + extra[5:6]
    at = lax.broadcasted_iota(jnp.int32, (steps, bands), 0)
    rates = jnp.log(damping_ref[...])
    phases = phases_ref[...]
    summed_log = jnp.broadcast_to(above_log, (steps, bands))
    summed_phase = jnp.broadcast_to(above_phase, (steps, bands))
    for step in range(steps):
        summed_log = summed_log + jnp.where(at <= step, rates[step : step + 1], 0.0)
        summed_phase = summed_phase + jnp.where(at <= step, phases[step : step + 1], 0.0)
    magnitude = jnp.exp(summed_log)
    both = jnp.concatenate(
        [magnitude * jnp.cos(summed_phase), -magnitude * jnp.sin(summed_phase)], axis=1
    )
    wide = lax.broadcasted_iota(jnp.int32, (steps, steps * bands), 1) // bands
    place = lax.broadcasted_iota(jnp.int32, (steps, steps * bands), 0)
    spreading = jnp.where(wide == place, 1.0, 0.0)
    factor = lax.dot_general(
        both, spreading, (((0,), (0,)), ((), ())), precision=HIGHEST, preferred_element_type=F32
    )
    collision = own_ref[:last, :].astype(F32) + other_ref[:last, :].astype(F32)
    chunks = [collision[2 * bands * k : 2 * bands * (k + 1)] for k in range(steps // 4)]
    row = packed_ref[...] + jnp.concatenate(chunks, axis=1)
    row_real, row_imag = (row[:bands], row[bands:])
    factor_real, factor_imag = (factor[:bands], factor[bands:])
    stepped = (
        factor_real * row_real - factor_imag * row_imag,
        factor_real * row_imag + factor_imag * row_real,
    )
    squares = jnp.sum(stepped[0] * stepped[0] + stepped[1] * stepped[1], keepdims=True)
    square_ref[...] = jnp.broadcast_to(squares, square_ref.shape)
    for part in range(2):
        for chunk in range(steps // 4):
            work[part, chunk] = stepped[part][:, chunk * lanes : (chunk + 1) * lanes]
    for part in range(2):
        for chunk in range(steps // 4):
            blocks = [work[part, chunk, pl.ds(k, groups, stride=4), :] for k in range(4)]
            for k, block in enumerate(swap_blocks(blocks)):
                first = (chunk * 4 + k) * groups * 2 + part
                out_ref[pl.ds(first, groups, stride=2), :] = block


def call(kernel, shapes, scratch, flops, moved, spaces, *operands):
    return pl.pallas_call(
        kernel,
        out_shape=shapes,
        in_specs=[pl.BlockSpec(memory_space=space) for space in spaces],
        out_specs=[pl.BlockSpec(memory_space=pltpu.VMEM)] * len(shapes),
        scratch_shapes=scratch,
        compiler_params=pltpu.CompilerParams(vmem_limit_bytes=VMEM_LIMIT),
        cost_estimate=pl.CostEstimate(flops=flops, bytes_accessed=moved, transcendentals=0),
    )(*operands)


def shards(
    row_less, row_great, coupling, damping, phases, lesser_hist, advanced_hist, retarded_hist
):
    bands = coupling.shape[0]
    lanes = 4 * bands
    groups = bands // 4
    steps = row_less.shape[1]
    rows = lesser_hist.shape[1]
    hist_count, row_count = (lax.axis_size("hist"), lax.axis_size("row"))
    ratio = hist_count // row_count
    all_steps = steps * hist_count
    weight = float(all_steps * bands) ** (-0.5)
    padded = -(-rows // 16) * 16
    taken = steps * bands
    sds = jax.ShapeDtypeStruct

    def grouped(x):
        x = x.reshape(2, steps, groups, lanes).transpose(1, 2, 0, 3)
        return x.reshape(steps * groups * 2, lanes)

    retarded = retarded_hist.transpose(0, 2, 1, 3)
    vmem = pltpu.VMEM
    (order,) = call(
        functools.partial(order_kernel, bands, steps, ratio),
        [sds((ratio * taken, bands * padded), BF16)],
        [],
        10**10,
        10**7,
        [],
    )
    send, packed = call(
        functools.partial(energy_kernel, bands, steps),
        [sds((taken + EXTRA, lanes), BF16), sds((2 * bands, taken), F32)],
        [vmem((2, 2, steps // 4 * bands, lanes), F32)],
        10**8,
        10**6,
        [pl.ANY] + [vmem] * 5,
        order,
        grouped(row_less),
        grouped(row_great),
        coupling,
        damping,
        phases,
    )
    arrived = [swap_places(send, turn) for turn in range(ratio)]
    column, give = call(
        functools.partial(column_kernel, bands, steps, rows, weight),
        [sds((groups * rows, lanes), F32)] * 2,
        [],
        10**9,
        4 * 10**6,
        [vmem] * 2,
        retarded,
        send,
    )

    def add(own, other, kind):
        (out,) = call(
            add_kernel, [sds(own.shape, kind)], [], 10**10, 10**6, [vmem] * 2, own, other
        )
        return out

    got = crossed(give, "hist", 1)
    order, got = lax.optimization_barrier((order, got))
    (partial_row,) = call(
        functools.partial(row_kernel, bands, steps, rows, weight, ratio),
        [sds((2 * bands + 8, taken), F32)],
        [],
        10**6,
        10**6,
        [vmem] * (3 + ratio),
        order,
        lesser_hist.transpose(0, 2, 1, 3),
        advanced_hist.transpose(0, 2, 1, 3),
        *arrived,
    )
    other = crossed(partial_row, "row", 1)
    bit = 2
    while 2 * bit < row_count:
        partial_row = add(partial_row, other, F32)
        other = crossed(partial_row, "row", bit)
        bit *= 2
    (narrow,) = call(
        functools.partial(narrow_kernel, bands),
        [sds((steps // 4 * 2 * bands + EXTRA, lanes), BF16)],
        [],
        10**6,
        10**6,
        [vmem] * 2,
        partial_row,
        other,
    )
    other = crossed(narrow, "row", bit)
    column = add(column, got, BF16)
    got = crossed(column, "hist", hist_count // 2)
    stepped, squares = call(
        functools.partial(step_kernel, bands, steps),
        [sds((steps * groups * 2, lanes), F32), sds((8, lanes), F32)],
        [vmem((2, steps // 4, bands, lanes), F32)],
        10**10,
        10**6,
        [vmem] * 5,
        damping,
        phases,
        packed,
        narrow,
        other,
    )
    ahead = [hist_count >> k for k in range(1, hist_count.bit_length() - 1)]
    beside = ahead[1:] + [1, None]
    for bit, each in zip([1] + ahead, beside):
        other = crossed(squares, "hist", bit)
        if each:
            column = add(column, got, BF16 if each == 2 else F32)
            got = crossed(column, "hist", each)
            squares = add(squares, other, F32)
    got, other = lax.optimization_barrier((got, other))
    stepped, column = call(
        functools.partial(final_kernel, float(2 * all_steps * bands * bands)),
        [sds(stepped.shape, F32), sds((2, rows, bands * bands), F32)],
        [],
        10**6,
        10**6,
        [vmem] * 5,
        stepped,
        squares,
        other,
        column,
        got,
    )
    stepped = stepped.reshape(steps, groups, 2, lanes).transpose(2, 0, 1, 3)
    return (stepped.reshape(2, steps, bands * bands), column)


def solution(mesh):
    return jax.shard_map(
        shards,
        mesh=mesh,
        in_specs=(
            P(None, "hist", None),
            P(None, "hist", None),
            P(),
            P("hist", None),
            P("hist", None),
            P(None, "row", "hist", None),
            P(None, "row", "hist", None),
            P(None, "row", "hist", None),
        ),
        out_specs=(P(None, "hist", None), P(None, "row", None)),
        check_vma=False,
    )
```

time: 219 us -> 34.9 us (0.16)
  blocking collectives: 90.2 us -> 0 us
  local copies, waits for them, and re-layouts: 41.8 us -> 0.55 us
  matrix products: 22.8 us -> 0 us
  waiting for transfers between devices: 35.6 us -> 16.6 us
  between operations: 16.6 us -> 0.75 us
  starting transfers between devices: 0.08 us -> 11.9 us
  other arithmetic: 11.3 us -> 0 us
  Pallas kernels: 0 us -> 4.83 us
    all_gather x3 -> x0, blocking collectives: 70.5 us -> none  [the longest x2 36.5 us: carried_in(): everything = jax.tree.map(lambda part: lax.all_gather(part, axis), x)]
    psum x2 -> x0, waiting for transfers between devices: 35.6 us -> none  [the longest x1 35.6 us: shards(): column_term = lax.psum(column_part, 'hist')]
    reshape x6 -> x0, local copies, waits for them, and re-layouts: 23.3 us -> none  [the longest x2 11.6 us: shards(): advanced_hist.reshape(2, rows_here, steps_here, bands, bands)]
    dot_general x16 -> x0, matrix products: 22.8 us -> none  [the longest x8 12.5 us: contract_row(): jnp.einsum('sik,stkj->tij', sigma, hist, preferred_element_type=jnp.float32)]
    psum x1 -> x0, blocking collectives: 19.6 us -> none  [shards(): squares = lax.psum(local_squares, 'hist')]
    ppermute x0 -> x11, waiting for transfers between devices: none -> 16.6 us  [the longest x9 16.6 us: crossed(): return lax.ppermute(x, axis, [(k, k ^ bit) for k in range(size)])]
    ppermute x0 -> x11, starting transfers between devices: none -> 11.9 us  [the longest x9 8.01 us: crossed(): return lax.ppermute(x, axis, [(k, k ^ bit) for k in range(size)])]
    squeeze x6 -> x0, local copies, waits for them, and re-layouts: 8.27 us -> none  [the longest x1 2.82 us: shards(): lesser[0]]
  transfers between devices with their start and end apart: 2 -> 11, of which waited for: 1 -> 8; matrix products, arithmetic and copies ran while one was open for 6% -> 0% of each run, Pallas kernels for 0% -> 4%
where the time goes in v1:
time: 34.9 us; the launch traced here: 34.7 us
  waiting for transfers between devices  16.6 us (48%)
  starting transfers between devices  11.9 us (34%)
  Pallas kernels  4.83 us (14%)
  between operations  0.75 us (2%)
  local copies, waits for them, and re-layouts  0.55 us (2%)
    ppermute x9, waiting for transfers between devices, crossed(): return lax.ppermute(x, axis, [(k, k ^ bit) for k in range(size)])  16.6 us
    ppermute x9, starting transfers between devices, crossed(): return lax.ppermute(x, axis, [(k, k ^ bit) for k in range(size)])  8.01 us
    pallas_call x12, Pallas kernels, call(): pl.pallas_call(kernel, out_shape=shapes, in_specs=[pl.BlockSpec(memory_sp...  4.83 us
    ppermute x2, starting transfers between devices, swap_places(): return lax.ppermute(x, ('hist', 'row'), pairs)  3.9 us
  transfers between devices with their start and end apart: 11, of which 8 were waited for; matrix products, arithmetic and copies ran while one was open for 0% of the time, Pallas kernels for 4%

profile of v1, /device:TPU:0, one launch (start us, length us, event | category | flops | bytes accessed | tf_op | source)
XLA Modules:
  0.0 34.7 jit_solution(18065091104531064071)
XLA Ops:
  0.7 0.4 %shard_map.95.order_ref = bf16[768,1024]{1,0:T(8,128)(2,1)S(1)} custom-call(), custom_call_target="tpu_custom_call" | custom-call | flops 10000000000 | bytes 10000000 | tf_op jit(solution)/shard_map/pallas_call | solution.py:370
  1.1 0.2 copy-done.6
  1.6 0.8 %shard_map.96 = (bf16[400,128]{1,0:T(8,128)(2,1)S(1)}, f32[64,384]{1,0:T(8,128)S(1)}) custom-call(bf16[768,1024]{1,0:T(8,128)(2,1)S(1)} %shard_map.95.order_ref, f32[192,128]{1,0:T(8,128)S(1)} %bitcast.20, f32[192,128]{1,0:T(8,128)S(1)} %bitcast.21, f32[32,32]{1,0:T(8,128)S(1)} %copy-done.4, f32[12,32]{1,0:T(8,128)S(1)} %copy-done.5, f32[12,32]{1,0:T(8,128)S(1)} %copy-done.6), custom_call_target="tpu_custom_call" | custom-call | flops 100000000 | bytes 1000000 | tf_op jit(solution)/shard_map/pallas_call | solution.py:370
  2.4 3.0 %collective-permute-start.2 = (bf16[400,128]{1,0:T(8,128)(2,1)S(1)}, bf16[400,128]{1,0:T(8,128)(2,1)S(1)}, u32[]{:S(2)}, u32[]{:S(2)}) collective-permute-start(bf16[400,128]{1,0:T(8,128)(2,1)S(1)} %get-tuple-element.15.send_ref), channel_id=1, source_target_pairs={{0,4},{1,20},{2,12},{3,28},{4,0},{5,16},{6,8},{7,24},{8,5},{9,21},... | collective-permute-start | bytes 307208 | tf_op jit(solution)/shard_map/ppermute | solution.py:29
  5.4 0.9 %collective-permute-start.1 = (bf16[400,128]{1,0:T(8,128)(2,1)S(1)}, bf16[400,128]{1,0:T(8,128)(2,1)S(1)}, u32[]{:S(2)}, u32[]{:S(2)}) collective-permute-start(bf16[400,128]{1,0:T(8,128)(2,1)S(1)} %get-tuple-element.15.send_ref), channel_id=1, source_target_pairs={{0,8},{1,24},{2,0},{3,16},{4,12},{5,28},{6,4},{7,20},{8,9},{9,25},... | collective-permute-start | bytes 307208 | tf_op jit(solution)/shard_map/ppermute | solution.py:29
  6.3 0.7 %shard_map.97 = (f32[192,128]{1,0:T(8,128)S(1)}, f32[192,128]{1,0:T(8,128)S(1)}) custom-call(bf16[2,12,24,1024]{3,2,1,0:T(8,128)(2,1)S(1)} %bitcast.22, bf16[400,128]{1,0:T(8,128)(2,1)S(1)} %get-tuple-element.15.send_ref), custom_call_target="tpu_custom_call" | custom-call | flops 1000000000 | bytes 4000000 | tf_op jit(solution)/shard_map/pallas_call | solution.py:370
  7.1 0.8 %collective-permute-start = (f32[192,128]{1,0:T(8,128)S(1)}, f32[192,128]{1,0:T(8,128)S(1)}, u32[]{:S(2)}, u32[]{:S(2)}) collective-permute-start(f32[192,128]{1,0:T(8,128)S(1)} %get-tuple-element.16), channel_id=1, source_target_pairs={{0,4},{4,0},{8,12},{12,8},{16,20},{20,16},{24,28},{28,24},{1,5},{5... | collective-permute-start | bytes 294920 | tf_op jit(solution)/shard_map/ppermute | solution.py:34
  7.9 6.5 %collective-permute-done.other_ref = f32[192,128]{1,0:T(8,128)S(1)} collective-permute-done((f32[192,128]{1,0:T(8,128)S(1)}, f32[192,128]{1,0:T(8,128)S(1)}, u32[]{:S(2)}, u32[]{:S(2)}) %collective-permute-start) | collective-permute-done | bytes 98336 | tf_op jit(solution)/shard_map/ppermute | solution.py:34
  14.4 1.5 %shard_map.98.own_ref = f32[72,384]{1,0:T(8,128)S(1)} custom-call(bf16[768,1024]{1,0:T(8,128)(2,1)S(1)} %shard_map.95.order_ref, bf16[2,12,24,1024]{3,2,1,0:T(8,128)(2,1)S(1)} %bitcast.18, bf16[2,12,24,1024]{3,2,1,0:T(8,128)(2,1)S(1)} %bitcast.19, bf16[400,128]{1,0:T(8,128)(2,1)S(1)} %collective-permute-done.1.refs_0_, ...), custom_call_target="tpu_custom_call" | custom-call | flops 1000000 | bytes 1000000 | tf_op jit(solution)/shard_map/pallas_call | solution.py:370
  16.1 1.2 %collective-permute-done.3.other_ref = f32[72,384]{1,0:T(8,128)S(1)} collective-permute-done((f32[72,384]{1,0:T(8,128)S(1)}, f32[72,384]{1,0:T(8,128)S(1)}, u32[]{:S(2)}, u32[]{:S(2)}) %collective-permute-start.3) | collective-permute-done | bytes 110624 | tf_op jit(solution)/shard_map/ppermute | solution.py:34
  17.3 2.0 %collective-permute-start.4 = (bf16[208,128]{1,0:T(8,128)(2,1)S(1)}, bf16[208,128]{1,0:T(8,128)(2,1)S(1)}, u32[]{:S(2)}, u32[]{:S(2)}) collective-permute-start(bf16[208,128]{1,0:T(8,128)(2,1)S(1)} %shard_map.99.own_ref), channel_id=1, source_target_pairs={{0,2},{1,3},{2,0},{3,1},{4,6},{5,7},{6,4},{7,5},{8,10},{9,11},{10,... | collective-permute-start | bytes 159752 | tf_op jit(solution)/shard_map/ppermute | solution.py:34
  19.4 0.4 %collective-permute-start.7 = (bf16[192,128]{1,0:T(8,128)(2,1)S(1)}, bf16[192,128]{1,0:T(8,128)(2,1)S(1)}, u32[]{:S(2)}, u32[]{:S(2)}) collective-permute-start(bf16[192,128]{1,0:T(8,128)(2,1)S(1)} %shard_map.103.own_ref), channel_id=1, source_target_pairs={{0,16},{4,20},{8,24},{12,28},{16,0},{20,4},{24,8},{28,12},{1,17},{... | collective-permute-start | bytes 147464 | tf_op jit(solution)/shard_map/ppermute | solution.py:34
  19.7 1.8 %collective-permute-done.4.other_ref = bf16[208,128]{1,0:T(8,128)(2,1)S(1)} collective-permute-done((bf16[208,128]{1,0:T(8,128)(2,1)S(1)}, bf16[208,128]{1,0:T(8,128)(2,1)S(1)}, u32[]{:S(2)}, u32[]{:S(2)}) %collective-permute-start.4) | collective-permute-done | bytes 53280 | tf_op jit(solution)/shard_map/ppermute | solution.py:34
  21.5 0.6 %shard_map.100 = (f32[192,128]{1,0:T(8,128)S(1)}, f32[8,128]{1,0:T(8,128)S(1)}) custom-call(f32[12,32]{1,0:T(8,128)S(1)} %copy-done.5, f32[12,32]{1,0:T(8,128)S(1)} %copy-done.6, f32[64,384]{1,0:T(8,128)S(1)} %get-tuple-element.14.packed_ref, bf16[208,128]{1,0:T(8,128)(2,1)S(1)} %shard_map.99.own_ref, bf16[208,128]{1,0:T(8,128)(2,1)S(1)} %collective-permute-done.4.other_ref), custom_call_target="tpu_custom_call" | custom-call | flops 10000000000 | bytes 1000000 | tf_op jit(solution)/shard_map/pallas_call | solution.py:370
  22.1 1.0 %collective-permute-start.5 = (f32[8,128]{1,0:T(8,128)S(1)}, f32[8,128]{1,0:T(8,128)S(1)}, u32[]{:S(2)}, u32[]{:S(2)}) collective-permute-start(f32[8,128]{1,0:T(8,128)S(1)} %get-tuple-element.19.own_ref), channel_id=1, source_target_pairs={{0,4},{4,0},{8,12},{12,8},{16,20},{20,16},{24,28},{28,24},{1,5},{5... | collective-permute-start | bytes 12296 | tf_op jit(solution)/shard_map/ppermute | solution.py:34
  23.1 1.8 %collective-permute-done.7.other_ref = bf16[192,128]{1,0:T(8,128)(2,1)S(1)} collective-permute-done((bf16[192,128]{1,0:T(8,128)(2,1)S(1)}, bf16[192,128]{1,0:T(8,128)(2,1)S(1)}, u32[]{:S(2)}, u32[]{:S(2)}) %collective-permute-start.7) | collective-permute-done | bytes 49184 | tf_op jit(solution)/shard_map/ppermute | solution.py:34
  25.0 0.8 %collective-permute-done.5.other_ref = f32[8,128]{1,0:T(8,128)S(1)} collective-permute-done((f32[8,128]{1,0:T(8,128)S(1)}, f32[8,128]{1,0:T(8,128)S(1)}, u32[]{:S(2)}, u32[]{:S(2)}) %collective-permute-start.5) | collective-permute-done | bytes 4128 | tf_op jit(solution)/shard_map/ppermute | solution.py:34
  25.8 1.8 %collective-permute-start.6 = (f32[8,128]{1,0:T(8,128)S(1)}, f32[8,128]{1,0:T(8,128)S(1)}, u32[]{:S(2)}, u32[]{:S(2)}) collective-permute-start(f32[8,128]{1,0:T(8,128)S(1)} %shard_map.101.own_ref), channel_id=1, source_target_pairs={{0,16},{4,20},{8,24},{12,28},{16,0},{20,4},{24,8},{28,12},{1,17},{... | collective-permute-start | bytes 12296 | tf_op jit(solution)/shard_map/ppermute | solution.py:34
  27.6 1.4 %collective-permute-done.8.other_ref = bf16[192,128]{1,0:T(8,128)(2,1)S(1)} collective-permute-done((bf16[192,128]{1,0:T(8,128)(2,1)S(1)}, bf16[192,128]{1,0:T(8,128)(2,1)S(1)}, u32[]{:S(2)}, u32[]{:S(2)}) %collective-permute-start.8) | collective-permute-done | bytes 49184 | tf_op jit(solution)/shard_map/ppermute | solution.py:34
  29.1 0.5 %collective-permute-start.9 = (f32[192,128]{1,0:T(8,128)S(1)}, f32[192,128]{1,0:T(8,128)S(1)}, u32[]{:S(2)}, u32[]{:S(2)}) collective-permute-start(f32[192,128]{1,0:T(8,128)S(1)} %shard_map.105.sum_ref), channel_id=1, source_target_pairs={{0,4},{4,0},{8,12},{12,8},{16,20},{20,16},{24,28},{28,24},{1,5},{5... | collective-permute-start | bytes 294920 | tf_op jit(solution)/shard_map/ppermute | solution.py:34
  29.5 0.8 %collective-permute-done.6.other_ref = f32[8,128]{1,0:T(8,128)S(1)} collective-permute-done((f32[8,128]{1,0:T(8,128)S(1)}, f32[8,128]{1,0:T(8,128)S(1)}, u32[]{:S(2)}, u32[]{:S(2)}) %collective-permute-start.6) | collective-permute-done | bytes 4128 | tf_op jit(solution)/shard_map/ppermute | solution.py:34
  30.3 1.2 %collective-permute-start.10 = (f32[8,128]{1,0:T(8,128)S(1)}, f32[8,128]{1,0:T(8,128)S(1)}, u32[]{:S(2)}, u32[]{:S(2)}) collective-permute-start(f32[8,128]{1,0:T(8,128)S(1)} %shard_map.102.own_ref), channel_id=1, source_target_pairs={{0,8},{4,12},{8,0},{12,4},{16,24},{20,28},{24,16},{28,20},{1,9},{5... | collective-permute-start | bytes 12296 | tf_op jit(solution)/shard_map/ppermute | solution.py:34
  31.5 2.4 %collective-permute-done.10.other_ref = f32[8,128]{1,0:T(8,128)S(1)} collective-permute-done((f32[8,128]{1,0:T(8,128)S(1)}, f32[8,128]{1,0:T(8,128)S(1)}, u32[]{:S(2)}, u32[]{:S(2)}) %collective-permute-start.10) | collective-permute-done | bytes 4128 | tf_op jit(solution)/shard_map/ppermute | solution.py:34
  33.9 0.7 %shard_map.106 = (f32[192,128]{1,0:T(8,128)}, f32[2,24,1024]{2,1,0:T(8,128)}) custom-call(f32[192,128]{1,0:T(8,128)S(1)} %get-tuple-element.18.stepped_ref, f32[8,128]{1,0:T(8,128)S(1)} %shard_map.102.own_ref, f32[8,128]{1,0:T(8,128)S(1)} %collective-permute-done.10.other_ref, f32[192,128]{1,0:T(8,128)S(1)} %shard_map.105.sum_ref, ...), custom_call_target="tpu_custom_call" | custom-call | flops 1000000 | bytes 1000000 | tf_op jit(solution)/shard_map/pallas_call | solution.py:370
  (26 shorter events, 0.7 us)
Async XLA Ops:
  0.6 0.7 %copy-start.6 = (f32[12,32]{1,0:T(8,128)S(1)}, f32[12,32]{1,0:T(8,128)}, u32[]{:S(2)}) copy-start(f32[12,32]{1,0:T(8,128)} %phases_ref.3) | copy-start | bytes 4612
  0.6 0.7 %copy-start.5 = (f32[12,32]{1,0:T(8,128)S(1)}, f32[12,32]{1,0:T(8,128)}, u32[]{:S(2)}) copy-start(f32[12,32]{1,0:T(8,128)} %damping_ref.3) | copy-start | bytes 4612
  0.7 0.7 %copy-start.4 = (f32[32,32]{1,0:T(8,128)S(1)}, f32[32,32]{1,0:T(8,128)}, u32[]{:S(2)}) copy-start(f32[32,32]{1,0:T(8,128)} %coupling_ref.1) | copy-start | bytes 12292
  0.7 0.9 %copy-start.3 = (f32[2,12,1024]{2,0,1:T(2,128)S(1)}, f32[2,12,1024]{2,0,1:T(2,128)}, u32[]{:S(2)}) copy-start(f32[2,12,1024]{2,0,1:T(2,128)} %param.9) | copy-start | bytes 294916
  0.7 0.9 %copy-start.2 = (f32[2,12,1024]{2,0,1:T(2,128)S(1)}, f32[2,12,1024]{2,0,1:T(2,128)}, u32[]{:S(2)}) copy-start(f32[2,12,1024]{2,0,1:T(2,128)} %param.8) | copy-start | bytes 294916
  1.1 5.2 %copy-start.7 = (bf16[2,24,12,1024]{3,1,2,0:T(8,128)(2,1)S(1)}, bf16[2,24,12,1024]{3,1,2,0:T(8,128)(2,1)}, u32[]{:S(2)}) copy-start(bf16[2,24,12,1024]{3,1,2,0:T(8,128)(2,1)} %param.15) | copy-start | bytes 3538948
  2.4 12.0 %collective-permute-start.2 = (bf16[400,128]{1,0:T(8,128)(2,1)S(1)}, bf16[400,128]{1,0:T(8,128)(2,1)S(1)}, u32[]{:S(2)}, u32[]{:S(2)}) collective-permute-start(bf16[400,128]{1,0:T(8,128)(2,1)S(1)} %get-tuple-element.15.send_ref), channel_id=1, source_target_pairs={{0,4},{1,20},{2,12},{3,28},{4,0},{5,16},{6,8},{7,24},{8,5},{9,21},... | collective-permute-start | bytes 307208 | tf_op jit(solution)/shard_map/ppermute | solution.py:29
  5.4 9.0 %collective-permute-start.1 = (bf16[400,128]{1,0:T(8,128)(2,1)S(1)}, bf16[400,128]{1,0:T(8,128)(2,1)S(1)}, u32[]{:S(2)}, u32[]{:S(2)}) collective-permute-start(bf16[400,128]{1,0:T(8,128)(2,1)S(1)} %get-tuple-element.15.send_ref), channel_id=1, source_target_pairs={{0,8},{1,24},{2,0},{3,16},{4,12},{5,28},{6,4},{7,20},{8,9},{9,25},... | collective-permute-start | bytes 307208 | tf_op jit(solution)/shard_map/ppermute | solution.py:29
  6.3 8.1 %copy-start = (bf16[2,24,12,1024]{3,1,2,0:T(8,128)(2,1)S(1)}, bf16[2,24,12,1024]{3,1,2,0:T(8,128)(2,1)}, u32[]{:S(2)}) copy-start(bf16[2,24,12,1024]{3,1,2,0:T(8,128)(2,1)} %param.13) | copy-start | bytes 3538948
  6.3 8.1 %copy-start.1 = (bf16[2,24,12,1024]{3,1,2,0:T(8,128)(2,1)S(1)}, bf16[2,24,12,1024]{3,1,2,0:T(8,128)(2,1)}, u32[]{:S(2)}) copy-start(bf16[2,24,12,1024]{3,1,2,0:T(8,128)(2,1)} %param.14) | copy-start | bytes 3538948
  7.1 7.3 %collective-permute-start = (f32[192,128]{1,0:T(8,128)S(1)}, f32[192,128]{1,0:T(8,128)S(1)}, u32[]{:S(2)}, u32[]{:S(2)}) collective-permute-start(f32[192,128]{1,0:T(8,128)S(1)} %get-tuple-element.16), channel_id=1, source_target_pairs={{0,4},{4,0},{8,12},{12,8},{16,20},{20,16},{24,28},{28,24},{1,5},{5... | collective-permute-start | bytes 294920 | tf_op jit(solution)/shard_map/ppermute | solution.py:34
  15.9 1.4 %collective-permute-start.3 = (f32[72,384]{1,0:T(8,128)S(1)}, f32[72,384]{1,0:T(8,128)S(1)}, u32[]{:S(2)}, u32[]{:S(2)}) collective-permute-start(f32[72,384]{1,0:T(8,128)S(1)} %shard_map.98.own_ref), channel_id=1, source_target_pairs={{0,1},{1,0},{2,3},{3,2},{4,5},{5,4},{6,7},{7,6},{8,9},{9,8},{10,11... | collective-permute-start | bytes 331784 | tf_op jit(solution)/shard_map/ppermute | solution.py:34
  17.3 4.2 %collective-permute-start.4 = (bf16[208,128]{1,0:T(8,128)(2,1)S(1)}, bf16[208,128]{1,0:T(8,128)(2,1)S(1)}, u32[]{:S(2)}, u32[]{:S(2)}) collective-permute-start(bf16[208,128]{1,0:T(8,128)(2,1)S(1)} %shard_map.99.own_ref), channel_id=1, source_target_pairs={{0,2},{1,3},{2,0},{3,1},{4,6},{5,7},{6,4},{7,5},{8,10},{9,11},{10,... | collective-permute-start | bytes 159752 | tf_op jit(solution)/shard_map/ppermute | solution.py:34
  19.4 5.5 %collective-permute-start.7 = (bf16[192,128]{1,0:T(8,128)(2,1)S(1)}, bf16[192,128]{1,0:T(8,128)(2,1)S(1)}, u32[]{:S(2)}, u32[]{:S(2)}) collective-permute-start(bf16[192,128]{1,0:T(8,128)(2,1)S(1)} %shard_map.103.own_ref), channel_id=1, source_target_pairs={{0,16},{4,20},{8,24},{12,28},{16,0},{20,4},{24,8},{28,12},{1,17},{... | collective-permute-start | bytes 147464 | tf_op jit(solution)/shard_map/ppermute | solution.py:34
  22.1 3.7 %collective-permute-start.5 = (f32[8,128]{1,0:T(8,128)S(1)}, f32[8,128]{1,0:T(8,128)S(1)}, u32[]{:S(2)}, u32[]{:S(2)}) collective-permute-start(f32[8,128]{1,0:T(8,128)S(1)} %get-tuple-element.19.own_ref), channel_id=1, source_target_pairs={{0,4},{4,0},{8,12},{12,8},{16,20},{20,16},{24,28},{28,24},{1,5},{5... | collective-permute-start | bytes 12296 | tf_op jit(solution)/shard_map/ppermute | solution.py:34
  24.9 4.2 %collective-permute-start.8 = (bf16[192,128]{1,0:T(8,128)(2,1)S(1)}, bf16[192,128]{1,0:T(8,128)(2,1)S(1)}, u32[]{:S(2)}, u32[]{:S(2)}) collective-permute-start(bf16[192,128]{1,0:T(8,128)(2,1)S(1)} %shard_map.104.own_ref), channel_id=1, source_target_pairs={{0,8},{4,12},{8,0},{12,4},{16,24},{20,28},{24,16},{28,20},{1,9},{5... | collective-permute-start | bytes 147464 | tf_op jit(solution)/shard_map/ppermute | solution.py:34
  25.8 4.5 %collective-permute-start.6 = (f32[8,128]{1,0:T(8,128)S(1)}, f32[8,128]{1,0:T(8,128)S(1)}, u32[]{:S(2)}, u32[]{:S(2)}) collective-permute-start(f32[8,128]{1,0:T(8,128)S(1)} %shard_map.101.own_ref), channel_id=1, source_target_pairs={{0,16},{4,20},{8,24},{12,28},{16,0},{20,4},{24,8},{28,12},{1,17},{... | collective-permute-start | bytes 12296 | tf_op jit(solution)/shard_map/ppermute | solution.py:34
  29.1 4.9 %collective-permute-start.9 = (f32[192,128]{1,0:T(8,128)S(1)}, f32[192,128]{1,0:T(8,128)S(1)}, u32[]{:S(2)}, u32[]{:S(2)}) collective-permute-start(f32[192,128]{1,0:T(8,128)S(1)} %shard_map.105.sum_ref), channel_id=1, source_target_pairs={{0,4},{4,0},{8,12},{12,8},{16,20},{20,16},{24,28},{28,24},{1,5},{5... | collective-permute-start | bytes 294920 | tf_op jit(solution)/shard_map/ppermute | solution.py:34
  30.3 3.6 %collective-permute-start.10 = (f32[8,128]{1,0:T(8,128)S(1)}, f32[8,128]{1,0:T(8,128)S(1)}, u32[]{:S(2)}, u32[]{:S(2)}) collective-permute-start(f32[8,128]{1,0:T(8,128)S(1)} %shard_map.102.own_ref), channel_id=1, source_target_pairs={{0,8},{4,12},{8,0},{12,4},{16,24},{20,28},{24,16},{28,20},{1,9},{5... | collective-permute-start | bytes 12296 | tf_op jit(solution)/shard_map/ppermute | solution.py:34

commit v2 on v1

--- a/solution.py
+++ b/solution.py
@@ -10,6 +10,7 @@
 F32, BF16 = (jnp.float32, jnp.bfloat16)
 HIGHEST = lax.Precision.HIGHEST
 EXTRA = 16
+WINDOW = 16
 VMEM_LIMIT = 48 * 1024 * 1024
 
 
@@ -121,15 +122,14 @@
 
 def order_kernel(bands, steps, ratio, order_ref):
     groups = bands // 4
-    padded = order_ref.shape[1] // bands
     taken = steps * bands
     source = lax.broadcasted_iota(jnp.int32, (taken, 1), 0)
     band = source % bands
-    target = (band % 4) * (groups * padded) + (band // 4) * padded + source // bands
+    target = (band % 4) * (groups * WINDOW) + (band // 4) * WINDOW + source // bands
     column = lax.broadcasted_iota(jnp.int32, (taken, order_ref.shape[1]), 1)
     for turn in range(ratio):
         fast = (lax.axis_index("hist") + ratio - turn) % ratio
-        hit = column == target + fast * steps
+        hit = column == target + fast * steps % 8
         order_ref[turn * taken : (turn + 1) * taken, :] = jnp.where(hit, 1.0, 0.0).astype(BF16)
 
 
@@ -208,64 +208,59 @@
             column_ref[part, :, g * lanes : (g + 1) * lanes] = column[at : at + rows]
 
 
-def row_kernel(bands, steps, rows, weight, ratio, order_ref, lesser_ref, advanced_ref, *refs):
-    arrived_refs, out_ref = (refs[:ratio], refs[ratio])
+def row_kernel(bands, steps, rows, weight, ratio, turn, order_ref, lesser_ref, advanced_ref, sent_ref, *refs):
+    out_ref = refs[-1]
     lanes = 4 * bands
     groups = bands // 4
-    padded = order_ref.shape[1] // bands
-    depth = groups * padded
+    depth = groups * WINDOW
     taken = steps * bands
-    ordered = None
-    for turn, ref in enumerate(arrived_refs):
-        sigma = jnp.concatenate([ref[c * lanes : (c + 1) * lanes, :] for c in range(steps // 4)], axis=1)
-        term = jnp.dot(
-            sigma,
-            order_ref[turn * taken : (turn + 1) * taken, :],
-            preferred_element_type=F32,
-        )
-        ordered = term if ordered is None else ordered + term
+    fast = (lax.axis_index("hist") + ratio - turn) % ratio
+    sigma = jnp.concatenate([sent_ref[c * lanes : (c + 1) * lanes, :] for c in range(steps // 4)], axis=1)
+    ordered = jnp.dot(
+        sigma,
+        order_ref[turn * taken : (turn + 1) * taken, :],
+        preferred_element_type=F32,
+    )
     lefts = []
     for which in range(2):
         real = ordered[2 * which * bands : (2 * which + 1) * bands]
         imag = ordered[(2 * which + 1) * bands : (2 * which + 2) * bands]
-        for pair in ((real, imag), (-imag, real)):
-            lefts.append(
-                jnp.concatenate(
-                    [part[:, k * depth : (k + 1) * depth] for k in range(4) for part in pair],
-                    axis=0,
-                ).astype(BF16)
-            )
-    hist_start, row_start = (lax.axis_index("hist") * steps, lax.axis_index("row") * rows)
-    earlier = row_start + lax.broadcasted_iota(jnp.int32, (rows, groups * lanes), 0)
-    filler = jnp.zeros((padded - rows, lanes), F32)
-
-    def right(which, part, step):
+        both = []
+        for k in range(4):
+            at = slice(k * depth, (k + 1) * depth)
+            both.append(jnp.concatenate([real[:, at], -imag[:, at]], axis=1))
+            both.append(jnp.concatenate([imag[:, at], real[:, at]], axis=1))
+        lefts.append(jnp.concatenate(both, axis=0).astype(BF16))
+    starts = [f * steps // 8 * 8 for f in range(ratio)]
+    start = fast * steps // 8 * 8
+    earlier = lax.axis_index("row") * rows + start
+    earlier = earlier + lax.broadcasted_iota(jnp.int32, (WINDOW, groups * lanes), 0)
+    hist_start = lax.axis_index("hist") * steps
+
+    def right(which, step):
         ref = (lesser_ref, advanced_ref)[which]
-        whole = ref[part, step].astype(F32)
-        if which == 1:
-            whole = jnp.where(earlier <= hist_start + step, whole, 0.0)
         pieces = []
-        for g in range(groups):
-            pieces.append(whole[:, g * lanes : (g + 1) * lanes])
-            if padded > rows:
-                pieces.append(filler)
+        for part in range(2):
+            whole = ref[part, step].astype(F32)
+            window = whole[:WINDOW]
+            for f in range(1, ratio):
+                window = jnp.where(fast == f, whole[starts[f] : starts[f] + WINDOW], window)
+            if which == 1:
+                window = jnp.where(earlier <= hist_start + step, window, 0.0)
+            pieces += [window[:, g * lanes : (g + 1) * lanes] for g in range(groups)]
         return jnp.concatenate(pieces, axis=0).astype(BF16)
 
     block = lane_block((2 * bands, lanes), bands)
+    sums = []
     for chunk in range(steps // 4):
         gathered = None
         for pair in range(2):
             first = chunk * 4 + pair * 2
             total = None
             for which in range(2):
-                for part in range(2):
-                    rights = jnp.concatenate(
-                        [right(which, part, first), right(which, part, first + 1)], axis=1
-                    )
-                    term = jnp.dot(
-                        lefts[2 * which + part], rights, preferred_element_type=F32
-                    )
-                    total = term if total is None else total + term
+                rights = jnp.concatenate([right(which, first), right(which, first + 1)], axis=1)
+                term = jnp.dot(lefts[which], rights, preferred_element_type=F32)
+                total = term if total is None else total + term
             for k in range(2):
                 own = total[:, k * lanes : (k + 1) * lanes]
                 picked = own[: 2 * bands]
@@ -276,15 +271,21 @@
                 gathered = (
                     picked if gathered is None else jnp.where(block == 2 * pair + k, picked, gathered)
                 )
-        out_ref[: 2 * bands, chunk * lanes : (chunk + 1) * lanes] = weight * gathered
-    above_log = jnp.zeros((1, bands), F32)
-    above_phase = jnp.zeros((1, bands), F32)
-    for turn, ref in enumerate(arrived_refs):
-        fast = (lax.axis_index("hist") + ratio - turn) % ratio
-        later = jnp.where(lax.axis_index("row") * ratio + fast > lax.axis_index("hist"), 1.0, 0.0)
-        extra = ref[taken:, :bands].astype(F32)
-        above_log = above_log + later * (extra[0:1] + extra[1:2] + extra[2:3])
-        above_phase = above_phase + later * (extra[3:4] + extra[4:5] + extra[5:6])
+        sums.append(weight * gathered)
+        if len(refs) > 1:
+            sums[-1] = sums[-1] + refs[0][: 2 * bands, chunk * lanes : (chunk + 1) * lanes]
+    later = jnp.where(lax.axis_index("row") * ratio + fast > lax.axis_index("hist"), 1.0, 0.0)
+    extra = sent_ref[taken:, :bands].astype(F32)
+    above_log = later * (extra[0:1] + extra[1:2] + extra[2:3])
+    above_phase = later * (extra[3:4] + extra[4:5] + extra[5:6])
+    if len(refs) > 1:
+        above_log = above_log + refs[0][2 * bands : 2 * bands + 1, :bands]
+        above_phase = above_phase + refs[0][2 * bands + 1 : 2 * bands + 2, :bands]
+    if turn == 0:
+        pack_sum(out_ref, bands, sums, (above_log, above_phase))
+        return
+    for chunk, part in enumerate(sums):
+        out_ref[: 2 * bands, chunk * lanes : (chunk + 1) * lanes] = part
     at = lax.broadcasted_iota(jnp.int32, (8, bands), 0)
     out_ref[2 * bands :, :] = jnp.zeros((8, steps * bands), F32)
     out_ref[2 * bands :, :bands] = jnp.where(at == 0, above_log, jnp.where(at == 1, above_phase, 0.0))
@@ -304,16 +305,24 @@
     return extra
 
 
+def pack_sum(out_ref, bands, chunks, above):
+    last = len(chunks) * 2 * bands
+    for k, part in enumerate(chunks):
+        out_ref[2 * bands * k : 2 * bands * (k + 1), :] = part.astype(BF16)
+    out_ref[last:, :] = jnp.zeros((EXTRA, 4 * bands), BF16)
+    out_ref[last:, :bands] = pieces_of(above).astype(BF16)
+
+
+def unpack_sum(own_ref, other_ref, bands):
+    last = own_ref.shape[0] - EXTRA
+    total = own_ref[...].astype(F32) + other_ref[...].astype(F32)
+    chunks = [total[2 * bands * k : 2 * bands * (k + 1)] for k in range(last // (2 * bands))]
+    extra = total[last:, :bands]
+    return chunks, (extra[0:1] + extra[1:2] + extra[2:3], extra[3:4] + extra[4:5] + extra[5:6])
+
+
 def narrow_kernel(bands, own_ref, other_ref, out_ref):
-    total = own_ref[...] + other_ref[...]
-    lanes = 4 * bands
-    last = total.shape[1] // lanes * 2 * bands
-    for k in range(total.shape[1] // lanes):
-        part = total[: 2 * bands, k * lanes : (k + 1) * lanes]
-        out_ref[2 * bands * k : 2 * bands * (k + 1), :] = part.astype(BF16)
-    out_ref[last:, :] = jnp.zeros((EXTRA, lanes), BF16)
-    above = total[2 * bands :, :bands]
-    out_ref[last:, :bands] = pieces_of((above[0:1], above[1:2])).astype(BF16)
+    pack_sum(out_ref, bands, *unpack_sum(own_ref, other_ref, bands))
 
 
 def step_kernel(
@@ -322,10 +331,7 @@
 ):
     lanes = 4 * bands
     groups = bands // 4
-    last = steps // 4 * 2 * bands
-    extra = own_ref[last:, :bands].astype(F32) + other_ref[last:, :bands].astype(F32)
-    above_log = extra[0:1] + extra[1:2] + extra[2:3]
-    above_phase = extra[3:4] + extra[4:5] + extra[5:6]
+    chunks, (above_log, above_phase) = unpack_sum(own_ref, other_ref, bands)
     at = lax.broadcasted_iota(jnp.int32, (steps, bands), 0)
     rates = jnp.log(damping_ref[...])
     phases = phases_ref[...]
@@ -344,8 +350,6 @@
     factor = lax.dot_general(
         both, spreading, (((0,), (0,)), ((), ())), precision=HIGHEST, preferred_element_type=F32
     )
-    collision = own_ref[:last, :].astype(F32) + other_ref[:last, :].astype(F32)
-    chunks = [collision[2 * bands * k : 2 * bands * (k + 1)] for k in range(steps // 4)]
     row = packed_ref[...] + jnp.concatenate(chunks, axis=1)
     row_real, row_imag = (row[:bands], row[bands:])
     factor_real, factor_imag = (factor[:bands], factor[bands:])
@@ -390,7 +394,6 @@
     ratio = hist_count // row_count
     all_steps = steps * hist_count
     weight = float(all_steps * bands) ** (-0.5)
-    padded = -(-rows // 16) * 16
     taken = steps * bands
     sds = jax.ShapeDtypeStruct
 
@@ -402,7 +405,7 @@
     vmem = pltpu.VMEM
     (order,) = call(
         functools.partial(order_kernel, bands, steps, ratio),
-        [sds((ratio * taken, bands * padded), BF16)],
+        [sds((ratio * taken, bands * WINDOW), BF16)],
         [],
         10**10,
         10**7,
@@ -441,36 +444,37 @@
         return out
 
     got = crossed(give, "hist", 1)
-    order, got = lax.optimization_barrier((order, got))
-    (partial_row,) = call(
-        functools.partial(row_kernel, bands, steps, rows, weight, ratio),
-        [sds((2 * bands + 8, taken), F32)],
-        [],
-        10**6,
-        10**6,
-        [vmem] * (3 + ratio),
-        order,
-        lesser_hist.transpose(0, 2, 1, 3),
-        advanced_hist.transpose(0, 2, 1, 3),
-        *arrived,
-    )
-    other = crossed(partial_row, "row", 1)
-    bit = 2
+    summed = sds((steps // 4 * 2 * bands + EXTRA, lanes), BF16)
+    partial_row = []
+    for turn in reversed(range(ratio)):
+        partial_row = call(
+            functools.partial(row_kernel, bands, steps, rows, weight, ratio, turn),
+            [summed if turn == 0 else sds((2 * bands + 8, taken), F32)],
+            [],
+            10**6 if turn == 0 else 10**6,
+            10**6,
+            [vmem] * (4 + len(partial_row)),
+            order,
+            lesser_hist.transpose(0, 2, 1, 3),
+            advanced_hist.transpose(0, 2, 1, 3),
+            arrived[turn],
+            *partial_row,
+        )
+    partial_row = partial_row[0]
+    bit = 1
     while 2 * bit < row_count:
-        partial_row = add(partial_row, other, F32)
-        other = crossed(partial_row, "row", bit)
+        (partial_row,) = call(
+            functools.partial(narrow_kernel, bands),
+            [summed],
+            [],
+            10**6,
+            10**6,
+            [vmem] * 2,
+            partial_row,
+            crossed(partial_row, "row", bit),
+        )
         bit *= 2
-    (narrow,) = call(
-        functools.partial(narrow_kernel, bands),
-        [sds((steps // 4 * 2 * bands + EXTRA, lanes), BF16)],
-        [],
-        10**6,
-        10**6,
-        [vmem] * 2,
-        partial_row,
-        other,
-    )
-    other = crossed(narrow, "row", bit)
+    other = crossed(partial_row, "row", bit)
     column = add(column, got, BF16)
     got = crossed(column, "hist", hist_count // 2)
     stepped, squares = call(
@@ -483,7 +487,7 @@
         damping,
         phases,
         packed,
-        narrow,
+        partial_row,
         other,
     )
     ahead = [hist_count >> k for k in range(1, hist_count.bit_length() - 1)]

time: 34.9 us -> 34.3 us (0.983)
  waiting for transfers between devices: 16.6 us -> 10.9 us
  starting transfers between devices: 11.9 us -> 16.5 us
    ppermute x9, waiting for transfers between devices: 16.6 us -> 9.26 us  [crossed(): return lax.ppermute(x, axis, [(k, k ^ bit) for k in range(size)])]
    ppermute x9, starting transfers between devices: 8.01 us -> 12.6 us  [crossed(): return lax.ppermute(x, axis, [(k, k ^ bit) for k in range(size)])]
    ppermute x2, waiting for transfers between devices: 0.01 us -> 1.61 us  [swap_places(): return lax.ppermute(x, ('hist', 'row'), pairs)]
    pallas_call x12 -> x13, Pallas kernels: 4.83 us -> 5.17 us  [call(): pl.pallas_call(kernel, out_shape=shapes, in_specs=[pl.BlockSpec(memory_sp...]
  transfers between devices with their start and end apart: 11 -> 11, of which waited for: 8 -> 9; matrix products, arithmetic and copies ran while one was open for 0% -> 0% of each run, Pallas kernels for 4% -> 10%
where the time goes in v2:
time: 34.3 us; the launch traced here: 34 us
  starting transfers between devices  16.5 us (48%)
  waiting for transfers between devices  10.9 us (32%)
  Pallas kernels  5.17 us (15%)
  between operations  0.75 us (2%)
  local copies, waits for them, and re-layouts  0.71 us (2%)
    ppermute x9, starting transfers between devices, crossed(): return lax.ppermute(x, axis, [(k, k ^ bit) for k in range(size)])  12.6 us
    ppermute x9, waiting for transfers between devices, crossed(): return lax.ppermute(x, axis, [(k, k ^ bit) for k in range(size)])  9.26 us
    pallas_call x13, Pallas kernels, call(): pl.pallas_call(kernel, out_shape=shapes, in_specs=[pl.BlockSpec(memory_sp...  5.17 us
    ppermute x2, starting transfers between devices, swap_places(): return lax.ppermute(x, ('hist', 'row'), pairs)  3.9 us
    ppermute x2, waiting for transfers between devices, swap_places(): return lax.ppermute(x, ('hist', 'row'), pairs)  1.61 us
    unnamed x16, local copies, waits for them, and re-layouts  0.71 us
  transfers between devices with their start and end apart: 11, of which 9 were waited for; matrix products, arithmetic and copies ran while one was open for 0% of the time, Pallas kernels for 10%

profile of v2, /device:TPU:0, one launch (start us, length us, event | category | flops | bytes accessed | tf_op | source)
XLA Modules:
  0.0 34.0 jit_solution(2288885937041265831)
XLA Ops:
  1.6 0.8 %shard_map.96 = (bf16[400,128]{1,0:T(8,128)(2,1)S(1)}, f32[64,384]{1,0:T(8,128)S(1)}) custom-call(bf16[768,512]{1,0:T(8,128)(2,1)S(1)} %shard_map.95.order_ref, f32[192,128]{1,0:T(8,128)S(1)} %bitcast.22, f32[192,128]{1,0:T(8,128)S(1)} %bitcast.23, f32[32,32]{1,0:T(8,128)S(1)} %copy-done.4, f32[12,32]{1,0:T(8,128)S(1)} %copy-done.5, f32[12,32]{1,0:T(8,128)S(1)} %copy-done.6), custom_call_target="tpu_custom_call" | custom-call | flops 100000000 | bytes 1000000 | tf_op jit(solution)/shard_map/pallas_call | solution.py:374
  2.4 3.0 %collective-permute-start.1 = (bf16[400,128]{1,0:T(8,128)(2,1)S(1)}, bf16[400,128]{1,0:T(8,128)(2,1)S(1)}, u32[]{:S(2)}, u32[]{:S(2)}) collective-permute-start(bf16[400,128]{1,0:T(8,128)(2,1)S(1)} %get-tuple-element.13.send_ref), channel_id=1, source_target_pairs={{0,4},{1,20},{2,12},{3,28},{4,0},{5,16},{6,8},{7,24},{8,5},{9,21},... | collective-permute-start | bytes 307208 | tf_op jit(solution)/shard_map/ppermute | solution.py:30
  5.4 0.9 %collective-permute-start = (bf16[400,128]{1,0:T(8,128)(2,1)S(1)}, bf16[400,128]{1,0:T(8,128)(2,1)S(1)}, u32[]{:S(2)}, u32[]{:S(2)}) collective-permute-start(bf16[400,128]{1,0:T(8,128)(2,1)S(1)} %get-tuple-element.13.send_ref), channel_id=1, source_target_pairs={{0,8},{1,24},{2,0},{3,16},{4,12},{5,28},{6,4},{7,20},{8,9},{9,25},... | collective-permute-start | bytes 307208 | tf_op jit(solution)/shard_map/ppermute | solution.py:30
  6.3 0.7 %shard_map.103 = (f32[192,128]{1,0:T(8,128)S(1)}, f32[192,128]{1,0:T(8,128)S(1)}) custom-call(bf16[2,12,24,1024]{3,2,1,0:T(8,128)(2,1)S(1)} %bitcast.24, bf16[400,128]{1,0:T(8,128)(2,1)S(1)} %get-tuple-element.13.send_ref), custom_call_target="tpu_custom_call" | custom-call | flops 1000000000 | bytes 4000000 | tf_op jit(solution)/shard_map/pallas_call | solution.py:374
  7.1 0.8 %collective-permute-start.6 = (f32[192,128]{1,0:T(8,128)S(1)}, f32[192,128]{1,0:T(8,128)S(1)}, u32[]{:S(2)}, u32[]{:S(2)}) collective-permute-start(f32[192,128]{1,0:T(8,128)S(1)} %get-tuple-element.17), channel_id=1, source_target_pairs={{0,4},{4,0},{8,12},{12,8},{16,20},{20,16},{24,28},{28,24},{1,5},{5... | collective-permute-start | bytes 294920 | tf_op jit(solution)/shard_map/ppermute | solution.py:35
  7.9 0.8 %collective-permute-done.1.sent_ref = bf16[400,128]{1,0:T(8,128)(2,1)S(1)} collective-permute-done((bf16[400,128]{1,0:T(8,128)(2,1)S(1)}, bf16[400,128]{1,0:T(8,128)(2,1)S(1)}, u32[]{:S(2)}, u32[]{:S(2)}) %collective-permute-start.1) | collective-permute-done | bytes 102432 | tf_op jit(solution)/shard_map/ppermute | solution.py:30
  8.7 1.0 %shard_map.97.refs_0_ = f32[72,384]{1,0:T(8,128)S(1)} custom-call(bf16[768,512]{1,0:T(8,128)(2,1)S(1)} %shard_map.95.order_ref, bf16[2,12,24,1024]{3,2,1,0:T(8,128)(2,1)S(1)} %bitcast.18, bf16[2,12,24,1024]{3,2,1,0:T(8,128)(2,1)S(1)} %bitcast.20, bf16[400,128]{1,0:T(8,128)(2,1)S(1)} %collective-permute-done.1.sent_ref), custom_call_target="tpu_custom_call" | custom-call | flops 1000000 | bytes 1000000 | tf_op jit(solution)/shard_map/pallas_call | solution.py:374
  9.7 0.8 %collective-permute-done.sent_ref = bf16[400,128]{1,0:T(8,128)(2,1)S(1)} collective-permute-done((bf16[400,128]{1,0:T(8,128)(2,1)S(1)}, bf16[400,128]{1,0:T(8,128)(2,1)S(1)}, u32[]{:S(2)}, u32[]{:S(2)}) %collective-permute-start) | collective-permute-done | bytes 102432 | tf_op jit(solution)/shard_map/ppermute | solution.py:30
  10.5 1.0 %shard_map.98.own_ref = bf16[208,128]{1,0:T(8,128)(2,1)S(1)} custom-call(bf16[768,512]{1,0:T(8,128)(2,1)S(1)} %shard_map.95.order_ref, bf16[2,12,24,1024]{3,2,1,0:T(8,128)(2,1)S(1)} %bitcast.19, bf16[2,12,24,1024]{3,2,1,0:T(8,128)(2,1)S(1)} %bitcast.21, bf16[400,128]{1,0:T(8,128)(2,1)S(1)} %collective-permute-done.sent_ref, f32[72,384]{1,0:T(8,128)S(1)} %shard_map.97.refs_0_), custom_call_target="tpu_custom_call" | custom-call | flops 1000000 | bytes 1000000 | tf_op jit(solution)/shard_map/pallas_call | solution.py:374
  11.5 2.1 %collective-permute-start.2 = (bf16[208,128]{1,0:T(8,128)(2,1)S(1)}, bf16[208,128]{1,0:T(8,128)(2,1)S(1)}, u32[]{:S(2)}, u32[]{:S(2)}) collective-permute-start(bf16[208,128]{1,0:T(8,128)(2,1)S(1)} %shard_map.98.own_ref), channel_id=1, source_target_pairs={{0,1},{1,0},{2,3},{3,2},{4,5},{5,4},{6,7},{7,6},{8,9},{9,8},{10,11... | collective-permute-start | bytes 159752 | tf_op jit(solution)/shard_map/ppermute | solution.py:35
  13.6 0.9 %collective-permute-done.2.other_ref = bf16[208,128]{1,0:T(8,128)(2,1)S(1)} collective-permute-done((bf16[208,128]{1,0:T(8,128)(2,1)S(1)}, bf16[208,128]{1,0:T(8,128)(2,1)S(1)}, u32[]{:S(2)}, u32[]{:S(2)}) %collective-permute-start.2) | collective-permute-done | bytes 53280 | tf_op jit(solution)/shard_map/ppermute | solution.py:35
  14.5 4.2 %collective-permute-start.3 = (bf16[208,128]{1,0:T(8,128)(2,1)S(1)}, bf16[208,128]{1,0:T(8,128)(2,1)S(1)}, u32[]{:S(2)}, u32[]{:S(2)}) collective-permute-start(bf16[208,128]{1,0:T(8,128)(2,1)S(1)} %shard_map.99.own_ref), channel_id=1, source_target_pairs={{0,2},{1,3},{2,0},{3,1},{4,6},{5,7},{6,4},{7,5},{8,10},{9,11},{10,... | collective-permute-start | bytes 159752 | tf_op jit(solution)/shard_map/ppermute | solution.py:35
  18.8 1.4 %collective-permute-start.7 = (bf16[192,128]{1,0:T(8,128)(2,1)S(1)}, bf16[192,128]{1,0:T(8,128)(2,1)S(1)}, u32[]{:S(2)}, u32[]{:S(2)}) collective-permute-start(bf16[192,128]{1,0:T(8,128)(2,1)S(1)} %shard_map.104.own_ref), channel_id=1, source_target_pairs={{0,16},{4,20},{8,24},{12,28},{16,0},{20,4},{24,8},{28,12},{1,17},{... | collective-permute-start | bytes 147464 | tf_op jit(solution)/shard_map/ppermute | solution.py:35
  20.2 0.7 %collective-permute-done.3.other_ref = bf16[208,128]{1,0:T(8,128)(2,1)S(1)} collective-permute-done((bf16[208,128]{1,0:T(8,128)(2,1)S(1)}, bf16[208,128]{1,0:T(8,128)(2,1)S(1)}, u32[]{:S(2)}, u32[]{:S(2)}) %collective-permute-start.3) | collective-permute-done | bytes 53280 | tf_op jit(solution)/shard_map/ppermute | solution.py:35
  21.5 0.9 %collective-permute-start.4 = (f32[8,128]{1,0:T(8,128)S(1)}, f32[8,128]{1,0:T(8,128)S(1)}, u32[]{:S(2)}, u32[]{:S(2)}) collective-permute-start(f32[8,128]{1,0:T(8,128)S(1)} %get-tuple-element.15.own_ref), channel_id=1, source_target_pairs={{0,4},{4,0},{8,12},{12,8},{16,20},{20,16},{24,28},{28,24},{1,5},{5... | collective-permute-start | bytes 12296 | tf_op jit(solution)/shard_map/ppermute | solution.py:35
  22.4 1.7 %collective-permute-done.7.other_ref = bf16[192,128]{1,0:T(8,128)(2,1)S(1)} collective-permute-done((bf16[192,128]{1,0:T(8,128)(2,1)S(1)}, bf16[192,128]{1,0:T(8,128)(2,1)S(1)}, u32[]{:S(2)}, u32[]{:S(2)}) %collective-permute-start.7) | collective-permute-done | bytes 49184 | tf_op jit(solution)/shard_map/ppermute | solution.py:35
  24.2 0.9 %collective-permute-done.4.other_ref = f32[8,128]{1,0:T(8,128)S(1)} collective-permute-done((f32[8,128]{1,0:T(8,128)S(1)}, f32[8,128]{1,0:T(8,128)S(1)}, u32[]{:S(2)}, u32[]{:S(2)}) %collective-permute-start.4) | collective-permute-done | bytes 4128 | tf_op jit(solution)/shard_map/ppermute | solution.py:35
  25.2 1.3 %collective-permute-start.5 = (f32[8,128]{1,0:T(8,128)S(1)}, f32[8,128]{1,0:T(8,128)S(1)}, u32[]{:S(2)}, u32[]{:S(2)}) collective-permute-start(f32[8,128]{1,0:T(8,128)S(1)} %shard_map.101.own_ref), channel_id=1, source_target_pairs={{0,16},{4,20},{8,24},{12,28},{16,0},{20,4},{24,8},{28,12},{1,17},{... | collective-permute-start | bytes 12296 | tf_op jit(solution)/shard_map/ppermute | solution.py:35
  26.5 1.7 %collective-permute-done.8.other_ref = bf16[192,128]{1,0:T(8,128)(2,1)S(1)} collective-permute-done((bf16[192,128]{1,0:T(8,128)(2,1)S(1)}, bf16[192,128]{1,0:T(8,128)(2,1)S(1)}, u32[]{:S(2)}, u32[]{:S(2)}) %collective-permute-start.8) | collective-permute-done | bytes 49184 | tf_op jit(solution)/shard_map/ppermute | solution.py:35
  28.3 0.7 %collective-permute-start.9 = (f32[192,128]{1,0:T(8,128)S(1)}, f32[192,128]{1,0:T(8,128)S(1)}, u32[]{:S(2)}, u32[]{:S(2)}) collective-permute-start(f32[192,128]{1,0:T(8,128)S(1)} %shard_map.106.sum_ref), channel_id=1, source_target_pairs={{0,4},{4,0},{8,12},{12,8},{16,20},{20,16},{24,28},{28,24},{1,5},{5... | collective-permute-start | bytes 294920 | tf_op jit(solution)/shard_map/ppermute | solution.py:35
  29.0 0.7 %collective-permute-done.5.other_ref = f32[8,128]{1,0:T(8,128)S(1)} collective-permute-done((f32[8,128]{1,0:T(8,128)S(1)}, f32[8,128]{1,0:T(8,128)S(1)}, u32[]{:S(2)}, u32[]{:S(2)}) %collective-permute-start.5) | collective-permute-done | bytes 4128 | tf_op jit(solution)/shard_map/ppermute | solution.py:35
  29.7 1.0 %collective-permute-start.10 = (f32[8,128]{1,0:T(8,128)S(1)}, f32[8,128]{1,0:T(8,128)S(1)}, u32[]{:S(2)}, u32[]{:S(2)}) collective-permute-start(f32[8,128]{1,0:T(8,128)S(1)} %shard_map.102.own_ref), channel_id=1, source_target_pairs={{0,8},{4,12},{8,0},{12,4},{16,24},{20,28},{24,16},{28,20},{1,9},{5... | collective-permute-start | bytes 12296 | tf_op jit(solution)/shard_map/ppermute | solution.py:35
  30.7 2.6 %collective-permute-done.10.other_ref = f32[8,128]{1,0:T(8,128)S(1)} collective-permute-done((f32[8,128]{1,0:T(8,128)S(1)}, f32[8,128]{1,0:T(8,128)S(1)}, u32[]{:S(2)}, u32[]{:S(2)}) %collective-permute-start.10) | collective-permute-done | bytes 4128 | tf_op jit(solution)/shard_map/ppermute | solution.py:35
  33.3 0.7 %shard_map.107 = (f32[192,128]{1,0:T(8,128)}, f32[2,24,1024]{2,1,0:T(8,128)}) custom-call(f32[192,128]{1,0:T(8,128)S(1)} %get-tuple-element.14.stepped_ref, f32[8,128]{1,0:T(8,128)S(1)} %shard_map.102.own_ref, f32[8,128]{1,0:T(8,128)S(1)} %collective-permute-done.10.other_ref, f32[192,128]{1,0:T(8,128)S(1)} %shard_map.106.sum_ref, ...), custom_call_target="tpu_custom_call" | custom-call | flops 1000000 | bytes 1000000 | tf_op jit(solution)/shard_map/pallas_call | solution.py:374
  (27 shorter events, 1.7 us)
Async XLA Ops:
  0.6 0.7 %copy-start.6 = (f32[12,32]{1,0:T(8,128)S(1)}, f32[12,32]{1,0:T(8,128)}, u32[]{:S(2)}) copy-start(f32[12,32]{1,0:T(8,128)} %phases_ref.3) | copy-start | bytes 4612
  0.6 0.7 %copy-start.5 = (f32[12,32]{1,0:T(8,128)S(1)}, f32[12,32]{1,0:T(8,128)}, u32[]{:S(2)}) copy-start(f32[12,32]{1,0:T(8,128)} %damping_ref.3) | copy-start | bytes 4612
  0.7 0.7 %copy-start.4 = (f32[32,32]{1,0:T(8,128)S(1)}, f32[32,32]{1,0:T(8,128)}, u32[]{:S(2)}) copy-start(f32[32,32]{1,0:T(8,128)} %coupling_ref.1) | copy-start | bytes 12292
  0.7 0.9 %copy-start.3 = (f32[2,12,1024]{2,0,1:T(2,128)S(1)}, f32[2,12,1024]{2,0,1:T(2,128)}, u32[]{:S(2)}) copy-start(f32[2,12,1024]{2,0,1:T(2,128)} %param.9) | copy-start | bytes 294916
  0.7 0.9 %copy-start.2 = (f32[2,12,1024]{2,0,1:T(2,128)S(1)}, f32[2,12,1024]{2,0,1:T(2,128)}, u32[]{:S(2)}) copy-start(f32[2,12,1024]{2,0,1:T(2,128)} %param.8) | copy-start | bytes 294916
  0.7 5.6 %copy-start.7 = (bf16[2,24,12,1024]{3,1,2,0:T(8,128)(2,1)S(1)}, bf16[2,24,12,1024]{3,1,2,0:T(8,128)(2,1)}, u32[]{:S(2)}) copy-start(bf16[2,24,12,1024]{3,1,2,0:T(8,128)(2,1)} %param.15) | copy-start | bytes 3538948
  2.4 6.3 %collective-permute-start.1 = (bf16[400,128]{1,0:T(8,128)(2,1)S(1)}, bf16[400,128]{1,0:T(8,128)(2,1)S(1)}, u32[]{:S(2)}, u32[]{:S(2)}) collective-permute-start(bf16[400,128]{1,0:T(8,128)(2,1)S(1)} %get-tuple-element.13.send_ref), channel_id=1, source_target_pairs={{0,4},{1,20},{2,12},{3,28},{4,0},{5,16},{6,8},{7,24},{8,5},{9,21},... | collective-permute-start | bytes 307208 | tf_op jit(solution)/shard_map/ppermute | solution.py:30
  5.4 5.1 %collective-permute-start = (bf16[400,128]{1,0:T(8,128)(2,1)S(1)}, bf16[400,128]{1,0:T(8,128)(2,1)S(1)}, u32[]{:S(2)}, u32[]{:S(2)}) collective-permute-start(bf16[400,128]{1,0:T(8,128)(2,1)S(1)} %get-tuple-element.13.send_ref), channel_id=1, source_target_pairs={{0,8},{1,24},{2,0},{3,16},{4,12},{5,28},{6,4},{7,20},{8,9},{9,25},... | collective-permute-start | bytes 307208 | tf_op jit(solution)/shard_map/ppermute | solution.py:30
  6.3 2.4 %copy-start = (bf16[2,24,12,1024]{3,1,2,0:T(8,128)(2,1)S(1)}, bf16[2,24,12,1024]{3,1,2,0:T(8,128)(2,1)}, u32[]{:S(2)}) copy-start(bf16[2,24,12,1024]{3,1,2,0:T(8,128)(2,1)} %param.13) | copy-start | bytes 3538948
  6.3 2.4 %copy-start.1 = (bf16[2,24,12,1024]{3,1,2,0:T(8,128)(2,1)S(1)}, bf16[2,24,12,1024]{3,1,2,0:T(8,128)(2,1)}, u32[]{:S(2)}) copy-start(bf16[2,24,12,1024]{3,1,2,0:T(8,128)(2,1)} %param.14) | copy-start | bytes 3538948
  7.1 11.7 %collective-permute-start.6 = (f32[192,128]{1,0:T(8,128)S(1)}, f32[192,128]{1,0:T(8,128)S(1)}, u32[]{:S(2)}, u32[]{:S(2)}) collective-permute-start(f32[192,128]{1,0:T(8,128)S(1)} %get-tuple-element.17), channel_id=1, source_target_pairs={{0,4},{4,0},{8,12},{12,8},{16,20},{20,16},{24,28},{28,24},{1,5},{5... | collective-permute-start | bytes 294920 | tf_op jit(solution)/shard_map/ppermute | solution.py:35
  11.5 3.0 %collective-permute-start.2 = (bf16[208,128]{1,0:T(8,128)(2,1)S(1)}, bf16[208,128]{1,0:T(8,128)(2,1)S(1)}, u32[]{:S(2)}, u32[]{:S(2)}) collective-permute-start(bf16[208,128]{1,0:T(8,128)(2,1)S(1)} %shard_map.98.own_ref), channel_id=1, source_target_pairs={{0,1},{1,0},{2,3},{3,2},{4,5},{5,4},{6,7},{7,6},{8,9},{9,8},{10,11... | collective-permute-start | bytes 159752 | tf_op jit(solution)/shard_map/ppermute | solution.py:35
  14.5 6.4 %collective-permute-start.3 = (bf16[208,128]{1,0:T(8,128)(2,1)S(1)}, bf16[208,128]{1,0:T(8,128)(2,1)S(1)}, u32[]{:S(2)}, u32[]{:S(2)}) collective-permute-start(bf16[208,128]{1,0:T(8,128)(2,1)S(1)} %shard_map.99.own_ref), channel_id=1, source_target_pairs={{0,2},{1,3},{2,0},{3,1},{4,6},{5,7},{6,4},{7,5},{8,10},{9,11},{10,... | collective-permute-start | bytes 159752 | tf_op jit(solution)/shard_map/ppermute | solution.py:35
  18.8 5.3 %collective-permute-start.7 = (bf16[192,128]{1,0:T(8,128)(2,1)S(1)}, bf16[192,128]{1,0:T(8,128)(2,1)S(1)}, u32[]{:S(2)}, u32[]{:S(2)}) collective-permute-start(bf16[192,128]{1,0:T(8,128)(2,1)S(1)} %shard_map.104.own_ref), channel_id=1, source_target_pairs={{0,16},{4,20},{8,24},{12,28},{16,0},{20,4},{24,8},{28,12},{1,17},{... | collective-permute-start | bytes 147464 | tf_op jit(solution)/shard_map/ppermute | solution.py:35
  21.5 3.7 %collective-permute-start.4 = (f32[8,128]{1,0:T(8,128)S(1)}, f32[8,128]{1,0:T(8,128)S(1)}, u32[]{:S(2)}, u32[]{:S(2)}) collective-permute-start(f32[8,128]{1,0:T(8,128)S(1)} %get-tuple-element.15.own_ref), channel_id=1, source_target_pairs={{0,4},{4,0},{8,12},{12,8},{16,20},{20,16},{24,28},{28,24},{1,5},{5... | collective-permute-start | bytes 12296 | tf_op jit(solution)/shard_map/ppermute | solution.py:35
  24.1 4.2 %collective-permute-start.8 = (bf16[192,128]{1,0:T(8,128)(2,1)S(1)}, bf16[192,128]{1,0:T(8,128)(2,1)S(1)}, u32[]{:S(2)}, u32[]{:S(2)}) collective-permute-start(bf16[192,128]{1,0:T(8,128)(2,1)S(1)} %shard_map.105.own_ref), channel_id=1, source_target_pairs={{0,8},{4,12},{8,0},{12,4},{16,24},{20,28},{24,16},{28,20},{1,9},{5... | collective-permute-start | bytes 147464 | tf_op jit(solution)/shard_map/ppermute | solution.py:35
  25.2 4.5 %collective-permute-start.5 = (f32[8,128]{1,0:T(8,128)S(1)}, f32[8,128]{1,0:T(8,128)S(1)}, u32[]{:S(2)}, u32[]{:S(2)}) collective-permute-start(f32[8,128]{1,0:T(8,128)S(1)} %shard_map.101.own_ref), channel_id=1, source_target_pairs={{0,16},{4,20},{8,24},{12,28},{16,0},{20,4},{24,8},{28,12},{1,17},{... | collective-permute-start | bytes 12296 | tf_op jit(solution)/shard_map/ppermute | solution.py:35
  28.3 5.0 %collective-permute-start.9 = (f32[192,128]{1,0:T(8,128)S(1)}, f32[192,128]{1,0:T(8,128)S(1)}, u32[]{:S(2)}, u32[]{:S(2)}) collective-permute-start(f32[192,128]{1,0:T(8,128)S(1)} %shard_map.106.sum_ref), channel_id=1, source_target_pairs={{0,4},{4,0},{8,12},{12,8},{16,20},{20,16},{24,28},{28,24},{1,5},{5... | collective-permute-start | bytes 294920 | tf_op jit(solution)/shard_map/ppermute | solution.py:35
  29.7 3.6 %collective-permute-start.10 = (f32[8,128]{1,0:T(8,128)S(1)}, f32[8,128]{1,0:T(8,128)S(1)}, u32[]{:S(2)}, u32[]{:S(2)}) collective-permute-start(f32[8,128]{1,0:T(8,128)S(1)} %shard_map.102.own_ref), channel_id=1, source_target_pairs={{0,8},{4,12},{8,0},{12,4},{16,24},{20,28},{24,16},{28,20},{1,9},{5... | collective-permute-start | bytes 12296 | tf_op jit(solution)/shard_map/ppermute | solution.py:35

commit v3 on v2

--- a/solution.py
+++ b/solution.py
@@ -54,6 +54,16 @@
                 new[a | bit] = jnp.where(keep, pltpu.roll(low, 4 * width - shift, 1), high)
         parts = new
     return parts
+
+
+def split_dot(left, right, dims):
+    highs = [x.astype(BF16) for x in (left, right)]
+    lows = [(x - high.astype(F32)).astype(BF16) for x, high in zip((left, right), highs)]
+
+    def product(a, b):
+        return lax.dot_general(a, b, dims, preferred_element_type=F32)
+
+    return product(highs[0], highs[1]) + (product(highs[0], lows[1]) + product(lows[0], highs[1]))
 
 
 def energy_kernel(bands, steps, order_ref, less_ref, great_ref, coupling_ref, damping_ref, phases_ref, send_ref, packed_ref, work):
@@ -82,21 +92,13 @@
     tall = jnp.concatenate([wide] * 4, axis=0)
     at_row = lax.broadcasted_iota(jnp.int32, tall.shape, 0) // bands
     blocked = jnp.where(at_row == lane_block(tall.shape, bands), tall, 0.0)
-    half = lax.dot_general(
-        polar, blocked, (((1,), (1,)), ((), ())), precision=HIGHEST, preferred_element_type=F32
-    )
+    half = split_dot(polar, blocked, (((1,), (1,)), ((), ())))
     rows = chunks * bands
     both = jnp.concatenate([half[:rows], half[rows:]], axis=1)
     screens = []
     for chunk in range(chunks):
-        screens.append(
-            jnp.dot(
-                coupling,
-                both[chunk * bands : (chunk + 1) * bands],
-                precision=HIGHEST,
-                preferred_element_type=F32,
-            )
-        )
+        part = both[chunk * bands : (chunk + 1) * bands]
+        screens.append(split_dot(coupling, part, (((1,), (0,)), ((), ()))))
     screen = jnp.concatenate(screens, axis=0)
     lanes = 4 * bands
     screen_real, screen_imag = (screen[:, :lanes], screen[:, lanes:])
@@ -179,6 +181,7 @@
             )
             total = term if total is None else total + term
     low = lax.axis_index("hist") % 2 == 0
+    give_ref[groups * rows :, :] = jnp.zeros((give_ref.shape[0] - groups * rows, lanes), BF16)
     for g in range(groups // 2):
         for part in range(2):
             halves = [
@@ -187,11 +190,11 @@
             ]
             to = slice((2 * g + part) * rows, (2 * g + part + 1) * rows)
             keep_ref[to, :] = jnp.where(low, halves[0], halves[1])
-            give_ref[to, :] = jnp.where(low, halves[1], halves[0])
+            give_ref[to, :] = jnp.where(low, halves[1], halves[0]).astype(BF16)
 
 
 def add_kernel(own_ref, other_ref, out_ref):
-    total = own_ref[...].astype(F32) + other_ref[...].astype(F32)
+    total = own_ref[...].astype(F32) + other_ref[: own_ref.shape[0], :].astype(F32)
     out_ref[...] = total.astype(out_ref.dtype)
 
 
@@ -208,29 +211,10 @@
             column_ref[part, :, g * lanes : (g + 1) * lanes] = column[at : at + rows]
 
 
-def row_kernel(bands, steps, rows, weight, ratio, turn, order_ref, lesser_ref, advanced_ref, sent_ref, *refs):
-    out_ref = refs[-1]
-    lanes = 4 * bands
-    groups = bands // 4
-    depth = groups * WINDOW
-    taken = steps * bands
+def right_operand(bands, steps, rows, ratio, turn, lesser_ref, advanced_ref):
+    lanes = 4 * bands
+    groups = bands // 4
     fast = (lax.axis_index("hist") + ratio - turn) % ratio
-    sigma = jnp.concatenate([sent_ref[c * lanes : (c + 1) * lanes, :] for c in range(steps // 4)], axis=1)
-    ordered = jnp.dot(
-        sigma,
-        order_ref[turn * taken : (turn + 1) * taken, :],
-        preferred_element_type=F32,
-    )
-    lefts = []
-    for which in range(2):
-        real = ordered[2 * which * bands : (2 * which + 1) * bands]
-        imag = ordered[(2 * which + 1) * bands : (2 * which + 2) * bands]
-        both = []
-        for k in range(4):
-            at = slice(k * depth, (k + 1) * depth)
-            both.append(jnp.concatenate([real[:, at], -imag[:, at]], axis=1))
-            both.append(jnp.concatenate([imag[:, at], real[:, at]], axis=1))
-        lefts.append(jnp.concatenate(both, axis=0).astype(BF16))
     starts = [f * steps // 8 * 8 for f in range(ratio)]
     start = fast * steps // 8 * 8
     earlier = lax.axis_index("row") * rows + start
@@ -250,6 +234,46 @@
             pieces += [window[:, g * lanes : (g + 1) * lanes] for g in range(groups)]
         return jnp.concatenate(pieces, axis=0).astype(BF16)
 
+    return right
+
+
+def right_kernel(bands, steps, rows, ratio, turn, lesser_ref, advanced_ref, out_ref):
+    right = right_operand(bands, steps, rows, ratio, turn, lesser_ref, advanced_ref)
+    depth = 2 * bands // 4 * WINDOW
+    for which in range(2):
+        for pair in range(steps // 2):
+            at = (which * steps // 2 + pair) * depth
+            both = [right(which, 2 * pair), right(which, 2 * pair + 1)]
+            out_ref[at : at + depth, :] = jnp.concatenate(both, axis=1)
+
+
+def row_kernel(bands, steps, rows, weight, ratio, turn, order_ref, lesser_ref, advanced_ref, sent_ref, *refs):
+    out_ref = refs[-1]
+    lanes = 4 * bands
+    groups = bands // 4
+    depth = groups * WINDOW
+    taken = steps * bands
+    fast = (lax.axis_index("hist") + ratio - turn) % ratio
+    sigma = jnp.concatenate([sent_ref[c * lanes : (c + 1) * lanes, :] for c in range(steps // 4)], axis=1)
+    ordered = jnp.dot(
+        sigma,
+        order_ref[turn * taken : (turn + 1) * taken, :],
+        preferred_element_type=F32,
+    )
+    lefts = []
+    for which in range(2):
+        real = ordered[2 * which * bands : (2 * which + 1) * bands]
+        imag = ordered[(2 * which + 1) * bands : (2 * which + 2) * bands]
+        both = []
+        for k in range(4):
+            at = slice(k * depth, (k + 1) * depth)
+            both.append(jnp.concatenate([real[:, at], -imag[:, at]], axis=1))
+            both.append(jnp.concatenate([imag[:, at], real[:, at]], axis=1))
+        lefts.append(jnp.concatenate(both, axis=0).astype(BF16))
+    built = len(lesser_ref.shape) == 2
+    if not built:
+        right = right_operand(bands, steps, rows, ratio, turn, lesser_ref, advanced_ref)
+
     block = lane_block((2 * bands, lanes), bands)
     sums = []
     for chunk in range(steps // 4):
@@ -258,7 +282,11 @@
             first = chunk * 4 + pair * 2
             total = None
             for which in range(2):
-                rights = jnp.concatenate([right(which, first), right(which, first + 1)], axis=1)
+                if built:
+                    at = (which * steps // 2 + first // 2) * 2 * depth
+                    rights = lesser_ref[at : at + 2 * depth, :]
+                else:
+                    rights = jnp.concatenate([right(which, first), right(which, first + 1)], axis=1)
                 term = jnp.dot(lefts[which], rights, preferred_element_type=F32)
                 total = term if total is None else total + term
             for k in range(2):
@@ -327,7 +355,7 @@
 
 def step_kernel(
     bands, steps, damping_ref, phases_ref, packed_ref, own_ref, other_ref,
-    out_ref, square_ref, work
+    out_ref, square_ref
 ):
     lanes = 4 * bands
     groups = bands // 4
@@ -359,9 +387,18 @@
     )
     squares = jnp.sum(stepped[0] * stepped[0] + stepped[1] * stepped[1], keepdims=True)
     square_ref[...] = jnp.broadcast_to(squares, square_ref.shape)
+    out_ref[:bands, :] = stepped[0]
+    out_ref[bands:, :] = stepped[1]
+
+
+def relayout_kernel(bands, steps, stepped_ref, out_ref, work):
+    lanes = 4 * bands
+    groups = bands // 4
     for part in range(2):
         for chunk in range(steps // 4):
-            work[part, chunk] = stepped[part][:, chunk * lanes : (chunk + 1) * lanes]
+            work[part, chunk] = stepped_ref[
+                part * bands : (part + 1) * bands, chunk * lanes : (chunk + 1) * lanes
+            ]
     for part in range(2):
         for chunk in range(steps // 4):
             blocks = [work[part, chunk, pl.ds(k, groups, stride=4), :] for k in range(4)]
@@ -428,7 +465,7 @@
     arrived = [swap_places(send, turn) for turn in range(ratio)]
     column, give = call(
         functools.partial(column_kernel, bands, steps, rows, weight),
-        [sds((groups * rows, lanes), F32)] * 2,
+        [sds((groups * rows, lanes), F32), sds((groups * rows + 2 * EXTRA, lanes), BF16)],
         [],
         10**9,
         4 * 10**6,
@@ -445,20 +482,29 @@
 
     got = crossed(give, "hist", 1)
     summed = sds((steps // 4 * 2 * bands + EXTRA, lanes), BF16)
+    histories = [lesser_hist.transpose(0, 2, 1, 3), advanced_hist.transpose(0, 2, 1, 3)]
+    (rights,) = call(
+        functools.partial(right_kernel, bands, steps, rows, ratio, 0),
+        [sds((steps * 2 * bands // 4 * WINDOW, 2 * lanes), BF16)],
+        [],
+        10**4,
+        10**4,
+        [vmem] * 2,
+        *histories,
+    )
+    order_first, rights = lax.optimization_barrier((order, rights))
     partial_row = []
     for turn in reversed(range(ratio)):
+        operands = [order_first] + histories if turn else [order, rights, rights]
+        operands += [arrived[turn], *partial_row]
         partial_row = call(
             functools.partial(row_kernel, bands, steps, rows, weight, ratio, turn),
             [summed if turn == 0 else sds((2 * bands + 8, taken), F32)],
             [],
-            10**6 if turn == 0 else 10**6,
-            10**6,
-            [vmem] * (4 + len(partial_row)),
-            order,
-            lesser_hist.transpose(0, 2, 1, 3),
-            advanced_hist.transpose(0, 2, 1, 3),
-            arrived[turn],
-            *partial_row,
+            10**4,
+            10**4,
+            [vmem] * len(operands),
+            *operands,
         )
     partial_row = partial_row[0]
     bit = 1
@@ -467,8 +513,8 @@
             functools.partial(narrow_kernel, bands),
             [summed],
             [],
-            10**6,
-            10**6,
+            10**4,
+            10**4,
             [vmem] * 2,
             partial_row,
             crossed(partial_row, "row", bit),
@@ -479,8 +525,8 @@
     got = crossed(column, "hist", hist_count // 2)
     stepped, squares = call(
         functools.partial(step_kernel, bands, steps),
-        [sds((steps * groups * 2, lanes), F32), sds((8, lanes), F32)],
-        [vmem((2, steps // 4, bands, lanes), F32)],
+        [sds((2 * bands, taken), F32), sds((8, lanes), F32)],
+        [],
         10**10,
         10**6,
         [vmem] * 5,
@@ -490,12 +536,21 @@
         partial_row,
         other,
     )
+    (stepped,) = call(
+        functools.partial(relayout_kernel, bands, steps),
+        [sds((steps * groups * 2, lanes), F32)],
+        [vmem((2, steps // 4, bands, lanes), F32)],
+        10**10,
+        10**6,
+        [vmem],
+        stepped,
+    )
     ahead = [hist_count >> k for k in range(1, hist_count.bit_length() - 1)]
     beside = ahead[1:] + [1, None]
     for bit, each in zip([1] + ahead, beside):
         other = crossed(squares, "hist", bit)
         if each:
-            column = add(column, got, BF16 if each == 2 else F32)
+            column = add(column, got, F32)
             got = crossed(column, "hist", each)
             squares = add(squares, other, F32)
     got, other = lax.optimization_barrier((got, other))

time: 34.3 us -> 34.1 us (level)
  starting transfers between devices: 16.5 us -> 15.8 us
  waiting for transfers between devices: 10.9 us -> 11.3 us
    ppermute x9, waiting for transfers between devices: 9.26 us -> 10.1 us  [crossed(): return lax.ppermute(x, axis, [(k, k ^ bit) for k in range(size)])]
    ppermute x9, starting transfers between devices: 12.6 us -> 11.9 us  [crossed(): return lax.ppermute(x, axis, [(k, k ^ bit) for k in range(size)])]
    ppermute x2, waiting for transfers between devices: 1.61 us -> 1.22 us  [swap_places(): return lax.ppermute(x, ('hist', 'row'), pairs)]
    pallas_call x13 -> x15, Pallas kernels: 5.17 us -> 5.4 us  [call(): pl.pallas_call(kernel, out_shape=shapes, in_specs=[pl.BlockSpec(memory_sp...]
  transfers between devices with their start and end apart: 11 -> 11, of which waited for: 9 -> 10; matrix products, arithmetic and copies ran while one was open for 0% -> 0% of each run, Pallas kernels for 10% -> 11%
where the time goes in v3:
time: 34.1 us; the launch traced here: 34 us
  starting transfers between devices  15.8 us (46%)
  waiting for transfers between devices  11.3 us (33%)
  Pallas kernels  5.4 us (16%)
  between operations  0.76 us (2%)
  local copies, waits for them, and re-layouts  0.72 us (2%)
    ppermute x9, starting transfers between devices, crossed(): return lax.ppermute(x, axis, [(k, k ^ bit) for k in range(size)])  11.9 us
    ppermute x9, waiting for transfers between devices, crossed(): return lax.ppermute(x, axis, [(k, k ^ bit) for k in range(size)])  10.1 us
    pallas_call x15, Pallas kernels, call(): pl.pallas_call(kernel, out_shape=shapes, in_specs=[pl.BlockSpec(memory_sp...  5.4 us
    ppermute x2, starting transfers between devices, swap_places(): return lax.ppermute(x, ('hist', 'row'), pairs)  3.9 us
    ppermute x2, waiting for transfers between devices, swap_places(): return lax.ppermute(x, ('hist', 'row'), pairs)  1.22 us
    unnamed x16, local copies, waits for them, and re-layouts  0.72 us
  transfers between devices with their start and end apart: 11, of which 10 were waited for; matrix products, arithmetic and copies ran while one was open for 0% of the time, Pallas kernels for 11%

profile of v3, /device:TPU:0, one launch (start us, length us, event | category | flops | bytes accessed | tf_op | source)
XLA Modules:
  0.0 34.0 jit_solution(17003887101320599899)
XLA Ops:
  0.9 0.6 %copy-done.2 = f32[2,12,1024]{2,0,1:T(2,128)S(1)} copy-done((f32[2,12,1024]{2,0,1:T(2,128)S(1)}, f32[2,12,1024]{2,0,1:T(2,128)}, u32[]{:S(2)}) %copy-start.2) | copy-done | bytes 98328
  1.6 0.6 %shard_map.96 = (bf16[400,128]{1,0:T(8,128)(2,1)S(1)}, f32[64,384]{1,0:T(8,128)S(1)}) custom-call(bf16[768,512]{1,0:T(8,128)(2,1)S(1)} %shard_map.95.order_ref, f32[192,128]{1,0:T(8,128)S(1)} %bitcast.22, f32[192,128]{1,0:T(8,128)S(1)} %bitcast.23, f32[32,32]{1,0:T(8,128)S(1)} %copy-done.4, f32[12,32]{1,0:T(8,128)S(1)} %copy-done.5, f32[12,32]{1,0:T(8,128)S(1)} %copy-done.6), custom_call_target="tpu_custom_call" | custom-call | flops 100000000 | bytes 1000000 | tf_op jit(solution)/shard_map/pallas_call | solution.py:411
  2.2 3.0 %collective-permute-start.1 = (bf16[400,128]{1,0:T(8,128)(2,1)S(1)}, bf16[400,128]{1,0:T(8,128)(2,1)S(1)}, u32[]{:S(2)}, u32[]{:S(2)}) collective-permute-start(bf16[400,128]{1,0:T(8,128)(2,1)S(1)} %get-tuple-element.16.send_ref), channel_id=1, source_target_pairs={{0,4},{1,20},{2,12},{3,28},{4,0},{5,16},{6,8},{7,24},{8,5},{9,21},... | collective-permute-start | bytes 307208 | tf_op jit(solution)/shard_map/ppermute | solution.py:30
  5.2 0.9 %collective-permute-start = (bf16[400,128]{1,0:T(8,128)(2,1)S(1)}, bf16[400,128]{1,0:T(8,128)(2,1)S(1)}, u32[]{:S(2)}, u32[]{:S(2)}) collective-permute-start(bf16[400,128]{1,0:T(8,128)(2,1)S(1)} %get-tuple-element.16.send_ref), channel_id=1, source_target_pairs={{0,8},{1,24},{2,0},{3,16},{4,12},{5,28},{6,4},{7,20},{8,9},{9,25},... | collective-permute-start | bytes 307208 | tf_op jit(solution)/shard_map/ppermute | solution.py:30
  6.1 0.7 %shard_map.105 = (f32[192,128]{1,0:T(8,128)S(1)}, bf16[224,128]{1,0:T(8,128)(2,1)S(1)}) custom-call(bf16[2,12,24,1024]{3,2,1,0:T(8,128)(2,1)S(1)} %bitcast.24, bf16[400,128]{1,0:T(8,128)(2,1)S(1)} %get-tuple-element.16.send_ref), custom_call_target="tpu_custom_call" | custom-call | flops 1000000000 | bytes 4000000 | tf_op jit(solution)/shard_map/pallas_call | solution.py:411
  6.9 0.8 %collective-permute-start.6 = (bf16[224,128]{1,0:T(8,128)(2,1)S(1)}, bf16[224,128]{1,0:T(8,128)(2,1)S(1)}, u32[]{:S(2)}, u32[]{:S(2)}) collective-permute-start(bf16[224,128]{1,0:T(8,128)(2,1)S(1)} %get-tuple-element.21), channel_id=1, source_target_pairs={{0,4},{4,0},{8,12},{12,8},{16,20},{20,16},{24,28},{28,24},{1,5},{5... | collective-permute-start | bytes 172040 | tf_op jit(solution)/shard_map/ppermute | solution.py:35
  8.5 1.0 %shard_map.98.refs_0_ = f32[72,384]{1,0:T(8,128)S(1)} custom-call(bf16[768,512]{1,0:T(8,128)(2,1)S(1)} %shard_map.95.order_ref, bf16[2,12,24,1024]{3,2,1,0:T(8,128)(2,1)S(1)} %bitcast.19, bf16[2,12,24,1024]{3,2,1,0:T(8,128)(2,1)S(1)} %bitcast.21, bf16[400,128]{1,0:T(8,128)(2,1)S(1)} %collective-permute-done.1.sent_ref), custom_call_target="tpu_custom_call" | custom-call | flops 10000 | bytes 10000 | tf_op jit(solution)/shard_map/pallas_call | solution.py:411
  9.5 0.9 %collective-permute-done.sent_ref = bf16[400,128]{1,0:T(8,128)(2,1)S(1)} collective-permute-done((bf16[400,128]{1,0:T(8,128)(2,1)S(1)}, bf16[400,128]{1,0:T(8,128)(2,1)S(1)}, u32[]{:S(2)}, u32[]{:S(2)}) %collective-permute-start) | collective-permute-done | bytes 102432 | tf_op jit(solution)/shard_map/ppermute | solution.py:30
  10.3 0.9 %shard_map.99.own_ref = bf16[208,128]{1,0:T(8,128)(2,1)S(1)} custom-call(bf16[768,512]{1,0:T(8,128)(2,1)S(1)} %shard_map.95.order_ref, bf16[3072,256]{1,0:T(8,128)(2,1)S(1)} %shard_map.97.lesser_ref.advanced_ref, bf16[3072,256]{1,0:T(8,128)(2,1)S(1)} %shard_map.97.lesser_ref.advanced_ref, bf16[400,128]{1,0:T(8,128)(2,1)S(1)} %collective-permute-done.sent_ref, ...), custom_call_target="tpu_custom_call" | custom-call | flops 10000 | bytes 10000 | tf_op jit(solution)/shard_map/pallas_call | solution.py:411
  11.3 2.1 %collective-permute-start.2 = (bf16[208,128]{1,0:T(8,128)(2,1)S(1)}, bf16[208,128]{1,0:T(8,128)(2,1)S(1)}, u32[]{:S(2)}, u32[]{:S(2)}) collective-permute-start(bf16[208,128]{1,0:T(8,128)(2,1)S(1)} %shard_map.99.own_ref), channel_id=1, source_target_pairs={{0,1},{1,0},{2,3},{3,2},{4,5},{5,4},{6,7},{7,6},{8,9},{9,8},{10,11... | collective-permute-start | bytes 159752 | tf_op jit(solution)/shard_map/ppermute | solution.py:35
  13.3 0.9 %collective-permute-done.2.other_ref = bf16[208,128]{1,0:T(8,128)(2,1)S(1)} collective-permute-done((bf16[208,128]{1,0:T(8,128)(2,1)S(1)}, bf16[208,128]{1,0:T(8,128)(2,1)S(1)}, u32[]{:S(2)}, u32[]{:S(2)}) %collective-permute-start.2) | collective-permute-done | bytes 53280 | tf_op jit(solution)/shard_map/ppermute | solution.py:35
  14.3 4.2 %collective-permute-start.3 = (bf16[208,128]{1,0:T(8,128)(2,1)S(1)}, bf16[208,128]{1,0:T(8,128)(2,1)S(1)}, u32[]{:S(2)}, u32[]{:S(2)}) collective-permute-start(bf16[208,128]{1,0:T(8,128)(2,1)S(1)} %shard_map.100.own_ref), channel_id=1, source_target_pairs={{0,2},{1,3},{2,0},{3,1},{4,6},{5,7},{6,4},{7,5},{8,10},{9,11},{10,... | collective-permute-start | bytes 159752 | tf_op jit(solution)/shard_map/ppermute | solution.py:35
  18.5 1.0 %collective-permute-start.7 = (bf16[192,128]{1,0:T(8,128)(2,1)S(1)}, bf16[192,128]{1,0:T(8,128)(2,1)S(1)}, u32[]{:S(2)}, u32[]{:S(2)}) collective-permute-start(bf16[192,128]{1,0:T(8,128)(2,1)S(1)} %shard_map.106.own_ref), channel_id=1, source_target_pairs={{0,16},{4,20},{8,24},{12,28},{16,0},{20,4},{24,8},{28,12},{1,17},{... | collective-permute-start | bytes 147464 | tf_op jit(solution)/shard_map/ppermute | solution.py:35
  19.5 1.1 %collective-permute-done.3.other_ref = bf16[208,128]{1,0:T(8,128)(2,1)S(1)} collective-permute-done((bf16[208,128]{1,0:T(8,128)(2,1)S(1)}, bf16[208,128]{1,0:T(8,128)(2,1)S(1)}, u32[]{:S(2)}, u32[]{:S(2)}) %collective-permute-start.3) | collective-permute-done | bytes 53280 | tf_op jit(solution)/shard_map/ppermute | solution.py:35
  20.6 0.5 %shard_map.101 = (f32[64,384]{1,0:T(8,128)S(1)}, f32[8,128]{1,0:T(8,128)S(1)}) custom-call(f32[12,32]{1,0:T(8,128)S(1)} %copy-done.5, f32[12,32]{1,0:T(8,128)S(1)} %copy-done.6, f32[64,384]{1,0:T(8,128)S(1)} %get-tuple-element.14.packed_ref, bf16[208,128]{1,0:T(8,128)(2,1)S(1)} %shard_map.100.own_ref, bf16[208,128]{1,0:T(8,128)(2,1)S(1)} %collective-permute-done.3.other_ref), custom_call_target="tpu_custom_call" | custom-call | flops 10000000000 | bytes 1000000 | tf_op jit(solution)/shard_map/pallas_call | solution.py:411
  21.2 0.6 %collective-permute-start.4 = (f32[8,128]{1,0:T(8,128)S(1)}, f32[8,128]{1,0:T(8,128)S(1)}, u32[]{:S(2)}, u32[]{:S(2)}) collective-permute-start(f32[8,128]{1,0:T(8,128)S(1)} %get-tuple-element.19.own_ref), channel_id=1, source_target_pairs={{0,4},{4,0},{8,12},{12,8},{16,20},{20,16},{24,28},{28,24},{1,5},{5... | collective-permute-start | bytes 12296 | tf_op jit(solution)/shard_map/ppermute | solution.py:35
  21.8 2.1 %collective-permute-done.7.other_ref = bf16[192,128]{1,0:T(8,128)(2,1)S(1)} collective-permute-done((bf16[192,128]{1,0:T(8,128)(2,1)S(1)}, bf16[192,128]{1,0:T(8,128)(2,1)S(1)}, u32[]{:S(2)}, u32[]{:S(2)}) %collective-permute-start.7) | collective-permute-done | bytes 49184 | tf_op jit(solution)/shard_map/ppermute | solution.py:35
  24.0 0.9 %collective-permute-done.4.other_ref = f32[8,128]{1,0:T(8,128)S(1)} collective-permute-done((f32[8,128]{1,0:T(8,128)S(1)}, f32[8,128]{1,0:T(8,128)S(1)}, u32[]{:S(2)}, u32[]{:S(2)}) %collective-permute-start.4) | collective-permute-done | bytes 4128 | tf_op jit(solution)/shard_map/ppermute | solution.py:35
  24.9 1.3 %collective-permute-start.5 = (f32[8,128]{1,0:T(8,128)S(1)}, f32[8,128]{1,0:T(8,128)S(1)}, u32[]{:S(2)}, u32[]{:S(2)}) collective-permute-start(f32[8,128]{1,0:T(8,128)S(1)} %shard_map.103.own_ref), channel_id=1, source_target_pairs={{0,16},{4,20},{8,24},{12,28},{16,0},{20,4},{24,8},{28,12},{1,17},{... | collective-permute-start | bytes 12296 | tf_op jit(solution)/shard_map/ppermute | solution.py:35
  26.2 2.4 %collective-permute-done.8.other_ref = f32[192,128]{1,0:T(8,128)S(1)} collective-permute-done((f32[192,128]{1,0:T(8,128)S(1)}, f32[192,128]{1,0:T(8,128)S(1)}, u32[]{:S(2)}, u32[]{:S(2)}) %collective-permute-start.8) | collective-permute-done | bytes 98336 | tf_op jit(solution)/shard_map/ppermute | solution.py:35
  28.6 0.7 %collective-permute-start.9 = (f32[192,128]{1,0:T(8,128)S(1)}, f32[192,128]{1,0:T(8,128)S(1)}, u32[]{:S(2)}, u32[]{:S(2)}) collective-permute-start(f32[192,128]{1,0:T(8,128)S(1)} %shard_map.108.sum_ref), channel_id=1, source_target_pairs={{0,4},{4,0},{8,12},{12,8},{16,20},{20,16},{24,28},{28,24},{1,5},{5... | collective-permute-start | bytes 294920 | tf_op jit(solution)/shard_map/ppermute | solution.py:35
  29.4 1.1 %collective-permute-start.10 = (f32[8,128]{1,0:T(8,128)S(1)}, f32[8,128]{1,0:T(8,128)S(1)}, u32[]{:S(2)}, u32[]{:S(2)}) collective-permute-start(f32[8,128]{1,0:T(8,128)S(1)} %shard_map.104.own_ref), channel_id=1, source_target_pairs={{0,8},{4,12},{8,0},{12,4},{16,24},{20,28},{24,16},{28,20},{1,9},{5... | collective-permute-start | bytes 12296 | tf_op jit(solution)/shard_map/ppermute | solution.py:35
  30.6 2.4 %collective-permute-done.10.other_ref = f32[8,128]{1,0:T(8,128)S(1)} collective-permute-done((f32[8,128]{1,0:T(8,128)S(1)}, f32[8,128]{1,0:T(8,128)S(1)}, u32[]{:S(2)}, u32[]{:S(2)}) %collective-permute-start.10) | collective-permute-done | bytes 4128 | tf_op jit(solution)/shard_map/ppermute | solution.py:35
  33.2 0.7 %shard_map.109 = (f32[192,128]{1,0:T(8,128)}, f32[2,24,1024]{2,1,0:T(8,128)}) custom-call(f32[192,128]{1,0:T(8,128)S(1)} %shard_map.102.stepped_ref, f32[8,128]{1,0:T(8,128)S(1)} %shard_map.104.own_ref, f32[8,128]{1,0:T(8,128)S(1)} %collective-permute-done.10.other_ref, f32[192,128]{1,0:T(8,128)S(1)} %shard_map.108.sum_ref, ...), custom_call_target="tpu_custom_call" | custom-call | flops 1000000 | bytes 1000000 | tf_op jit(solution)/shard_map/pallas_call | solution.py:411
  (29 shorter events, 1.9 us)
Async XLA Ops:
  0.6 0.9 %copy-start.2 = (f32[2,12,1024]{2,0,1:T(2,128)S(1)}, f32[2,12,1024]{2,0,1:T(2,128)}, u32[]{:S(2)}) copy-start(f32[2,12,1024]{2,0,1:T(2,128)} %param.8) | copy-start | bytes 294916
  0.6 0.9 %copy-start.3 = (f32[2,12,1024]{2,0,1:T(2,128)S(1)}, f32[2,12,1024]{2,0,1:T(2,128)}, u32[]{:S(2)}) copy-start(f32[2,12,1024]{2,0,1:T(2,128)} %param.9) | copy-start | bytes 294916
  0.7 0.9 %copy-start.4 = (f32[32,32]{1,0:T(8,128)S(1)}, f32[32,32]{1,0:T(8,128)}, u32[]{:S(2)}) copy-start(f32[32,32]{1,0:T(8,128)} %coupling_ref.1) | copy-start | bytes 12292
  0.7 0.9 %copy-start.5 = (f32[12,32]{1,0:T(8,128)S(1)}, f32[12,32]{1,0:T(8,128)}, u32[]{:S(2)}) copy-start(f32[12,32]{1,0:T(8,128)} %damping_ref.3) | copy-start | bytes 4612
  0.7 0.9 %copy-start.6 = (f32[12,32]{1,0:T(8,128)S(1)}, f32[12,32]{1,0:T(8,128)}, u32[]{:S(2)}) copy-start(f32[12,32]{1,0:T(8,128)} %phases_ref.3) | copy-start | bytes 4612
  0.7 5.4 %copy-start.7 = (bf16[2,24,12,1024]{3,1,2,0:T(8,128)(2,1)S(1)}, bf16[2,24,12,1024]{3,1,2,0:T(8,128)(2,1)}, u32[]{:S(2)}) copy-start(bf16[2,24,12,1024]{3,1,2,0:T(8,128)(2,1)} %param.15) | copy-start | bytes 3538948
  2.2 6.3 %collective-permute-start.1 = (bf16[400,128]{1,0:T(8,128)(2,1)S(1)}, bf16[400,128]{1,0:T(8,128)(2,1)S(1)}, u32[]{:S(2)}, u32[]{:S(2)}) collective-permute-start(bf16[400,128]{1,0:T(8,128)(2,1)S(1)} %get-tuple-element.16.send_ref), channel_id=1, source_target_pairs={{0,4},{1,20},{2,12},{3,28},{4,0},{5,16},{6,8},{7,24},{8,5},{9,21},... | collective-permute-start | bytes 307208 | tf_op jit(solution)/shard_map/ppermute | solution.py:30
  5.2 5.1 %collective-permute-start = (bf16[400,128]{1,0:T(8,128)(2,1)S(1)}, bf16[400,128]{1,0:T(8,128)(2,1)S(1)}, u32[]{:S(2)}, u32[]{:S(2)}) collective-permute-start(bf16[400,128]{1,0:T(8,128)(2,1)S(1)} %get-tuple-element.16.send_ref), channel_id=1, source_target_pairs={{0,8},{1,24},{2,0},{3,16},{4,12},{5,28},{6,4},{7,20},{8,9},{9,25},... | collective-permute-start | bytes 307208 | tf_op jit(solution)/shard_map/ppermute | solution.py:30
  6.1 1.6 %copy-start = (bf16[2,24,12,1024]{3,1,2,0:T(8,128)(2,1)S(1)}, bf16[2,24,12,1024]{3,1,2,0:T(8,128)(2,1)}, u32[]{:S(2)}) copy-start(bf16[2,24,12,1024]{3,1,2,0:T(8,128)(2,1)} %param.13) | copy-start | bytes 3538948
  6.1 1.6 %copy-start.1 = (bf16[2,24,12,1024]{3,1,2,0:T(8,128)(2,1)S(1)}, bf16[2,24,12,1024]{3,1,2,0:T(8,128)(2,1)}, u32[]{:S(2)}) copy-start(bf16[2,24,12,1024]{3,1,2,0:T(8,128)(2,1)} %param.14) | copy-start | bytes 3538948
  6.9 11.6 %collective-permute-start.6 = (bf16[224,128]{1,0:T(8,128)(2,1)S(1)}, bf16[224,128]{1,0:T(8,128)(2,1)S(1)}, u32[]{:S(2)}, u32[]{:S(2)}) collective-permute-start(bf16[224,128]{1,0:T(8,128)(2,1)S(1)} %get-tuple-element.21), channel_id=1, source_target_pairs={{0,4},{4,0},{8,12},{12,8},{16,20},{20,16},{24,28},{28,24},{1,5},{5... | collective-permute-start | bytes 172040 | tf_op jit(solution)/shard_map/ppermute | solution.py:35
  11.3 3.0 %collective-permute-start.2 = (bf16[208,128]{1,0:T(8,128)(2,1)S(1)}, bf16[208,128]{1,0:T(8,128)(2,1)S(1)}, u32[]{:S(2)}, u32[]{:S(2)}) collective-permute-start(bf16[208,128]{1,0:T(8,128)(2,1)S(1)} %shard_map.99.own_ref), channel_id=1, source_target_pairs={{0,1},{1,0},{2,3},{3,2},{4,5},{5,4},{6,7},{7,6},{8,9},{9,8},{10,11... | collective-permute-start | bytes 159752 | tf_op jit(solution)/shard_map/ppermute | solution.py:35
  14.3 6.4 %collective-permute-start.3 = (bf16[208,128]{1,0:T(8,128)(2,1)S(1)}, bf16[208,128]{1,0:T(8,128)(2,1)S(1)}, u32[]{:S(2)}, u32[]{:S(2)}) collective-permute-start(bf16[208,128]{1,0:T(8,128)(2,1)S(1)} %shard_map.100.own_ref), channel_id=1, source_target_pairs={{0,2},{1,3},{2,0},{3,1},{4,6},{5,7},{6,4},{7,5},{8,10},{9,11},{10,... | collective-permute-start | bytes 159752 | tf_op jit(solution)/shard_map/ppermute | solution.py:35
  18.5 5.3 %collective-permute-start.7 = (bf16[192,128]{1,0:T(8,128)(2,1)S(1)}, bf16[192,128]{1,0:T(8,128)(2,1)S(1)}, u32[]{:S(2)}, u32[]{:S(2)}) collective-permute-start(bf16[192,128]{1,0:T(8,128)(2,1)S(1)} %shard_map.106.own_ref), channel_id=1, source_target_pairs={{0,16},{4,20},{8,24},{12,28},{16,0},{20,4},{24,8},{28,12},{1,17},{... | collective-permute-start | bytes 147464 | tf_op jit(solution)/shard_map/ppermute | solution.py:35
  21.2 3.7 %collective-permute-start.4 = (f32[8,128]{1,0:T(8,128)S(1)}, f32[8,128]{1,0:T(8,128)S(1)}, u32[]{:S(2)}, u32[]{:S(2)}) collective-permute-start(f32[8,128]{1,0:T(8,128)S(1)} %get-tuple-element.19.own_ref), channel_id=1, source_target_pairs={{0,4},{4,0},{8,12},{12,8},{16,20},{20,16},{24,28},{28,24},{1,5},{5... | collective-permute-start | bytes 12296 | tf_op jit(solution)/shard_map/ppermute | solution.py:35
  23.9 4.7 %collective-permute-start.8 = (f32[192,128]{1,0:T(8,128)S(1)}, f32[192,128]{1,0:T(8,128)S(1)}, u32[]{:S(2)}, u32[]{:S(2)}) collective-permute-start(f32[192,128]{1,0:T(8,128)S(1)} %shard_map.107.own_ref), channel_id=1, source_target_pairs={{0,8},{4,12},{8,0},{12,4},{16,24},{20,28},{24,16},{28,20},{1,9},{5... | collective-permute-start | bytes 294920 | tf_op jit(solution)/shard_map/ppermute | solution.py:35
  24.9 4.5 %collective-permute-start.5 = (f32[8,128]{1,0:T(8,128)S(1)}, f32[8,128]{1,0:T(8,128)S(1)}, u32[]{:S(2)}, u32[]{:S(2)}) collective-permute-start(f32[8,128]{1,0:T(8,128)S(1)} %shard_map.103.own_ref), channel_id=1, source_target_pairs={{0,16},{4,20},{8,24},{12,28},{16,0},{20,4},{24,8},{28,12},{1,17},{... | collective-permute-start | bytes 12296 | tf_op jit(solution)/shard_map/ppermute | solution.py:35
  28.6 4.7 %collective-permute-start.9 = (f32[192,128]{1,0:T(8,128)S(1)}, f32[192,128]{1,0:T(8,128)S(1)}, u32[]{:S(2)}, u32[]{:S(2)}) collective-permute-start(f32[192,128]{1,0:T(8,128)S(1)} %shard_map.108.sum_ref), channel_id=1, source_target_pairs={{0,4},{4,0},{8,12},{12,8},{16,20},{20,16},{24,28},{28,24},{1,5},{5... | collective-permute-start | bytes 294920 | tf_op jit(solution)/shard_map/ppermute | solution.py:35
  29.4 3.6 %collective-permute-start.10 = (f32[8,128]{1,0:T(8,128)S(1)}, f32[8,128]{1,0:T(8,128)S(1)}, u32[]{:S(2)}, u32[]{:S(2)}) collective-permute-start(f32[8,128]{1,0:T(8,128)S(1)} %shard_map.104.own_ref), channel_id=1, source_target_pairs={{0,8},{4,12},{8,0},{12,4},{16,24},{20,28},{24,16},{28,20},{1,9},{5... | collective-permute-start | bytes 12296 | tf_op jit(solution)/shard_map/ppermute | solution.py:35

commit v4 on v3

--- a/solution.py
+++ b/solution.py
@@ -24,7 +24,8 @@
         for fast in range(ratio):
             for row in range(row_count):
                 source = (slow * ratio + fast) * row_count + row
-                goal = row % cores * span + (row // cores + 1 + turn) % span
+                shift = turn + (1 if slow in (0, row_count - 1) else 0)
+                goal = row % cores * span + (row // cores + shift) % span
                 target = (goal * ratio + (fast + turn) % ratio) * row_count + slow
                 pairs.append((source, target))
     return lax.ppermute(x, ("hist", "row"), pairs)

time: 34.1 us -> 34.2 us (level)
  starting transfers between devices: 15.8 us -> 14.1 us
  waiting for transfers between devices: 11.3 us -> 13 us
    ppermute x9, starting transfers between devices: 11.9 us -> 10.1 us  [crossed(): return lax.ppermute(x, axis, [(k, k ^ bit) for k in range(size)])]
    ppermute x9, waiting for transfers between devices: 10.1 us -> 11.3 us  [crossed(): return lax.ppermute(x, axis, [(k, k ^ bit) for k in range(size)])]
    ppermute x2, waiting for transfers between devices: 1.22 us -> 1.7 us  [swap_places(): return lax.ppermute(x, ('hist', 'row'), pairs)]
  transfers between devices with their start and end apart: 11 -> 11, of which waited for: 10 -> 9; matrix products, arithmetic and copies ran while one was open for 0% -> 0% of each run, Pallas kernels for 11% -> 11%
where the time goes in v4:
time: 34.2 us; the launch traced here: 34.1 us
  starting transfers between devices  14.1 us (41%)
  waiting for transfers between devices  13 us (38%)
  Pallas kernels  5.4 us (16%)
  local copies, waits for them, and re-layouts  0.84 us (2%)
  between operations  0.77 us (2%)
    ppermute x9, waiting for transfers between devices, crossed(): return lax.ppermute(x, axis, [(k, k ^ bit) for k in range(size)])  11.3 us
    ppermute x9, starting transfers between devices, crossed(): return lax.ppermute(x, axis, [(k, k ^ bit) for k in range(size)])  10.1 us
    pallas_call x15, Pallas kernels, call(): pl.pallas_call(kernel, out_shape=shapes, in_specs=[pl.BlockSpec(memory_sp...  5.4 us
    ppermute x2, starting transfers between devices, swap_places(): return lax.ppermute(x, ('hist', 'row'), pairs)  4.01 us
    ppermute x2, waiting for transfers between devices, swap_places(): return lax.ppermute(x, ('hist', 'row'), pairs)  1.7 us
    unnamed x16, local copies, waits for them, and re-layouts  0.84 us
  transfers between devices with their start and end apart: 11, of which 9 were waited for; matrix products, arithmetic and copies ran while one was open for 0% of the time, Pallas kernels for 11%

profile of v4, /device:TPU:0, one launch (start us, length us, event | category | flops | bytes accessed | tf_op | source)
XLA Modules:
  0.0 34.1 jit_solution(13496254769056992683)
XLA Ops:
  0.9 0.6 %copy-done.2 = f32[2,12,1024]{2,0,1:T(2,128)S(1)} copy-done((f32[2,12,1024]{2,0,1:T(2,128)S(1)}, f32[2,12,1024]{2,0,1:T(2,128)}, u32[]{:S(2)}) %copy-start.2) | copy-done | bytes 98328
  1.6 0.6 %shard_map.96 = (bf16[400,128]{1,0:T(8,128)(2,1)S(1)}, f32[64,384]{1,0:T(8,128)S(1)}) custom-call(bf16[768,512]{1,0:T(8,128)(2,1)S(1)} %shard_map.95.order_ref, f32[192,128]{1,0:T(8,128)S(1)} %bitcast.22, f32[192,128]{1,0:T(8,128)S(1)} %bitcast.23, f32[32,32]{1,0:T(8,128)S(1)} %copy-done.4, f32[12,32]{1,0:T(8,128)S(1)} %copy-done.5, f32[12,32]{1,0:T(8,128)S(1)} %copy-done.6), custom_call_target="tpu_custom_call" | custom-call | flops 100000000 | bytes 1000000 | tf_op jit(solution)/shard_map/pallas_call | solution.py:412
  2.2 3.0 %collective-permute-start.1 = (bf16[400,128]{1,0:T(8,128)(2,1)S(1)}, bf16[400,128]{1,0:T(8,128)(2,1)S(1)}, u32[]{:S(2)}, u32[]{:S(2)}) collective-permute-start(bf16[400,128]{1,0:T(8,128)(2,1)S(1)} %get-tuple-element.16.send_ref), channel_id=1, source_target_pairs={{0,4},{1,20},{2,12},{3,28},{4,0},{5,16},{6,8},{7,24},{8,13},{9,29}... | collective-permute-start | bytes 307208 | tf_op jit(solution)/shard_map/ppermute | solution.py:31
  5.2 1.0 %collective-permute-start = (bf16[400,128]{1,0:T(8,128)(2,1)S(1)}, bf16[400,128]{1,0:T(8,128)(2,1)S(1)}, u32[]{:S(2)}, u32[]{:S(2)}) collective-permute-start(bf16[400,128]{1,0:T(8,128)(2,1)S(1)} %get-tuple-element.16.send_ref), channel_id=1, source_target_pairs={{0,8},{1,24},{2,0},{3,16},{4,12},{5,28},{6,4},{7,20},{8,1},{9,17},... | collective-permute-start | bytes 307208 | tf_op jit(solution)/shard_map/ppermute | solution.py:31
  6.2 0.7 %shard_map.105 = (f32[192,128]{1,0:T(8,128)S(1)}, bf16[224,128]{1,0:T(8,128)(2,1)S(1)}) custom-call(bf16[2,12,24,1024]{3,2,1,0:T(8,128)(2,1)S(1)} %bitcast.24, bf16[400,128]{1,0:T(8,128)(2,1)S(1)} %get-tuple-element.16.send_ref), custom_call_target="tpu_custom_call" | custom-call | flops 1000000000 | bytes 4000000 | tf_op jit(solution)/shard_map/pallas_call | solution.py:412
  7.0 0.7 %collective-permute-start.6 = (bf16[224,128]{1,0:T(8,128)(2,1)S(1)}, bf16[224,128]{1,0:T(8,128)(2,1)S(1)}, u32[]{:S(2)}, u32[]{:S(2)}) collective-permute-start(bf16[224,128]{1,0:T(8,128)(2,1)S(1)} %get-tuple-element.21), channel_id=1, source_target_pairs={{0,4},{4,0},{8,12},{12,8},{16,20},{20,16},{24,28},{28,24},{1,5},{5... | collective-permute-start | bytes 172040 | tf_op jit(solution)/shard_map/ppermute | solution.py:36
  7.9 0.4 %shard_map.97.lesser_ref.advanced_ref = bf16[3072,256]{1,0:T(8,128)(2,1)S(1)} custom-call(bf16[2,12,24,1024]{3,2,1,0:T(8,128)(2,1)S(1)} %bitcast.18, bf16[2,12,24,1024]{3,2,1,0:T(8,128)(2,1)S(1)} %bitcast.20), custom_call_target="tpu_custom_call" | custom-call | flops 10000 | bytes 10000 | tf_op jit(solution)/shard_map/pallas_call | solution.py:412
  8.2 1.0 %shard_map.98.refs_0_ = f32[72,384]{1,0:T(8,128)S(1)} custom-call(bf16[768,512]{1,0:T(8,128)(2,1)S(1)} %shard_map.95.order_ref, bf16[2,12,24,1024]{3,2,1,0:T(8,128)(2,1)S(1)} %bitcast.19, bf16[2,12,24,1024]{3,2,1,0:T(8,128)(2,1)S(1)} %bitcast.21, bf16[400,128]{1,0:T(8,128)(2,1)S(1)} %collective-permute-done.1.sent_ref), custom_call_target="tpu_custom_call" | custom-call | flops 10000 | bytes 10000 | tf_op jit(solution)/shard_map/pallas_call | solution.py:412
  9.2 1.7 %collective-permute-done.sent_ref = bf16[400,128]{1,0:T(8,128)(2,1)S(1)} collective-permute-done((bf16[400,128]{1,0:T(8,128)(2,1)S(1)}, bf16[400,128]{1,0:T(8,128)(2,1)S(1)}, u32[]{:S(2)}, u32[]{:S(2)}) %collective-permute-start) | collective-permute-done | bytes 102432 | tf_op jit(solution)/shard_map/ppermute | solution.py:31
  10.9 0.9 %shard_map.99.own_ref = bf16[208,128]{1,0:T(8,128)(2,1)S(1)} custom-call(bf16[768,512]{1,0:T(8,128)(2,1)S(1)} %shard_map.95.order_ref, bf16[3072,256]{1,0:T(8,128)(2,1)S(1)} %shard_map.97.lesser_ref.advanced_ref, bf16[3072,256]{1,0:T(8,128)(2,1)S(1)} %shard_map.97.lesser_ref.advanced_ref, bf16[400,128]{1,0:T(8,128)(2,1)S(1)} %collective-permute-done.sent_ref, ...), custom_call_target="tpu_custom_call" | custom-call | flops 10000 | bytes 10000 | tf_op jit(solution)/shard_map/pallas_call | solution.py:412
  11.8 1.7 %collective-permute-start.2 = (bf16[208,128]{1,0:T(8,128)(2,1)S(1)}, bf16[208,128]{1,0:T(8,128)(2,1)S(1)}, u32[]{:S(2)}, u32[]{:S(2)}) collective-permute-start(bf16[208,128]{1,0:T(8,128)(2,1)S(1)} %shard_map.99.own_ref), channel_id=1, source_target_pairs={{0,1},{1,0},{2,3},{3,2},{4,5},{5,4},{6,7},{7,6},{8,9},{9,8},{10,11... | collective-permute-start | bytes 159752 | tf_op jit(solution)/shard_map/ppermute | solution.py:36
  13.5 0.9 %collective-permute-done.2.other_ref = bf16[208,128]{1,0:T(8,128)(2,1)S(1)} collective-permute-done((bf16[208,128]{1,0:T(8,128)(2,1)S(1)}, bf16[208,128]{1,0:T(8,128)(2,1)S(1)}, u32[]{:S(2)}, u32[]{:S(2)}) %collective-permute-start.2) | collective-permute-done | bytes 53280 | tf_op jit(solution)/shard_map/ppermute | solution.py:36
  14.4 3.9 %collective-permute-start.3 = (bf16[208,128]{1,0:T(8,128)(2,1)S(1)}, bf16[208,128]{1,0:T(8,128)(2,1)S(1)}, u32[]{:S(2)}, u32[]{:S(2)}) collective-permute-start(bf16[208,128]{1,0:T(8,128)(2,1)S(1)} %shard_map.100.own_ref), channel_id=1, source_target_pairs={{0,2},{1,3},{2,0},{3,1},{4,6},{5,7},{6,4},{7,5},{8,10},{9,11},{10,... | collective-permute-start | bytes 159752 | tf_op jit(solution)/shard_map/ppermute | solution.py:36
  18.5 2.1 %collective-permute-done.3.other_ref = bf16[208,128]{1,0:T(8,128)(2,1)S(1)} collective-permute-done((bf16[208,128]{1,0:T(8,128)(2,1)S(1)}, bf16[208,128]{1,0:T(8,128)(2,1)S(1)}, u32[]{:S(2)}, u32[]{:S(2)}) %collective-permute-start.3) | collective-permute-done | bytes 53280 | tf_op jit(solution)/shard_map/ppermute | solution.py:36
  20.5 0.5 %shard_map.101 = (f32[64,384]{1,0:T(8,128)S(1)}, f32[8,128]{1,0:T(8,128)S(1)}) custom-call(f32[12,32]{1,0:T(8,128)S(1)} %copy-done.5, f32[12,32]{1,0:T(8,128)S(1)} %copy-done.6, f32[64,384]{1,0:T(8,128)S(1)} %get-tuple-element.14.packed_ref, bf16[208,128]{1,0:T(8,128)(2,1)S(1)} %shard_map.100.own_ref, bf16[208,128]{1,0:T(8,128)(2,1)S(1)} %collective-permute-done.3.other_ref), custom_call_target="tpu_custom_call" | custom-call | flops 10000000000 | bytes 1000000 | tf_op jit(solution)/shard_map/pallas_call | solution.py:412
  21.1 0.6 %collective-permute-start.4 = (f32[8,128]{1,0:T(8,128)S(1)}, f32[8,128]{1,0:T(8,128)S(1)}, u32[]{:S(2)}, u32[]{:S(2)}) collective-permute-start(f32[8,128]{1,0:T(8,128)S(1)} %get-tuple-element.19.own_ref), channel_id=1, source_target_pairs={{0,4},{4,0},{8,12},{12,8},{16,20},{20,16},{24,28},{28,24},{1,5},{5... | collective-permute-start | bytes 12296 | tf_op jit(solution)/shard_map/ppermute | solution.py:36
  21.7 2.3 %collective-permute-done.7.other_ref = bf16[192,128]{1,0:T(8,128)(2,1)S(1)} collective-permute-done((bf16[192,128]{1,0:T(8,128)(2,1)S(1)}, bf16[192,128]{1,0:T(8,128)(2,1)S(1)}, u32[]{:S(2)}, u32[]{:S(2)}) %collective-permute-start.7) | collective-permute-done | bytes 49184 | tf_op jit(solution)/shard_map/ppermute | solution.py:36
  24.1 0.6 %collective-permute-done.4.other_ref = f32[8,128]{1,0:T(8,128)S(1)} collective-permute-done((f32[8,128]{1,0:T(8,128)S(1)}, f32[8,128]{1,0:T(8,128)S(1)}, u32[]{:S(2)}, u32[]{:S(2)}) %collective-permute-start.4) | collective-permute-done | bytes 4128 | tf_op jit(solution)/shard_map/ppermute | solution.py:36
  24.7 1.3 %collective-permute-start.5 = (f32[8,128]{1,0:T(8,128)S(1)}, f32[8,128]{1,0:T(8,128)S(1)}, u32[]{:S(2)}, u32[]{:S(2)}) collective-permute-start(f32[8,128]{1,0:T(8,128)S(1)} %shard_map.103.own_ref), channel_id=1, source_target_pairs={{0,16},{4,20},{8,24},{12,28},{16,0},{20,4},{24,8},{28,12},{1,17},{... | collective-permute-start | bytes 12296 | tf_op jit(solution)/shard_map/ppermute | solution.py:36
  26.0 2.6 %collective-permute-done.8.other_ref = f32[192,128]{1,0:T(8,128)S(1)} collective-permute-done((f32[192,128]{1,0:T(8,128)S(1)}, f32[192,128]{1,0:T(8,128)S(1)}, u32[]{:S(2)}, u32[]{:S(2)}) %collective-permute-start.8) | collective-permute-done | bytes 98336 | tf_op jit(solution)/shard_map/ppermute | solution.py:36
  29.3 1.3 %collective-permute-start.10 = (f32[8,128]{1,0:T(8,128)S(1)}, f32[8,128]{1,0:T(8,128)S(1)}, u32[]{:S(2)}, u32[]{:S(2)}) collective-permute-start(f32[8,128]{1,0:T(8,128)S(1)} %shard_map.104.own_ref), channel_id=1, source_target_pairs={{0,8},{4,12},{8,0},{12,4},{16,24},{20,28},{24,16},{28,20},{1,9},{5... | collective-permute-start | bytes 12296 | tf_op jit(solution)/shard_map/ppermute | solution.py:36
  30.7 2.1 %collective-permute-done.10.other_ref = f32[8,128]{1,0:T(8,128)S(1)} collective-permute-done((f32[8,128]{1,0:T(8,128)S(1)}, f32[8,128]{1,0:T(8,128)S(1)}, u32[]{:S(2)}, u32[]{:S(2)}) %collective-permute-start.10) | collective-permute-done | bytes 4128 | tf_op jit(solution)/shard_map/ppermute | solution.py:36
  32.9 0.5 %collective-permute-done.9.more_ref = f32[192,128]{1,0:T(8,128)S(1)} collective-permute-done((f32[192,128]{1,0:T(8,128)S(1)}, f32[192,128]{1,0:T(8,128)S(1)}, u32[]{:S(2)}, u32[]{:S(2)}) %collective-permute-start.9) | collective-permute-done | bytes 98336 | tf_op jit(solution)/shard_map/ppermute | solution.py:36
  33.3 0.7 %shard_map.109 = (f32[192,128]{1,0:T(8,128)}, f32[2,24,1024]{2,1,0:T(8,128)}) custom-call(f32[192,128]{1,0:T(8,128)S(1)} %shard_map.102.stepped_ref, f32[8,128]{1,0:T(8,128)S(1)} %shard_map.104.own_ref, f32[8,128]{1,0:T(8,128)S(1)} %collective-permute-done.10.other_ref, f32[192,128]{1,0:T(8,128)S(1)} %shard_map.108.sum_ref, ...), custom_call_target="tpu_custom_call" | custom-call | flops 1000000 | bytes 1000000 | tf_op jit(solution)/shard_map/pallas_call | solution.py:412
  (29 shorter events, 1.6 us)
Async XLA Ops:
  0.6 0.9 %copy-start.2 = (f32[2,12,1024]{2,0,1:T(2,128)S(1)}, f32[2,12,1024]{2,0,1:T(2,128)}, u32[]{:S(2)}) copy-start(f32[2,12,1024]{2,0,1:T(2,128)} %param.8) | copy-start | bytes 294916
  0.6 0.9 %copy-start.3 = (f32[2,12,1024]{2,0,1:T(2,128)S(1)}, f32[2,12,1024]{2,0,1:T(2,128)}, u32[]{:S(2)}) copy-start(f32[2,12,1024]{2,0,1:T(2,128)} %param.9) | copy-start | bytes 294916
  0.7 0.9 %copy-start.4 = (f32[32,32]{1,0:T(8,128)S(1)}, f32[32,32]{1,0:T(8,128)}, u32[]{:S(2)}) copy-start(f32[32,32]{1,0:T(8,128)} %coupling_ref.1) | copy-start | bytes 12292
  0.7 0.9 %copy-start.5 = (f32[12,32]{1,0:T(8,128)S(1)}, f32[12,32]{1,0:T(8,128)}, u32[]{:S(2)}) copy-start(f32[12,32]{1,0:T(8,128)} %damping_ref.3) | copy-start | bytes 4612
  0.7 0.9 %copy-start.6 = (f32[12,32]{1,0:T(8,128)S(1)}, f32[12,32]{1,0:T(8,128)}, u32[]{:S(2)}) copy-start(f32[12,32]{1,0:T(8,128)} %phases_ref.3) | copy-start | bytes 4612
  0.7 5.5 %copy-start.7 = (bf16[2,24,12,1024]{3,1,2,0:T(8,128)(2,1)S(1)}, bf16[2,24,12,1024]{3,1,2,0:T(8,128)(2,1)}, u32[]{:S(2)}) copy-start(bf16[2,24,12,1024]{3,1,2,0:T(8,128)(2,1)} %param.15) | copy-start | bytes 3538948
  2.2 6.0 %collective-permute-start.1 = (bf16[400,128]{1,0:T(8,128)(2,1)S(1)}, bf16[400,128]{1,0:T(8,128)(2,1)S(1)}, u32[]{:S(2)}, u32[]{:S(2)}) collective-permute-start(bf16[400,128]{1,0:T(8,128)(2,1)S(1)} %get-tuple-element.16.send_ref), channel_id=1, source_target_pairs={{0,4},{1,20},{2,12},{3,28},{4,0},{5,16},{6,8},{7,24},{8,13},{9,29}... | collective-permute-start | bytes 307208 | tf_op jit(solution)/shard_map/ppermute | solution.py:31
  5.2 5.7 %collective-permute-start = (bf16[400,128]{1,0:T(8,128)(2,1)S(1)}, bf16[400,128]{1,0:T(8,128)(2,1)S(1)}, u32[]{:S(2)}, u32[]{:S(2)}) collective-permute-start(bf16[400,128]{1,0:T(8,128)(2,1)S(1)} %get-tuple-element.16.send_ref), channel_id=1, source_target_pairs={{0,8},{1,24},{2,0},{3,16},{4,12},{5,28},{6,4},{7,20},{8,1},{9,17},... | collective-permute-start | bytes 307208 | tf_op jit(solution)/shard_map/ppermute | solution.py:31
  6.2 1.4 %copy-start = (bf16[2,24,12,1024]{3,1,2,0:T(8,128)(2,1)S(1)}, bf16[2,24,12,1024]{3,1,2,0:T(8,128)(2,1)}, u32[]{:S(2)}) copy-start(bf16[2,24,12,1024]{3,1,2,0:T(8,128)(2,1)} %param.13) | copy-start | bytes 3538948
  6.2 1.6 %copy-start.1 = (bf16[2,24,12,1024]{3,1,2,0:T(8,128)(2,1)S(1)}, bf16[2,24,12,1024]{3,1,2,0:T(8,128)(2,1)}, u32[]{:S(2)}) copy-start(bf16[2,24,12,1024]{3,1,2,0:T(8,128)(2,1)} %param.14) | copy-start | bytes 3538948
  7.0 11.4 %collective-permute-start.6 = (bf16[224,128]{1,0:T(8,128)(2,1)S(1)}, bf16[224,128]{1,0:T(8,128)(2,1)S(1)}, u32[]{:S(2)}, u32[]{:S(2)}) collective-permute-start(bf16[224,128]{1,0:T(8,128)(2,1)S(1)} %get-tuple-element.21), channel_id=1, source_target_pairs={{0,4},{4,0},{8,12},{12,8},{16,20},{20,16},{24,28},{28,24},{1,5},{5... | collective-permute-start | bytes 172040 | tf_op jit(solution)/shard_map/ppermute | solution.py:36
  11.8 2.6 %collective-permute-start.2 = (bf16[208,128]{1,0:T(8,128)(2,1)S(1)}, bf16[208,128]{1,0:T(8,128)(2,1)S(1)}, u32[]{:S(2)}, u32[]{:S(2)}) collective-permute-start(bf16[208,128]{1,0:T(8,128)(2,1)S(1)} %shard_map.99.own_ref), channel_id=1, source_target_pairs={{0,1},{1,0},{2,3},{3,2},{4,5},{5,4},{6,7},{7,6},{8,9},{9,8},{10,11... | collective-permute-start | bytes 159752 | tf_op jit(solution)/shard_map/ppermute | solution.py:36
  14.4 6.1 %collective-permute-start.3 = (bf16[208,128]{1,0:T(8,128)(2,1)S(1)}, bf16[208,128]{1,0:T(8,128)(2,1)S(1)}, u32[]{:S(2)}, u32[]{:S(2)}) collective-permute-start(bf16[208,128]{1,0:T(8,128)(2,1)S(1)} %shard_map.100.own_ref), channel_id=1, source_target_pairs={{0,2},{1,3},{2,0},{3,1},{4,6},{5,7},{6,4},{7,5},{8,10},{9,11},{10,... | collective-permute-start | bytes 159752 | tf_op jit(solution)/shard_map/ppermute | solution.py:36
  18.4 5.6 %collective-permute-start.7 = (bf16[192,128]{1,0:T(8,128)(2,1)S(1)}, bf16[192,128]{1,0:T(8,128)(2,1)S(1)}, u32[]{:S(2)}, u32[]{:S(2)}) collective-permute-start(bf16[192,128]{1,0:T(8,128)(2,1)S(1)} %shard_map.106.own_ref), channel_id=1, source_target_pairs={{0,16},{4,20},{8,24},{12,28},{16,0},{20,4},{24,8},{28,12},{1,17},{... | collective-permute-start | bytes 147464 | tf_op jit(solution)/shard_map/ppermute | solution.py:36
  21.1 3.7 %collective-permute-start.4 = (f32[8,128]{1,0:T(8,128)S(1)}, f32[8,128]{1,0:T(8,128)S(1)}, u32[]{:S(2)}, u32[]{:S(2)}) collective-permute-start(f32[8,128]{1,0:T(8,128)S(1)} %get-tuple-element.19.own_ref), channel_id=1, source_target_pairs={{0,4},{4,0},{8,12},{12,8},{16,20},{20,16},{24,28},{28,24},{1,5},{5... | collective-permute-start | bytes 12296 | tf_op jit(solution)/shard_map/ppermute | solution.py:36
  23.9 4.7 %collective-permute-start.8 = (f32[192,128]{1,0:T(8,128)S(1)}, f32[192,128]{1,0:T(8,128)S(1)}, u32[]{:S(2)}, u32[]{:S(2)}) collective-permute-start(f32[192,128]{1,0:T(8,128)S(1)} %shard_map.107.own_ref), channel_id=1, source_target_pairs={{0,8},{4,12},{8,0},{12,4},{16,24},{20,28},{24,16},{28,20},{1,9},{5... | collective-permute-start | bytes 294920 | tf_op jit(solution)/shard_map/ppermute | solution.py:36
  24.7 4.5 %collective-permute-start.5 = (f32[8,128]{1,0:T(8,128)S(1)}, f32[8,128]{1,0:T(8,128)S(1)}, u32[]{:S(2)}, u32[]{:S(2)}) collective-permute-start(f32[8,128]{1,0:T(8,128)S(1)} %shard_map.103.own_ref), channel_id=1, source_target_pairs={{0,16},{4,20},{8,24},{12,28},{16,0},{20,4},{24,8},{28,12},{1,17},{... | collective-permute-start | bytes 12296 | tf_op jit(solution)/shard_map/ppermute | solution.py:36
  28.6 4.7 %collective-permute-start.9 = (f32[192,128]{1,0:T(8,128)S(1)}, f32[192,128]{1,0:T(8,128)S(1)}, u32[]{:S(2)}, u32[]{:S(2)}) collective-permute-start(f32[192,128]{1,0:T(8,128)S(1)} %shard_map.108.sum_ref), channel_id=1, source_target_pairs={{0,4},{4,0},{8,12},{12,8},{16,20},{20,16},{24,28},{28,24},{1,5},{5... | collective-permute-start | bytes 294920 | tf_op jit(solution)/shard_map/ppermute | solution.py:36
  29.3 3.6 %collective-permute-start.10 = (f32[8,128]{1,0:T(8,128)S(1)}, f32[8,128]{1,0:T(8,128)S(1)}, u32[]{:S(2)}, u32[]{:S(2)}) collective-permute-start(f32[8,128]{1,0:T(8,128)S(1)} %shard_map.104.own_ref), channel_id=1, source_target_pairs={{0,8},{4,12},{8,0},{12,4},{16,24},{20,28},{24,16},{28,20},{1,9},{5... | collective-permute-start | bytes 12296 | tf_op jit(solution)/shard_map/ppermute | solution.py:36

commit v5 on v4

--- a/solution.py
+++ b/solution.py
@@ -8,7 +8,6 @@
 from jax.sharding import PartitionSpec as P
 
 F32, BF16 = (jnp.float32, jnp.bfloat16)
-HIGHEST = lax.Precision.HIGHEST
 EXTRA = 16
 WINDOW = 16
 VMEM_LIMIT = 48 * 1024 * 1024
@@ -375,10 +374,14 @@
     )
     wide = lax.broadcasted_iota(jnp.int32, (steps, steps * bands), 1) // bands
     place = lax.broadcasted_iota(jnp.int32, (steps, steps * bands), 0)
-    spreading = jnp.where(wide == place, 1.0, 0.0)
-    factor = lax.dot_general(
-        both, spreading, (((0,), (0,)), ((), ())), precision=HIGHEST, preferred_element_type=F32
-    )
+    spreading = jnp.where(wide == place, 1.0, 0.0).astype(BF16)
+    factor = jnp.zeros((2 * bands, steps * bands), F32)
+    for _ in range(3):
+        piece = both.astype(BF16)
+        both = both - piece.astype(F32)
+        factor = factor + lax.dot_general(
+            piece, spreading, (((0,), (0,)), ((), ())), preferred_element_type=F32
+        )
     row = packed_ref[...] + jnp.concatenate(chunks, axis=1)
     row_real, row_imag = (row[:bands], row[bands:])
     factor_real, factor_imag = (factor[:bands], factor[bands:])
@@ -526,7 +529,7 @@
     got = crossed(column, "hist", hist_count // 2)
     stepped, squares = call(
         functools.partial(step_kernel, bands, steps),
-        [sds((2 * bands, taken), F32), sds((8, lanes), F32)],
+        [sds((2 * bands, taken), F32), sds((1, lanes), F32)],
         [],
         10**10,
         10**6,

time: 34.2 us -> 34.2 us (level)
  no operation moved by 1% of the time
where the time goes in v5:
time: 34.2 us; the launch traced here: 34.1 us
  starting transfers between devices  14.2 us (42%)
  waiting for transfers between devices  12.9 us (38%)
  Pallas kernels  5.34 us (16%)
  local copies, waits for them, and re-layouts  0.84 us (2%)
  between operations  0.77 us (2%)
    ppermute x9, waiting for transfers between devices, crossed(): return lax.ppermute(x, axis, [(k, k ^ bit) for k in range(size)])  11.2 us
    ppermute x9, starting transfers between devices, crossed(): return lax.ppermute(x, axis, [(k, k ^ bit) for k in range(size)])  10.2 us
    pallas_call x15, Pallas kernels, call(): pl.pallas_call(kernel, out_shape=shapes, in_specs=[pl.BlockSpec(memory_sp...  5.34 us
    ppermute x2, starting transfers between devices, swap_places(): return lax.ppermute(x, ('hist', 'row'), pairs)  4.01 us
    ppermute x2, waiting for transfers between devices, swap_places(): return lax.ppermute(x, ('hist', 'row'), pairs)  1.7 us
    unnamed x16, local copies, waits for them, and re-layouts  0.84 us
  transfers between devices with their start and end apart: 11, of which 9 were waited for; matrix products, arithmetic and copies ran while one was open for 0% of the time, Pallas kernels for 11%

profile of v5, /device:TPU:0, one launch (start us, length us, event | category | flops | bytes accessed | tf_op | source)
XLA Modules:
  0.0 34.1 jit_solution(9330795313844372318)
XLA Ops:
  0.9 0.6 %copy-done.2 = f32[2,12,1024]{2,0,1:T(2,128)S(1)} copy-done((f32[2,12,1024]{2,0,1:T(2,128)S(1)}, f32[2,12,1024]{2,0,1:T(2,128)}, u32[]{:S(2)}) %copy-start.2) | copy-done | bytes 98328
  1.6 0.6 %shard_map.96 = (bf16[400,128]{1,0:T(8,128)(2,1)S(1)}, f32[64,384]{1,0:T(8,128)S(1)}) custom-call(bf16[768,512]{1,0:T(8,128)(2,1)S(1)} %shard_map.95.order_ref, f32[192,128]{1,0:T(8,128)S(1)} %bitcast.22, f32[192,128]{1,0:T(8,128)S(1)} %bitcast.23, f32[32,32]{1,0:T(8,128)S(1)} %copy-done.4, f32[12,32]{1,0:T(8,128)S(1)} %copy-done.5, f32[12,32]{1,0:T(8,128)S(1)} %copy-done.6), custom_call_target="tpu_custom_call" | custom-call | flops 100000000 | bytes 1000000 | tf_op jit(solution)/shard_map/pallas_call | solution.py:415
  2.2 3.0 %collective-permute-start.1 = (bf16[400,128]{1,0:T(8,128)(2,1)S(1)}, bf16[400,128]{1,0:T(8,128)(2,1)S(1)}, u32[]{:S(2)}, u32[]{:S(2)}) collective-permute-start(bf16[400,128]{1,0:T(8,128)(2,1)S(1)} %get-tuple-element.16.send_ref), channel_id=1, source_target_pairs={{0,4},{1,20},{2,12},{3,28},{4,0},{5,16},{6,8},{7,24},{8,13},{9,29}... | collective-permute-start | bytes 307208 | tf_op jit(solution)/shard_map/ppermute | solution.py:30
  5.2 1.0 %collective-permute-start = (bf16[400,128]{1,0:T(8,128)(2,1)S(1)}, bf16[400,128]{1,0:T(8,128)(2,1)S(1)}, u32[]{:S(2)}, u32[]{:S(2)}) collective-permute-start(bf16[400,128]{1,0:T(8,128)(2,1)S(1)} %get-tuple-element.16.send_ref), channel_id=1, source_target_pairs={{0,8},{1,24},{2,0},{3,16},{4,12},{5,28},{6,4},{7,20},{8,1},{9,17},... | collective-permute-start | bytes 307208 | tf_op jit(solution)/shard_map/ppermute | solution.py:30
  6.2 0.7 %shard_map.105 = (f32[192,128]{1,0:T(8,128)S(1)}, bf16[224,128]{1,0:T(8,128)(2,1)S(1)}) custom-call(bf16[2,12,24,1024]{3,2,1,0:T(8,128)(2,1)S(1)} %bitcast.24, bf16[400,128]{1,0:T(8,128)(2,1)S(1)} %get-tuple-element.16.send_ref), custom_call_target="tpu_custom_call" | custom-call | flops 1000000000 | bytes 4000000 | tf_op jit(solution)/shard_map/pallas_call | solution.py:415
  7.0 0.7 %collective-permute-start.6 = (bf16[224,128]{1,0:T(8,128)(2,1)S(1)}, bf16[224,128]{1,0:T(8,128)(2,1)S(1)}, u32[]{:S(2)}, u32[]{:S(2)}) collective-permute-start(bf16[224,128]{1,0:T(8,128)(2,1)S(1)} %get-tuple-element.21), channel_id=1, source_target_pairs={{0,4},{4,0},{8,12},{12,8},{16,20},{20,16},{24,28},{28,24},{1,5},{5... | collective-permute-start | bytes 172040 | tf_op jit(solution)/shard_map/ppermute | solution.py:35
  7.9 0.4 %shard_map.97.lesser_ref.advanced_ref = bf16[3072,256]{1,0:T(8,128)(2,1)S(1)} custom-call(bf16[2,12,24,1024]{3,2,1,0:T(8,128)(2,1)S(1)} %bitcast.18, bf16[2,12,24,1024]{3,2,1,0:T(8,128)(2,1)S(1)} %bitcast.20), custom_call_target="tpu_custom_call" | custom-call | flops 10000 | bytes 10000 | tf_op jit(solution)/shard_map/pallas_call | solution.py:415
  8.2 1.0 %shard_map.98.refs_0_ = f32[72,384]{1,0:T(8,128)S(1)} custom-call(bf16[768,512]{1,0:T(8,128)(2,1)S(1)} %shard_map.95.order_ref, bf16[2,12,24,1024]{3,2,1,0:T(8,128)(2,1)S(1)} %bitcast.19, bf16[2,12,24,1024]{3,2,1,0:T(8,128)(2,1)S(1)} %bitcast.21, bf16[400,128]{1,0:T(8,128)(2,1)S(1)} %collective-permute-done.1.sent_ref), custom_call_target="tpu_custom_call" | custom-call | flops 10000 | bytes 10000 | tf_op jit(solution)/shard_map/pallas_call | solution.py:415
  9.2 1.7 %collective-permute-done.sent_ref = bf16[400,128]{1,0:T(8,128)(2,1)S(1)} collective-permute-done((bf16[400,128]{1,0:T(8,128)(2,1)S(1)}, bf16[400,128]{1,0:T(8,128)(2,1)S(1)}, u32[]{:S(2)}, u32[]{:S(2)}) %collective-permute-start) | collective-permute-done | bytes 102432 | tf_op jit(solution)/shard_map/ppermute | solution.py:30
  10.9 0.9 %shard_map.99.own_ref = bf16[208,128]{1,0:T(8,128)(2,1)S(1)} custom-call(bf16[768,512]{1,0:T(8,128)(2,1)S(1)} %shard_map.95.order_ref, bf16[3072,256]{1,0:T(8,128)(2,1)S(1)} %shard_map.97.lesser_ref.advanced_ref, bf16[3072,256]{1,0:T(8,128)(2,1)S(1)} %shard_map.97.lesser_ref.advanced_ref, bf16[400,128]{1,0:T(8,128)(2,1)S(1)} %collective-permute-done.sent_ref, ...), custom_call_target="tpu_custom_call" | custom-call | flops 10000 | bytes 10000 | tf_op jit(solution)/shard_map/pallas_call | solution.py:415
  11.8 1.7 %collective-permute-start.2 = (bf16[208,128]{1,0:T(8,128)(2,1)S(1)}, bf16[208,128]{1,0:T(8,128)(2,1)S(1)}, u32[]{:S(2)}, u32[]{:S(2)}) collective-permute-start(bf16[208,128]{1,0:T(8,128)(2,1)S(1)} %shard_map.99.own_ref), channel_id=1, source_target_pairs={{0,1},{1,0},{2,3},{3,2},{4,5},{5,4},{6,7},{7,6},{8,9},{9,8},{10,11... | collective-permute-start | bytes 159752 | tf_op jit(solution)/shard_map/ppermute | solution.py:35
  13.5 0.9 %collective-permute-done.2.other_ref = bf16[208,128]{1,0:T(8,128)(2,1)S(1)} collective-permute-done((bf16[208,128]{1,0:T(8,128)(2,1)S(1)}, bf16[208,128]{1,0:T(8,128)(2,1)S(1)}, u32[]{:S(2)}, u32[]{:S(2)}) %collective-permute-start.2) | collective-permute-done | bytes 53280 | tf_op jit(solution)/shard_map/ppermute | solution.py:35
  14.4 3.9 %collective-permute-start.3 = (bf16[208,128]{1,0:T(8,128)(2,1)S(1)}, bf16[208,128]{1,0:T(8,128)(2,1)S(1)}, u32[]{:S(2)}, u32[]{:S(2)}) collective-permute-start(bf16[208,128]{1,0:T(8,128)(2,1)S(1)} %shard_map.100.own_ref), channel_id=1, source_target_pairs={{0,2},{1,3},{2,0},{3,1},{4,6},{5,7},{6,4},{7,5},{8,10},{9,11},{10,... | collective-permute-start | bytes 159752 | tf_op jit(solution)/shard_map/ppermute | solution.py:35
  18.5 2.1 %collective-permute-done.3.other_ref = bf16[208,128]{1,0:T(8,128)(2,1)S(1)} collective-permute-done((bf16[208,128]{1,0:T(8,128)(2,1)S(1)}, bf16[208,128]{1,0:T(8,128)(2,1)S(1)}, u32[]{:S(2)}, u32[]{:S(2)}) %collective-permute-start.3) | collective-permute-done | bytes 53280 | tf_op jit(solution)/shard_map/ppermute | solution.py:35
  20.5 0.5 %shard_map.101 = (f32[64,384]{1,0:T(8,128)S(1)}, f32[1,128]{1,0:T(1,128)S(1)}) custom-call(f32[12,32]{1,0:T(8,128)S(1)} %copy-done.5, f32[12,32]{1,0:T(8,128)S(1)} %copy-done.6, f32[64,384]{1,0:T(8,128)S(1)} %get-tuple-element.14.packed_ref, bf16[208,128]{1,0:T(8,128)(2,1)S(1)} %shard_map.100.own_ref, bf16[208,128]{1,0:T(8,128)(2,1)S(1)} %collective-permute-done.3.other_ref), custom_call_target="tpu_custom_call" | custom-call | flops 10000000000 | bytes 1000000 | tf_op jit(solution)/shard_map/pallas_call | solution.py:415
  21.0 0.6 %collective-permute-start.4 = (f32[1,128]{1,0:T(1,128)S(1)}, f32[1,128]{1,0:T(1,128)S(1)}, u32[]{:S(2)}, u32[]{:S(2)}) collective-permute-start(f32[1,128]{1,0:T(1,128)S(1)} %get-tuple-element.19.own_ref), channel_id=1, source_target_pairs={{0,4},{4,0},{8,12},{12,8},{16,20},{20,16},{24,28},{28,24},{1,5},{5... | collective-permute-start | bytes 1544 | tf_op jit(solution)/shard_map/ppermute | solution.py:35
  21.6 2.3 %collective-permute-done.7.other_ref = bf16[192,128]{1,0:T(8,128)(2,1)S(1)} collective-permute-done((bf16[192,128]{1,0:T(8,128)(2,1)S(1)}, bf16[192,128]{1,0:T(8,128)(2,1)S(1)}, u32[]{:S(2)}, u32[]{:S(2)}) %collective-permute-start.7) | collective-permute-done | bytes 49184 | tf_op jit(solution)/shard_map/ppermute | solution.py:35
  24.1 0.5 %collective-permute-done.4.other_ref = f32[1,128]{1,0:T(1,128)S(1)} collective-permute-done((f32[1,128]{1,0:T(1,128)S(1)}, f32[1,128]{1,0:T(1,128)S(1)}, u32[]{:S(2)}, u32[]{:S(2)}) %collective-permute-start.4) | collective-permute-done | bytes 544 | tf_op jit(solution)/shard_map/ppermute | solution.py:35
  24.6 1.3 %collective-permute-start.5 = (f32[1,128]{1,0:T(1,128)S(1)}, f32[1,128]{1,0:T(1,128)S(1)}, u32[]{:S(2)}, u32[]{:S(2)}) collective-permute-start(f32[1,128]{1,0:T(1,128)S(1)} %shard_map.103.own_ref), channel_id=1, source_target_pairs={{0,16},{4,20},{8,24},{12,28},{16,0},{20,4},{24,8},{28,12},{1,17},{... | collective-permute-start | bytes 1544 | tf_op jit(solution)/shard_map/ppermute | solution.py:35
  25.9 2.7 %collective-permute-done.8.other_ref = f32[192,128]{1,0:T(8,128)S(1)} collective-permute-done((f32[192,128]{1,0:T(8,128)S(1)}, f32[192,128]{1,0:T(8,128)S(1)}, u32[]{:S(2)}, u32[]{:S(2)}) %collective-permute-start.8) | collective-permute-done | bytes 98336 | tf_op jit(solution)/shard_map/ppermute | solution.py:35
  29.1 1.4 %collective-permute-start.10 = (f32[1,128]{1,0:T(1,128)S(1)}, f32[1,128]{1,0:T(1,128)S(1)}, u32[]{:S(2)}, u32[]{:S(2)}) collective-permute-start(f32[1,128]{1,0:T(1,128)S(1)} %shard_map.104.own_ref), channel_id=1, source_target_pairs={{0,8},{4,12},{8,0},{12,4},{16,24},{20,28},{24,16},{28,20},{1,9},{5... | collective-permute-start | bytes 1544 | tf_op jit(solution)/shard_map/ppermute | solution.py:35
  30.7 1.9 %collective-permute-done.10.other_ref = f32[1,128]{1,0:T(1,128)S(1)} collective-permute-done((f32[1,128]{1,0:T(1,128)S(1)}, f32[1,128]{1,0:T(1,128)S(1)}, u32[]{:S(2)}, u32[]{:S(2)}) %collective-permute-start.10) | collective-permute-done | bytes 544 | tf_op jit(solution)/shard_map/ppermute | solution.py:35
  32.6 0.7 %collective-permute-done.9.more_ref = f32[192,128]{1,0:T(8,128)S(1)} collective-permute-done((f32[192,128]{1,0:T(8,128)S(1)}, f32[192,128]{1,0:T(8,128)S(1)}, u32[]{:S(2)}, u32[]{:S(2)}) %collective-permute-start.9) | collective-permute-done | bytes 98336 | tf_op jit(solution)/shard_map/ppermute | solution.py:35
  33.3 0.7 %shard_map.109 = (f32[192,128]{1,0:T(8,128)}, f32[2,24,1024]{2,1,0:T(8,128)}) custom-call(f32[192,128]{1,0:T(8,128)S(1)} %shard_map.102.stepped_ref, f32[1,128]{1,0:T(1,128)S(1)} %shard_map.104.own_ref, f32[1,128]{1,0:T(1,128)S(1)} %collective-permute-done.10.other_ref, f32[192,128]{1,0:T(8,128)S(1)} %shard_map.108.sum_ref, ...), custom_call_target="tpu_custom_call" | custom-call | flops 1000000 | bytes 1000000 | tf_op jit(solution)/shard_map/pallas_call | solution.py:415
  (29 shorter events, 1.4 us)
Async XLA Ops:
  0.6 0.9 %copy-start.2 = (f32[2,12,1024]{2,0,1:T(2,128)S(1)}, f32[2,12,1024]{2,0,1:T(2,128)}, u32[]{:S(2)}) copy-start(f32[2,12,1024]{2,0,1:T(2,128)} %param.8) | copy-start | bytes 294916
  0.6 0.9 %copy-start.3 = (f32[2,12,1024]{2,0,1:T(2,128)S(1)}, f32[2,12,1024]{2,0,1:T(2,128)}, u32[]{:S(2)}) copy-start(f32[2,12,1024]{2,0,1:T(2,128)} %param.9) | copy-start | bytes 294916
  0.7 0.9 %copy-start.4 = (f32[32,32]{1,0:T(8,128)S(1)}, f32[32,32]{1,0:T(8,128)}, u32[]{:S(2)}) copy-start(f32[32,32]{1,0:T(8,128)} %coupling_ref.1) | copy-start | bytes 12292
  0.7 0.9 %copy-start.5 = (f32[12,32]{1,0:T(8,128)S(1)}, f32[12,32]{1,0:T(8,128)}, u32[]{:S(2)}) copy-start(f32[12,32]{1,0:T(8,128)} %damping_ref.3) | copy-start | bytes 4612
  0.7 0.9 %copy-start.6 = (f32[12,32]{1,0:T(8,128)S(1)}, f32[12,32]{1,0:T(8,128)}, u32[]{:S(2)}) copy-start(f32[12,32]{1,0:T(8,128)} %phases_ref.3) | copy-start | bytes 4612
  0.7 5.5 %copy-start.7 = (bf16[2,24,12,1024]{3,1,2,0:T(8,128)(2,1)S(1)}, bf16[2,24,12,1024]{3,1,2,0:T(8,128)(2,1)}, u32[]{:S(2)}) copy-start(bf16[2,24,12,1024]{3,1,2,0:T(8,128)(2,1)} %param.15) | copy-start | bytes 3538948
  2.2 6.0 %collective-permute-start.1 = (bf16[400,128]{1,0:T(8,128)(2,1)S(1)}, bf16[400,128]{1,0:T(8,128)(2,1)S(1)}, u32[]{:S(2)}, u32[]{:S(2)}) collective-permute-start(bf16[400,128]{1,0:T(8,128)(2,1)S(1)} %get-tuple-element.16.send_ref), channel_id=1, source_target_pairs={{0,4},{1,20},{2,12},{3,28},{4,0},{5,16},{6,8},{7,24},{8,13},{9,29}... | collective-permute-start | bytes 307208 | tf_op jit(solution)/shard_map/ppermute | solution.py:30
  5.2 5.7 %collective-permute-start = (bf16[400,128]{1,0:T(8,128)(2,1)S(1)}, bf16[400,128]{1,0:T(8,128)(2,1)S(1)}, u32[]{:S(2)}, u32[]{:S(2)}) collective-permute-start(bf16[400,128]{1,0:T(8,128)(2,1)S(1)} %get-tuple-element.16.send_ref), channel_id=1, source_target_pairs={{0,8},{1,24},{2,0},{3,16},{4,12},{5,28},{6,4},{7,20},{8,1},{9,17},... | collective-permute-start | bytes 307208 | tf_op jit(solution)/shard_map/ppermute | solution.py:30
  6.2 1.4 %copy-start = (bf16[2,24,12,1024]{3,1,2,0:T(8,128)(2,1)S(1)}, bf16[2,24,12,1024]{3,1,2,0:T(8,128)(2,1)}, u32[]{:S(2)}) copy-start(bf16[2,24,12,1024]{3,1,2,0:T(8,128)(2,1)} %param.13) | copy-start | bytes 3538948
  6.2 1.6 %copy-start.1 = (bf16[2,24,12,1024]{3,1,2,0:T(8,128)(2,1)S(1)}, bf16[2,24,12,1024]{3,1,2,0:T(8,128)(2,1)}, u32[]{:S(2)}) copy-start(bf16[2,24,12,1024]{3,1,2,0:T(8,128)(2,1)} %param.14) | copy-start | bytes 3538948
  7.0 11.4 %collective-permute-start.6 = (bf16[224,128]{1,0:T(8,128)(2,1)S(1)}, bf16[224,128]{1,0:T(8,128)(2,1)S(1)}, u32[]{:S(2)}, u32[]{:S(2)}) collective-permute-start(bf16[224,128]{1,0:T(8,128)(2,1)S(1)} %get-tuple-element.21), channel_id=1, source_target_pairs={{0,4},{4,0},{8,12},{12,8},{16,20},{20,16},{24,28},{28,24},{1,5},{5... | collective-permute-start | bytes 172040 | tf_op jit(solution)/shard_map/ppermute | solution.py:35
  11.8 2.6 %collective-permute-start.2 = (bf16[208,128]{1,0:T(8,128)(2,1)S(1)}, bf16[208,128]{1,0:T(8,128)(2,1)S(1)}, u32[]{:S(2)}, u32[]{:S(2)}) collective-permute-start(bf16[208,128]{1,0:T(8,128)(2,1)S(1)} %shard_map.99.own_ref), channel_id=1, source_target_pairs={{0,1},{1,0},{2,3},{3,2},{4,5},{5,4},{6,7},{7,6},{8,9},{9,8},{10,11... | collective-permute-start | bytes 159752 | tf_op jit(solution)/shard_map/ppermute | solution.py:35
  14.4 6.1 %collective-permute-start.3 = (bf16[208,128]{1,0:T(8,128)(2,1)S(1)}, bf16[208,128]{1,0:T(8,128)(2,1)S(1)}, u32[]{:S(2)}, u32[]{:S(2)}) collective-permute-start(bf16[208,128]{1,0:T(8,128)(2,1)S(1)} %shard_map.100.own_ref), channel_id=1, source_target_pairs={{0,2},{1,3},{2,0},{3,1},{4,6},{5,7},{6,4},{7,5},{8,10},{9,11},{10,... | collective-permute-start | bytes 159752 | tf_op jit(solution)/shard_map/ppermute | solution.py:35
  18.4 5.6 %collective-permute-start.7 = (bf16[192,128]{1,0:T(8,128)(2,1)S(1)}, bf16[192,128]{1,0:T(8,128)(2,1)S(1)}, u32[]{:S(2)}, u32[]{:S(2)}) collective-permute-start(bf16[192,128]{1,0:T(8,128)(2,1)S(1)} %shard_map.106.own_ref), channel_id=1, source_target_pairs={{0,16},{4,20},{8,24},{12,28},{16,0},{20,4},{24,8},{28,12},{1,17},{... | collective-permute-start | bytes 147464 | tf_op jit(solution)/shard_map/ppermute | solution.py:35
  21.0 3.6 %collective-permute-start.4 = (f32[1,128]{1,0:T(1,128)S(1)}, f32[1,128]{1,0:T(1,128)S(1)}, u32[]{:S(2)}, u32[]{:S(2)}) collective-permute-start(f32[1,128]{1,0:T(1,128)S(1)} %get-tuple-element.19.own_ref), channel_id=1, source_target_pairs={{0,4},{4,0},{8,12},{12,8},{16,20},{20,16},{24,28},{28,24},{1,5},{5... | collective-permute-start | bytes 1544 | tf_op jit(solution)/shard_map/ppermute | solution.py:35
  23.9 4.7 %collective-permute-start.8 = (f32[192,128]{1,0:T(8,128)S(1)}, f32[192,128]{1,0:T(8,128)S(1)}, u32[]{:S(2)}, u32[]{:S(2)}) collective-permute-start(f32[192,128]{1,0:T(8,128)S(1)} %shard_map.107.own_ref), channel_id=1, source_target_pairs={{0,8},{4,12},{8,0},{12,4},{16,24},{20,28},{24,16},{28,20},{1,9},{5... | collective-permute-start | bytes 294920 | tf_op jit(solution)/shard_map/ppermute | solution.py:35
  24.6 4.4 %collective-permute-start.5 = (f32[1,128]{1,0:T(1,128)S(1)}, f32[1,128]{1,0:T(1,128)S(1)}, u32[]{:S(2)}, u32[]{:S(2)}) collective-permute-start(f32[1,128]{1,0:T(1,128)S(1)} %shard_map.103.own_ref), channel_id=1, source_target_pairs={{0,16},{4,20},{8,24},{12,28},{16,0},{20,4},{24,8},{28,12},{1,17},{... | collective-permute-start | bytes 1544 | tf_op jit(solution)/shard_map/ppermute | solution.py:35
  28.6 4.7 %collective-permute-start.9 = (f32[192,128]{1,0:T(8,128)S(1)}, f32[192,128]{1,0:T(8,128)S(1)}, u32[]{:S(2)}, u32[]{:S(2)}) collective-permute-start(f32[192,128]{1,0:T(8,128)S(1)} %shard_map.108.sum_ref), channel_id=1, source_target_pairs={{0,4},{4,0},{8,12},{12,8},{16,20},{20,16},{24,28},{28,24},{1,5},{5... | collective-permute-start | bytes 294920 | tf_op jit(solution)/shard_map/ppermute | solution.py:35
  29.1 3.5 %collective-permute-start.10 = (f32[1,128]{1,0:T(1,128)S(1)}, f32[1,128]{1,0:T(1,128)S(1)}, u32[]{:S(2)}, u32[]{:S(2)}) collective-permute-start(f32[1,128]{1,0:T(1,128)S(1)} %shard_map.104.own_ref), channel_id=1, source_target_pairs={{0,8},{4,12},{8,0},{12,4},{16,24},{20,28},{24,16},{28,20},{1,9},{5... | collective-permute-start | bytes 1544 | tf_op jit(solution)/shard_map/ppermute | solution.py:35

commit v6 on v5

--- a/solution.py
+++ b/solution.py
@@ -66,20 +66,22 @@
     return product(highs[0], highs[1]) + (product(highs[0], lows[1]) + product(lows[0], highs[1]))
 
 
-def energy_kernel(bands, steps, order_ref, less_ref, great_ref, coupling_ref, damping_ref, phases_ref, send_ref, packed_ref, work):
+def energy_kernel(bands, steps, order_ref, less_ref, great_ref, coupling_ref, damping_ref, phases_ref, send_ref, packed_ref, mixed, work):
     groups = bands // 4
     chunks = steps // 4
     for which, ref in enumerate((less_ref, great_ref)):
+        mixed[which, : ref.shape[0], :] = ref[...]
         for part in range(2):
             for chunk in range(chunks):
                 blocks = [
-                    ref[pl.ds((chunk * 4 + k) * groups * 2 + part, groups, stride=2), :]
+                    mixed[which, pl.ds((chunk * 4 + k) * groups * 2 + part, groups, stride=2), :]
                     for k in range(4)
                 ]
                 for k, block in enumerate(swap_blocks(blocks)):
                     work[which, part, pl.ds(chunk * bands + k, groups, stride=4), :] = block
-    less_real, less_imag = (work[0, 0], work[0, 1])
-    great_real, great_imag = (work[1, 0], work[1, 1])
+    rows = chunks * bands
+    less_real, less_imag = (work[0, 0, :rows], work[0, 1, :rows])
+    great_real, great_imag = (work[1, 0, :rows], work[1, 1, :rows])
     polar = jnp.concatenate(
         [
             -(less_real * great_real + less_imag * great_imag),
@@ -395,12 +397,12 @@
     out_ref[bands:, :] = stepped[1]
 
 
-def relayout_kernel(bands, steps, stepped_ref, out_ref, work):
+def relayout_kernel(bands, steps, stepped_ref, out_ref, work, mixed):
     lanes = 4 * bands
     groups = bands // 4
     for part in range(2):
         for chunk in range(steps // 4):
-            work[part, chunk] = stepped_ref[
+            work[part, chunk, :bands] = stepped_ref[
                 part * bands : (part + 1) * bands, chunk * lanes : (chunk + 1) * lanes
             ]
     for part in range(2):
@@ -408,7 +410,8 @@
             blocks = [work[part, chunk, pl.ds(k, groups, stride=4), :] for k in range(4)]
             for k, block in enumerate(swap_blocks(blocks)):
                 first = (chunk * 4 + k) * groups * 2 + part
-                out_ref[pl.ds(first, groups, stride=2), :] = block
+                mixed[pl.ds(first, groups, stride=2), :] = block
+    out_ref[...] = mixed[: out_ref.shape[0], :]
 
 
 def call(kernel, shapes, scratch, flops, moved, spaces, *operands):
@@ -455,7 +458,10 @@
     send, packed = call(
         functools.partial(energy_kernel, bands, steps),
         [sds((taken + EXTRA, lanes), BF16), sds((2 * bands, taken), F32)],
-        [vmem((2, 2, steps // 4 * bands, lanes), F32)],
+        [
+            vmem((2, steps * groups * 2 + 8, lanes), F32),
+            vmem((2, 2, steps // 4 * bands + 8, lanes), F32),
+        ],
         10**8,
         10**6,
         [pl.ANY] + [vmem] * 5,
@@ -529,7 +535,7 @@
     got = crossed(column, "hist", hist_count // 2)
     stepped, squares = call(
         functools.partial(step_kernel, bands, steps),
-        [sds((2 * bands, taken), F32), sds((1, lanes), F32)],
+        [sds((2 * bands, taken), F32), sds((8, lanes), F32)],
         [],
         10**10,
         10**6,
@@ -543,7 +549,7 @@
     (stepped,) = call(
         functools.partial(relayout_kernel, bands, steps),
         [sds((steps * groups * 2, lanes), F32)],
-        [vmem((2, steps // 4, bands, lanes), F32)],
+        [vmem((2, steps // 4, bands + 8, lanes), F32), vmem((steps * groups * 2 + 8, lanes), F32)],
         10**10,
         10**6,
         [vmem],

time: 34.2 us -> 34.2 us (level)
  no operation moved by 1% of the time
where the time goes in v6:
time: 34.2 us; the launch traced here: 34.1 us
  starting transfers between devices  14.1 us (41%)
  waiting for transfers between devices  13 us (38%)
  Pallas kernels  5.36 us (16%)
  local copies, waits for them, and re-layouts  0.84 us (2%)
  between operations  0.77 us (2%)
    ppermute x9, waiting for transfers between devices, crossed(): return lax.ppermute(x, axis, [(k, k ^ bit) for k in range(size)])  11.3 us
    ppermute x9, starting transfers between devices, crossed(): return lax.ppermute(x, axis, [(k, k ^ bit) for k in range(size)])  10.1 us
    pallas_call x15, Pallas kernels, call(): pl.pallas_call(kernel, out_shape=shapes, in_specs=[pl.BlockSpec(memory_sp...  5.36 us
    ppermute x2, starting transfers between devices, swap_places(): return lax.ppermute(x, ('hist', 'row'), pairs)  4.01 us
    ppermute x2, waiting for transfers between devices, swap_places(): return lax.ppermute(x, ('hist', 'row'), pairs)  1.7 us
    unnamed x16, local copies, waits for them, and re-layouts  0.84 us
  transfers between devices with their start and end apart: 11, of which 9 were waited for; matrix products, arithmetic and copies ran while one was open for 0% of the time, Pallas kernels for 11%

profile of v6, /device:TPU:0, one launch (start us, length us, event | category | flops | bytes accessed | tf_op | source)
XLA Modules:
  0.0 34.1 jit_solution(14238890146691108661)
XLA Ops:
  0.9 0.6 %copy-done.2 = f32[2,12,1024]{2,0,1:T(2,128)S(1)} copy-done((f32[2,12,1024]{2,0,1:T(2,128)S(1)}, f32[2,12,1024]{2,0,1:T(2,128)}, u32[]{:S(2)}) %copy-start.2) | copy-done | bytes 98328
  1.6 0.6 %shard_map.96 = (bf16[400,128]{1,0:T(8,128)(2,1)S(1)}, f32[64,384]{1,0:T(8,128)S(1)}) custom-call(bf16[768,512]{1,0:T(8,128)(2,1)S(1)} %shard_map.95.order_ref, f32[192,128]{1,0:T(8,128)S(1)} %bitcast.22, f32[192,128]{1,0:T(8,128)S(1)} %bitcast.23, f32[32,32]{1,0:T(8,128)S(1)} %copy-done.4, f32[12,32]{1,0:T(8,128)S(1)} %copy-done.5, f32[12,32]{1,0:T(8,128)S(1)} %copy-done.6), custom_call_target="tpu_custom_call" | custom-call | flops 100000000 | bytes 1000000 | tf_op jit(solution)/shard_map/pallas_call | solution.py:418
  2.2 3.0 %collective-permute-start.1 = (bf16[400,128]{1,0:T(8,128)(2,1)S(1)}, bf16[400,128]{1,0:T(8,128)(2,1)S(1)}, u32[]{:S(2)}, u32[]{:S(2)}) collective-permute-start(bf16[400,128]{1,0:T(8,128)(2,1)S(1)} %get-tuple-element.16.send_ref), channel_id=1, source_target_pairs={{0,4},{1,20},{2,12},{3,28},{4,0},{5,16},{6,8},{7,24},{8,13},{9,29}... | collective-permute-start | bytes 307208 | tf_op jit(solution)/shard_map/ppermute | solution.py:30
  5.2 1.0 %collective-permute-start = (bf16[400,128]{1,0:T(8,128)(2,1)S(1)}, bf16[400,128]{1,0:T(8,128)(2,1)S(1)}, u32[]{:S(2)}, u32[]{:S(2)}) collective-permute-start(bf16[400,128]{1,0:T(8,128)(2,1)S(1)} %get-tuple-element.16.send_ref), channel_id=1, source_target_pairs={{0,8},{1,24},{2,0},{3,16},{4,12},{5,28},{6,4},{7,20},{8,1},{9,17},... | collective-permute-start | bytes 307208 | tf_op jit(solution)/shard_map/ppermute | solution.py:30
  6.2 0.7 %shard_map.105 = (f32[192,128]{1,0:T(8,128)S(1)}, bf16[224,128]{1,0:T(8,128)(2,1)S(1)}) custom-call(bf16[2,12,24,1024]{3,2,1,0:T(8,128)(2,1)S(1)} %bitcast.24, bf16[400,128]{1,0:T(8,128)(2,1)S(1)} %get-tuple-element.16.send_ref), custom_call_target="tpu_custom_call" | custom-call | flops 1000000000 | bytes 4000000 | tf_op jit(solution)/shard_map/pallas_call | solution.py:418
  7.0 0.7 %collective-permute-start.6 = (bf16[224,128]{1,0:T(8,128)(2,1)S(1)}, bf16[224,128]{1,0:T(8,128)(2,1)S(1)}, u32[]{:S(2)}, u32[]{:S(2)}) collective-permute-start(bf16[224,128]{1,0:T(8,128)(2,1)S(1)} %get-tuple-element.21), channel_id=1, source_target_pairs={{0,4},{4,0},{8,12},{12,8},{16,20},{20,16},{24,28},{28,24},{1,5},{5... | collective-permute-start | bytes 172040 | tf_op jit(solution)/shard_map/ppermute | solution.py:35
  7.9 0.4 %shard_map.97.lesser_ref.advanced_ref = bf16[3072,256]{1,0:T(8,128)(2,1)S(1)} custom-call(bf16[2,12,24,1024]{3,2,1,0:T(8,128)(2,1)S(1)} %bitcast.18, bf16[2,12,24,1024]{3,2,1,0:T(8,128)(2,1)S(1)} %bitcast.20), custom_call_target="tpu_custom_call" | custom-call | flops 10000 | bytes 10000 | tf_op jit(solution)/shard_map/pallas_call | solution.py:418
  8.3 1.0 %shard_map.98.refs_0_ = f32[72,384]{1,0:T(8,128)S(1)} custom-call(bf16[768,512]{1,0:T(8,128)(2,1)S(1)} %shard_map.95.order_ref, bf16[2,12,24,1024]{3,2,1,0:T(8,128)(2,1)S(1)} %bitcast.19, bf16[2,12,24,1024]{3,2,1,0:T(8,128)(2,1)S(1)} %bitcast.21, bf16[400,128]{1,0:T(8,128)(2,1)S(1)} %collective-permute-done.1.sent_ref), custom_call_target="tpu_custom_call" | custom-call | flops 10000 | bytes 10000 | tf_op jit(solution)/shard_map/pallas_call | solution.py:418
  9.2 1.7 %collective-permute-done.sent_ref = bf16[400,128]{1,0:T(8,128)(2,1)S(1)} collective-permute-done((bf16[400,128]{1,0:T(8,128)(2,1)S(1)}, bf16[400,128]{1,0:T(8,128)(2,1)S(1)}, u32[]{:S(2)}, u32[]{:S(2)}) %collective-permute-start) | collective-permute-done | bytes 102432 | tf_op jit(solution)/shard_map/ppermute | solution.py:30
  10.9 0.9 %shard_map.99.own_ref = bf16[208,128]{1,0:T(8,128)(2,1)S(1)} custom-call(bf16[768,512]{1,0:T(8,128)(2,1)S(1)} %shard_map.95.order_ref, bf16[3072,256]{1,0:T(8,128)(2,1)S(1)} %shard_map.97.lesser_ref.advanced_ref, bf16[3072,256]{1,0:T(8,128)(2,1)S(1)} %shard_map.97.lesser_ref.advanced_ref, bf16[400,128]{1,0:T(8,128)(2,1)S(1)} %collective-permute-done.sent_ref, ...), custom_call_target="tpu_custom_call" | custom-call | flops 10000 | bytes 10000 | tf_op jit(solution)/shard_map/pallas_call | solution.py:418
  11.9 1.7 %collective-permute-start.2 = (bf16[208,128]{1,0:T(8,128)(2,1)S(1)}, bf16[208,128]{1,0:T(8,128)(2,1)S(1)}, u32[]{:S(2)}, u32[]{:S(2)}) collective-permute-start(bf16[208,128]{1,0:T(8,128)(2,1)S(1)} %shard_map.99.own_ref), channel_id=1, source_target_pairs={{0,1},{1,0},{2,3},{3,2},{4,5},{5,4},{6,7},{7,6},{8,9},{9,8},{10,11... | collective-permute-start | bytes 159752 | tf_op jit(solution)/shard_map/ppermute | solution.py:35
  13.5 0.9 %collective-permute-done.2.other_ref = bf16[208,128]{1,0:T(8,128)(2,1)S(1)} collective-permute-done((bf16[208,128]{1,0:T(8,128)(2,1)S(1)}, bf16[208,128]{1,0:T(8,128)(2,1)S(1)}, u32[]{:S(2)}, u32[]{:S(2)}) %collective-permute-start.2) | collective-permute-done | bytes 53280 | tf_op jit(solution)/shard_map/ppermute | solution.py:35
  14.4 3.9 %collective-permute-start.3 = (bf16[208,128]{1,0:T(8,128)(2,1)S(1)}, bf16[208,128]{1,0:T(8,128)(2,1)S(1)}, u32[]{:S(2)}, u32[]{:S(2)}) collective-permute-start(bf16[208,128]{1,0:T(8,128)(2,1)S(1)} %shard_map.100.own_ref), channel_id=1, source_target_pairs={{0,2},{1,3},{2,0},{3,1},{4,6},{5,7},{6,4},{7,5},{8,10},{9,11},{10,... | collective-permute-start | bytes 159752 | tf_op jit(solution)/shard_map/ppermute | solution.py:35
  18.5 2.1 %collective-permute-done.3.other_ref = bf16[208,128]{1,0:T(8,128)(2,1)S(1)} collective-permute-done((bf16[208,128]{1,0:T(8,128)(2,1)S(1)}, bf16[208,128]{1,0:T(8,128)(2,1)S(1)}, u32[]{:S(2)}, u32[]{:S(2)}) %collective-permute-start.3) | collective-permute-done | bytes 53280 | tf_op jit(solution)/shard_map/ppermute | solution.py:35
  20.5 0.5 %shard_map.101 = (f32[64,384]{1,0:T(8,128)S(1)}, f32[8,128]{1,0:T(8,128)S(1)}) custom-call(f32[12,32]{1,0:T(8,128)S(1)} %copy-done.5, f32[12,32]{1,0:T(8,128)S(1)} %copy-done.6, f32[64,384]{1,0:T(8,128)S(1)} %get-tuple-element.14.packed_ref, bf16[208,128]{1,0:T(8,128)(2,1)S(1)} %shard_map.100.own_ref, bf16[208,128]{1,0:T(8,128)(2,1)S(1)} %collective-permute-done.3.other_ref), custom_call_target="tpu_custom_call" | custom-call | flops 10000000000 | bytes 1000000 | tf_op jit(solution)/shard_map/pallas_call | solution.py:418
  21.0 0.6 %collective-permute-start.4 = (f32[8,128]{1,0:T(8,128)S(1)}, f32[8,128]{1,0:T(8,128)S(1)}, u32[]{:S(2)}, u32[]{:S(2)}) collective-permute-start(f32[8,128]{1,0:T(8,128)S(1)} %get-tuple-element.19.own_ref), channel_id=1, source_target_pairs={{0,4},{4,0},{8,12},{12,8},{16,20},{20,16},{24,28},{28,24},{1,5},{5... | collective-permute-start | bytes 12296 | tf_op jit(solution)/shard_map/ppermute | solution.py:35
  21.6 2.3 %collective-permute-done.7.other_ref = bf16[192,128]{1,0:T(8,128)(2,1)S(1)} collective-permute-done((bf16[192,128]{1,0:T(8,128)(2,1)S(1)}, bf16[192,128]{1,0:T(8,128)(2,1)S(1)}, u32[]{:S(2)}, u32[]{:S(2)}) %collective-permute-start.7) | collective-permute-done | bytes 49184 | tf_op jit(solution)/shard_map/ppermute | solution.py:35
  24.1 0.6 %collective-permute-done.4.other_ref = f32[8,128]{1,0:T(8,128)S(1)} collective-permute-done((f32[8,128]{1,0:T(8,128)S(1)}, f32[8,128]{1,0:T(8,128)S(1)}, u32[]{:S(2)}, u32[]{:S(2)}) %collective-permute-start.4) | collective-permute-done | bytes 4128 | tf_op jit(solution)/shard_map/ppermute | solution.py:35
  24.7 1.3 %collective-permute-start.5 = (f32[8,128]{1,0:T(8,128)S(1)}, f32[8,128]{1,0:T(8,128)S(1)}, u32[]{:S(2)}, u32[]{:S(2)}) collective-permute-start(f32[8,128]{1,0:T(8,128)S(1)} %shard_map.103.own_ref), channel_id=1, source_target_pairs={{0,16},{4,20},{8,24},{12,28},{16,0},{20,4},{24,8},{28,12},{1,17},{... | collective-permute-start | bytes 12296 | tf_op jit(solution)/shard_map/ppermute | solution.py:35
  26.0 2.7 %collective-permute-done.8.other_ref = f32[192,128]{1,0:T(8,128)S(1)} collective-permute-done((f32[192,128]{1,0:T(8,128)S(1)}, f32[192,128]{1,0:T(8,128)S(1)}, u32[]{:S(2)}, u32[]{:S(2)}) %collective-permute-start.8) | collective-permute-done | bytes 98336 | tf_op jit(solution)/shard_map/ppermute | solution.py:35
  29.2 1.4 %collective-permute-start.10 = (f32[8,128]{1,0:T(8,128)S(1)}, f32[8,128]{1,0:T(8,128)S(1)}, u32[]{:S(2)}, u32[]{:S(2)}) collective-permute-start(f32[8,128]{1,0:T(8,128)S(1)} %shard_map.104.own_ref), channel_id=1, source_target_pairs={{0,8},{4,12},{8,0},{12,4},{16,24},{20,28},{24,16},{28,20},{1,9},{5... | collective-permute-start | bytes 12296 | tf_op jit(solution)/shard_map/ppermute | solution.py:35
  30.7 2.1 %collective-permute-done.10.other_ref = f32[8,128]{1,0:T(8,128)S(1)} collective-permute-done((f32[8,128]{1,0:T(8,128)S(1)}, f32[8,128]{1,0:T(8,128)S(1)}, u32[]{:S(2)}, u32[]{:S(2)}) %collective-permute-start.10) | collective-permute-done | bytes 4128 | tf_op jit(solution)/shard_map/ppermute | solution.py:35
  32.8 0.5 %collective-permute-done.9.more_ref = f32[192,128]{1,0:T(8,128)S(1)} collective-permute-done((f32[192,128]{1,0:T(8,128)S(1)}, f32[192,128]{1,0:T(8,128)S(1)}, u32[]{:S(2)}, u32[]{:S(2)}) %collective-permute-start.9) | collective-permute-done | bytes 98336 | tf_op jit(solution)/shard_map/ppermute | solution.py:35
  33.3 0.7 %shard_map.109 = (f32[192,128]{1,0:T(8,128)}, f32[2,24,1024]{2,1,0:T(8,128)}) custom-call(f32[192,128]{1,0:T(8,128)S(1)} %shard_map.102.stepped_ref, f32[8,128]{1,0:T(8,128)S(1)} %shard_map.104.own_ref, f32[8,128]{1,0:T(8,128)S(1)} %collective-permute-done.10.other_ref, f32[192,128]{1,0:T(8,128)S(1)} %shard_map.108.sum_ref, ...), custom_call_target="tpu_custom_call" | custom-call | flops 1000000 | bytes 1000000 | tf_op jit(solution)/shard_map/pallas_call | solution.py:418
  (29 shorter events, 1.5 us)
Async XLA Ops:
  0.6 0.9 %copy-start.2 = (f32[2,12,1024]{2,0,1:T(2,128)S(1)}, f32[2,12,1024]{2,0,1:T(2,128)}, u32[]{:S(2)}) copy-start(f32[2,12,1024]{2,0,1:T(2,128)} %param.8) | copy-start | bytes 294916
  0.6 0.9 %copy-start.3 = (f32[2,12,1024]{2,0,1:T(2,128)S(1)}, f32[2,12,1024]{2,0,1:T(2,128)}, u32[]{:S(2)}) copy-start(f32[2,12,1024]{2,0,1:T(2,128)} %param.9) | copy-start | bytes 294916
  0.7 0.9 %copy-start.4 = (f32[32,32]{1,0:T(8,128)S(1)}, f32[32,32]{1,0:T(8,128)}, u32[]{:S(2)}) copy-start(f32[32,32]{1,0:T(8,128)} %coupling_ref.1) | copy-start | bytes 12292
  0.7 0.9 %copy-start.5 = (f32[12,32]{1,0:T(8,128)S(1)}, f32[12,32]{1,0:T(8,128)}, u32[]{:S(2)}) copy-start(f32[12,32]{1,0:T(8,128)} %damping_ref.3) | copy-start | bytes 4612
  0.7 0.9 %copy-start.6 = (f32[12,32]{1,0:T(8,128)S(1)}, f32[12,32]{1,0:T(8,128)}, u32[]{:S(2)}) copy-start(f32[12,32]{1,0:T(8,128)} %phases_ref.3) | copy-start | bytes 4612
  0.7 5.6 %copy-start.7 = (bf16[2,24,12,1024]{3,1,2,0:T(8,128)(2,1)S(1)}, bf16[2,24,12,1024]{3,1,2,0:T(8,128)(2,1)}, u32[]{:S(2)}) copy-start(bf16[2,24,12,1024]{3,1,2,0:T(8,128)(2,1)} %param.15) | copy-start | bytes 3538948
  2.2 6.0 %collective-permute-start.1 = (bf16[400,128]{1,0:T(8,128)(2,1)S(1)}, bf16[400,128]{1,0:T(8,128)(2,1)S(1)}, u32[]{:S(2)}, u32[]{:S(2)}) collective-permute-start(bf16[400,128]{1,0:T(8,128)(2,1)S(1)} %get-tuple-element.16.send_ref), channel_id=1, source_target_pairs={{0,4},{1,20},{2,12},{3,28},{4,0},{5,16},{6,8},{7,24},{8,13},{9,29}... | collective-permute-start | bytes 307208 | tf_op jit(solution)/shard_map/ppermute | solution.py:30
  5.2 5.7 %collective-permute-start = (bf16[400,128]{1,0:T(8,128)(2,1)S(1)}, bf16[400,128]{1,0:T(8,128)(2,1)S(1)}, u32[]{:S(2)}, u32[]{:S(2)}) collective-permute-start(bf16[400,128]{1,0:T(8,128)(2,1)S(1)} %get-tuple-element.16.send_ref), channel_id=1, source_target_pairs={{0,8},{1,24},{2,0},{3,16},{4,12},{5,28},{6,4},{7,20},{8,1},{9,17},... | collective-permute-start | bytes 307208 | tf_op jit(solution)/shard_map/ppermute | solution.py:30
  6.2 1.5 %copy-start = (bf16[2,24,12,1024]{3,1,2,0:T(8,128)(2,1)S(1)}, bf16[2,24,12,1024]{3,1,2,0:T(8,128)(2,1)}, u32[]{:S(2)}) copy-start(bf16[2,24,12,1024]{3,1,2,0:T(8,128)(2,1)} %param.13) | copy-start | bytes 3538948
  6.2 1.6 %copy-start.1 = (bf16[2,24,12,1024]{3,1,2,0:T(8,128)(2,1)S(1)}, bf16[2,24,12,1024]{3,1,2,0:T(8,128)(2,1)}, u32[]{:S(2)}) copy-start(bf16[2,24,12,1024]{3,1,2,0:T(8,128)(2,1)} %param.14) | copy-start | bytes 3538948
  7.0 11.4 %collective-permute-start.6 = (bf16[224,128]{1,0:T(8,128)(2,1)S(1)}, bf16[224,128]{1,0:T(8,128)(2,1)S(1)}, u32[]{:S(2)}, u32[]{:S(2)}) collective-permute-start(bf16[224,128]{1,0:T(8,128)(2,1)S(1)} %get-tuple-element.21), channel_id=1, source_target_pairs={{0,4},{4,0},{8,12},{12,8},{16,20},{20,16},{24,28},{28,24},{1,5},{5... | collective-permute-start | bytes 172040 | tf_op jit(solution)/shard_map/ppermute | solution.py:35
  11.9 2.6 %collective-permute-start.2 = (bf16[208,128]{1,0:T(8,128)(2,1)S(1)}, bf16[208,128]{1,0:T(8,128)(2,1)S(1)}, u32[]{:S(2)}, u32[]{:S(2)}) collective-permute-start(bf16[208,128]{1,0:T(8,128)(2,1)S(1)} %shard_map.99.own_ref), channel_id=1, source_target_pairs={{0,1},{1,0},{2,3},{3,2},{4,5},{5,4},{6,7},{7,6},{8,9},{9,8},{10,11... | collective-permute-start | bytes 159752 | tf_op jit(solution)/shard_map/ppermute | solution.py:35
  14.4 6.1 %collective-permute-start.3 = (bf16[208,128]{1,0:T(8,128)(2,1)S(1)}, bf16[208,128]{1,0:T(8,128)(2,1)S(1)}, u32[]{:S(2)}, u32[]{:S(2)}) collective-permute-start(bf16[208,128]{1,0:T(8,128)(2,1)S(1)} %shard_map.100.own_ref), channel_id=1, source_target_pairs={{0,2},{1,3},{2,0},{3,1},{4,6},{5,7},{6,4},{7,5},{8,10},{9,11},{10,... | collective-permute-start | bytes 159752 | tf_op jit(solution)/shard_map/ppermute | solution.py:35
  18.4 5.6 %collective-permute-start.7 = (bf16[192,128]{1,0:T(8,128)(2,1)S(1)}, bf16[192,128]{1,0:T(8,128)(2,1)S(1)}, u32[]{:S(2)}, u32[]{:S(2)}) collective-permute-start(bf16[192,128]{1,0:T(8,128)(2,1)S(1)} %shard_map.106.own_ref), channel_id=1, source_target_pairs={{0,16},{4,20},{8,24},{12,28},{16,0},{20,4},{24,8},{28,12},{1,17},{... | collective-permute-start | bytes 147464 | tf_op jit(solution)/shard_map/ppermute | solution.py:35
  21.0 3.7 %collective-permute-start.4 = (f32[8,128]{1,0:T(8,128)S(1)}, f32[8,128]{1,0:T(8,128)S(1)}, u32[]{:S(2)}, u32[]{:S(2)}) collective-permute-start(f32[8,128]{1,0:T(8,128)S(1)} %get-tuple-element.19.own_ref), channel_id=1, source_target_pairs={{0,4},{4,0},{8,12},{12,8},{16,20},{20,16},{24,28},{28,24},{1,5},{5... | collective-permute-start | bytes 12296 | tf_op jit(solution)/shard_map/ppermute | solution.py:35
  24.0 4.7 %collective-permute-start.8 = (f32[192,128]{1,0:T(8,128)S(1)}, f32[192,128]{1,0:T(8,128)S(1)}, u32[]{:S(2)}, u32[]{:S(2)}) collective-permute-start(f32[192,128]{1,0:T(8,128)S(1)} %shard_map.107.own_ref), channel_id=1, source_target_pairs={{0,8},{4,12},{8,0},{12,4},{16,24},{20,28},{24,16},{28,20},{1,9},{5... | collective-permute-start | bytes 294920 | tf_op jit(solution)/shard_map/ppermute | solution.py:35
  24.7 4.5 %collective-permute-start.5 = (f32[8,128]{1,0:T(8,128)S(1)}, f32[8,128]{1,0:T(8,128)S(1)}, u32[]{:S(2)}, u32[]{:S(2)}) collective-permute-start(f32[8,128]{1,0:T(8,128)S(1)} %shard_map.103.own_ref), channel_id=1, source_target_pairs={{0,16},{4,20},{8,24},{12,28},{16,0},{20,4},{24,8},{28,12},{1,17},{... | collective-permute-start | bytes 12296 | tf_op jit(solution)/shard_map/ppermute | solution.py:35
  28.7 4.7 %collective-permute-start.9 = (f32[192,128]{1,0:T(8,128)S(1)}, f32[192,128]{1,0:T(8,128)S(1)}, u32[]{:S(2)}, u32[]{:S(2)}) collective-permute-start(f32[192,128]{1,0:T(8,128)S(1)} %shard_map.108.sum_ref), channel_id=1, source_target_pairs={{0,4},{4,0},{8,12},{12,8},{16,20},{20,16},{24,28},{28,24},{1,5},{5... | collective-permute-start | bytes 294920 | tf_op jit(solution)/shard_map/ppermute | solution.py:35
  29.2 3.6 %collective-permute-start.10 = (f32[8,128]{1,0:T(8,128)S(1)}, f32[8,128]{1,0:T(8,128)S(1)}, u32[]{:S(2)}, u32[]{:S(2)}) collective-permute-start(f32[8,128]{1,0:T(8,128)S(1)} %shard_map.104.own_ref), channel_id=1, source_target_pairs={{0,8},{4,12},{8,0},{12,4},{16,24},{20,28},{24,16},{28,20},{1,9},{5... | collective-permute-start | bytes 12296 | tf_op jit(solution)/shard_map/ppermute | solution.py:35
